TPU v7x, 32 devices: a whole 2x2x4 slice. The times are simulated.
32 devices in a mesh: canvas: 8 (over y, x, core), rows: 4 (over z).
Axes of the slice: x: 2, y: 2, z: 4, core: 2. Of those that a mesh axis runs over, the one named last changes fastest.
Arguments:
- tokens: bfloat16 [16, 1024, 768], P('canvas', 'rows'), may hold values from -6 to 6
- latent: int32 [16, 1024], P('canvas', 'rows'), may hold values from 0 to 3, as said below
- condition: float32 [16, 4, 768], P('canvas'), may hold values from -6 to 6
- w_ada: bfloat16 [768, 4608], replicated, may hold values from -0.21875 to 0.21875
- b_ada: bfloat16 [4608], replicated, may hold values from -1.5 to 1.5
- conv_attn: bfloat16 [9, 768], replicated, may hold values from -2 to 2
- w_qkv: bfloat16 [768, 2304], replicated, may hold values from -0.21875 to 0.21875
- bias_qv: bfloat16 [1536], replicated, may hold values from -1.5 to 1.5
- w_out: bfloat16 [768, 768], replicated, may hold values from -0.875 to 0.875
- b_out: bfloat16 [768], replicated, may hold values from -1.5 to 1.5
- w_up: bfloat16 [768, 3072], replicated, may hold values from -0.21875 to 0.21875
- b_up: bfloat16 [3072], replicated, may hold values from -1.5 to 1.5
- conv_ffn: bfloat16 [9, 3072], replicated, may hold values from -2 to 2
- w_down: bfloat16 [3072, 768], replicated, may hold values from -0.109375 to 0.109375
- b_down: bfloat16 [768], replicated, may hold values from -1.5 to 1.5
- cotangent: bfloat16 [16, 1024, 768], P('canvas', 'rows'), may hold values from -6 to 6
Outputs:
- output: bfloat16 [16, 1024, 768], P('canvas', 'rows')
- grad_input: float32 [16, 1024, 768], P('canvas', 'rows')
- grad_condition: float32 [16, 4, 768], P('canvas')
- grad_w_ada: float32 [768, 4608], P('canvas')
- grad_b_ada: float32 [4608], P('canvas')
- grad_conv_attn: float32 [9, 768], P(None, 'canvas')
- grad_w_qkv: float32 [768, 2304], P('canvas')
- grad_bias_qv: float32 [1536], P('canvas')
- grad_w_out: float32 [768, 768], P('canvas')
- grad_b_out: float32 [768], P('canvas')
- grad_w_up: float32 [768, 3072], P('canvas')
- grad_b_up: float32 [3072], P('canvas')
- grad_conv_ffn: float32 [9, 3072], P(None, 'canvas')
- grad_w_down: float32 [3072, 768], P('canvas')
- grad_b_down: float32 [768], P('canvas')
Inputs may be any that keep to these rules, and one draw needn't show every extreme that they name: In each canvas of 32 x 32 tokens each of the four latent ids marks 16 * 16 tokens: either four strips of 32 rows by 8 columns, or two such strips filling one half of the columns beside two 16 x 16 squares filling the other half. Some latent of every canvas covers all rows.
All inputs are finite; a program needn't handle non-finite values.
Results may differ from a plain program's by a relative error of at most 0.02.
The roundings to bfloat16 on the way count: a program that leaves them out, or rounds other values in their place, can miss the bound.
Values may be sent and summed in bfloat16 or wider, within the bound.
A program may use at most 256 MiB of HBM per device.

v0:
```python
import jax
import jax.numpy as jnp
from jax import lax
from jax.sharding import PartitionSpec as P

HEADS = 12
HEAD_DIM = 64
SIDE = 32


EPSILON = 1e-06
NEG_FILL = -1e30
PRECISE = lax.Precision.HIGHEST


def padded_2(cells, sides, width):
    for axis, dim in sides:
        count = lax.axis_size(axis)
        ends = count - 1
        head = lax.slice_in_dim(cells, 0, width, axis=dim)
        tail = lax.slice_in_dim(cells, cells.shape[dim] - width, cells.shape[dim], axis=dim)
        cells = jnp.concatenate(
            [
                lax.ppermute(tail, axis, [(i, (i + 1) % count) for i in range(ends)]),
                cells,
                lax.ppermute(head, axis, [((i + 1) % count, i) for i in range(ends)]),
            ],
            axis=dim,
        )
    return cells


def passed_along(block, axis, distance):
    devices = range(lax.axis_size(axis))
    route = [((i - distance) % len(devices), i) for i in devices]
    return lax.ppermute(block, axis, route)


def layer_norm(values):
    centered = values - jnp.mean(values, axis=-1, keepdims=True)
    return centered * lax.rsqrt(jnp.mean(centered * centered, axis=-1, keepdims=True) + EPSILON)


def modulate_norm(values, shift, scale_part):
    return layer_norm(values) * (1.0 + scale_part) + shift


def gelu_tanh(values):
    return jax.nn.gelu(values, approximate=True)


def pad_columns(field):
    return jnp.pad(field, ((0, 0), (0, 0), (1, 1), (0, 0)))


def grid_taps(padded, kernel, rows_here, cols_here):
    summed = padded[:, 0:rows_here, 0:cols_here].astype(jnp.float32) * kernel[0]
    for tap_row in range(3):
        for tap_col in range(3):
            if tap_row + tap_col > 0:
                window = padded[
                    :, tap_row : tap_row + rows_here, tap_col : tap_col + cols_here
                ].astype(jnp.float32)
                summed = summed + window * kernel[3 * tap_row + tap_col]
    return summed


def kernel_grad(padded, grad_grid):
    rows_here = grad_grid.shape[1]
    cols_here = grad_grid.shape[2]
    grad_f = grad_grid.astype(jnp.float32)
    tap_sums = []
    for tap_row in range(3):
        for tap_col in range(3):
            window = padded[:, tap_row : tap_row + rows_here, tap_col : tap_col + cols_here].astype(
                jnp.float32
            )
            tap_sums.append(jnp.sum(window * grad_f, axis=(0, 1, 2)))
    return jnp.stack(tap_sums)


def to_groups(field, rows_here):
    canvases = field.shape[0]
    channels = field.shape[-1]
    shaped = field.reshape(canvases, rows_here // 2, 2, SIDE // 2, 2, channels)
    return shaped.transpose(0, 2, 4, 1, 3, 5).reshape(
        canvases, 4, rows_here // 2 * (SIDE // 2), channels
    )


def from_groups(field, rows_here):
    canvases = field.shape[0]
    channels = field.shape[-1]
    shaped = field.reshape(canvases, 2, 2, rows_here // 2, SIDE // 2, channels)
    return shaped.transpose(0, 3, 1, 4, 2, 5).reshape(canvases, rows_here * SIDE, channels)


def block_scores(query_heads, key_piece, query_lat, key_lat):
    canvases = key_piece.shape[0]
    count = key_piece.shape[2]
    key_heads = key_piece.reshape(canvases, 4, count, HEADS, HEAD_DIM)
    scores = jnp.einsum(
        "cgqhe,cgkhe->cghqk", query_heads, key_heads, preferred_element_type=jnp.float32
    ) * HEAD_DIM ** (-0.5)
    same_latent = query_lat[:, :, None, :, None] == key_lat[:, :, None, None, :]
    return (scores, same_latent, key_heads)


def shards(
    tokens,
    latent,
    condition,
    w_ada,
    b_ada,
    conv_attn,
    w_qkv,
    bias_qv,
    w_out,
    b_out,
    w_up,
    b_up,
    conv_ffn,
    w_down,
    b_down,
    cotangent,
):
    canvases = tokens.shape[0]
    local_tokens = tokens.shape[1]
    model_width = tokens.shape[2]
    ffn_width = w_up.shape[1]
    rows_here = local_tokens // SIDE
    group_len = local_tokens // 4
    score_scale = HEAD_DIM ** (-0.5)
    tokens_f = tokens.astype(jnp.float32)
    onehot = (latent[..., None] == jnp.arange(4)).astype(jnp.float32)
    silu_cond, silu_pull = jax.vjp(jax.nn.silu, condition)
    cond_low = silu_cond.astype(jnp.bfloat16)
    modulation = jnp.einsum(
        "ckd,df->ckf", cond_low, w_ada, preferred_element_type=jnp.float32
    ) + b_ada.astype(jnp.float32)
    per_token = jnp.einsum("cnk,ckf->cnf", onehot, modulation, precision=PRECISE)
    shift_one, scale_one, gate_one, shift_two, scale_two, gate_two = jnp.split(
        per_token, 6, axis=-1
    )
    h_one, norm_one_pull = jax.vjp(modulate_norm, tokens_f, shift_one, scale_one)
    attn_in = h_one.astype(jnp.bfloat16).reshape(canvases, rows_here, SIDE, model_width)
    attn_pad = pad_columns(padded_2(attn_in, (("rows", 1),), 1))
    conv_attn_f = conv_attn.astype(jnp.float32)
    conv_low = (
        grid_taps(attn_pad, conv_attn_f, rows_here, SIDE)
        .astype(jnp.bfloat16)
        .reshape(-1, model_width)
    )
    bias_full = jnp.concatenate(
        [bias_qv[:model_width], jnp.zeros((model_width,), jnp.bfloat16), bias_qv[model_width:]]
    ).astype(jnp.float32)
    projected = (jnp.dot(conv_low, w_qkv, preferred_element_type=jnp.float32) + bias_full).astype(
        jnp.bfloat16
    )
    grouped = to_groups(projected.reshape(canvases, local_tokens, 3 * model_width), rows_here)
    queries = grouped[..., :model_width]
    key_rows = grouped[..., model_width : 2 * model_width]
    value_rows = grouped[..., 2 * model_width :]
    lat_groups = to_groups(latent[..., None], rows_here)[..., 0]
    all_lat = lax.all_gather(lat_groups, "rows", axis=2, tiled=True)
    query_heads = queries.reshape(canvases, 4, group_len, HEADS, HEAD_DIM)
    start_best = jnp.full((canvases, 4, HEADS, group_len), NEG_FILL, jnp.float32)
    best = start_best
    key_piece = lax.all_gather(key_rows, "rows", axis=2, tiled=True)
    value_piece = lax.all_gather(value_rows, "rows", axis=2, tiled=True)
    count = key_piece.shape[2]
    fold_scores, fold_same_latent, fold_key_heads = block_scores(
        query_heads, key_piece, lat_groups, all_lat
    )
    masked = jnp.where(fold_same_latent, fold_scores, NEG_FILL)
    newest = jnp.maximum(best, jnp.max(masked, axis=-1))
    weights = jnp.where(fold_same_latent, jnp.exp(masked - newest[..., None]), 0.0)
    fold_value_heads = value_piece.astype(jnp.float32).reshape(canvases, 4, count, HEADS, HEAD_DIM)
    accum = jnp.einsum("cghqk,cgkhe->cghqe", weights, fold_value_heads, precision=PRECISE)
    best, weight_sum, accum = (newest, jnp.sum(weights, axis=-1), accum)
    attn_heads = accum / weight_sum[..., None]
    log_norm = best + jnp.log(weight_sum)
    attended = from_groups(
        attn_heads.transpose(0, 1, 3, 2, 4).reshape(canvases, 4, group_len, model_width), rows_here
    )
    attended_low = attended.astype(jnp.bfloat16).reshape(-1, model_width)
    attn_out = (
        jnp.dot(attended_low, w_out, preferred_element_type=jnp.float32) + b_out.astype(jnp.float32)
    ).reshape(canvases, local_tokens, model_width)
    middle = tokens_f + gate_one * attn_out
    h_two, norm_two_pull = jax.vjp(modulate_norm, middle, shift_two, scale_two)
    ffn_in = h_two.astype(jnp.bfloat16).reshape(-1, model_width)
    up_rows = (
        jnp.dot(ffn_in, w_up, preferred_element_type=jnp.float32) + b_up.astype(jnp.float32)
    ).astype(jnp.bfloat16)
    up_grid = up_rows.reshape(canvases, rows_here, SIDE, ffn_width)
    up_pad = pad_columns(padded_2(up_grid, (("rows", 1),), 1))
    conv_ffn_f = conv_ffn.astype(jnp.float32)
    conv_two = grid_taps(up_pad, conv_ffn_f, rows_here, SIDE)
    activated, gelu_pull = jax.vjp(gelu_tanh, conv_two)
    act_low = activated.astype(jnp.bfloat16).reshape(-1, ffn_width)
    branch = (
        jnp.dot(act_low, w_down, preferred_element_type=jnp.float32) + b_down.astype(jnp.float32)
    ).reshape(canvases, local_tokens, model_width)
    result = (middle + gate_two * branch).astype(jnp.bfloat16)
    out_grad = cotangent.astype(jnp.float32)
    branch_grad = (gate_two * out_grad).astype(jnp.bfloat16).reshape(-1, model_width)
    gate_two_grad = out_grad * branch
    g_b_down = jnp.sum(branch_grad.astype(jnp.float32), axis=0)
    g_w_down = jnp.dot(act_low.T, branch_grad, preferred_element_type=jnp.float32)
    act_grad = jnp.dot(branch_grad, w_down.T, preferred_element_type=jnp.float32).reshape(
        canvases, rows_here, SIDE, ffn_width
    )
    conv_two_grad = gelu_pull(act_grad)[0].astype(jnp.bfloat16)
    conv_two_pad = pad_columns(padded_2(conv_two_grad, (("rows", 1),), 1))
    up_grad = (
        grid_taps(conv_two_pad, conv_ffn_f[::-1], rows_here, SIDE)
        .astype(jnp.bfloat16)
        .reshape(-1, ffn_width)
    )
    g_conv_ffn = kernel_grad(up_pad, conv_two_grad)
    g_b_up = jnp.sum(up_grad.astype(jnp.float32), axis=0)
    g_w_up = jnp.dot(ffn_in.T, up_grad, preferred_element_type=jnp.float32)
    ffn_grad = jnp.dot(up_grad, w_up.T, preferred_element_type=jnp.float32).reshape(
        canvases, local_tokens, model_width
    )
    middle_part, shift_two_grad, scale_two_grad = norm_two_pull(ffn_grad)
    middle_grad = middle_part + out_grad
    gate_one_grad = middle_grad * attn_out
    attn_grad = (gate_one * middle_grad).astype(jnp.bfloat16).reshape(-1, model_width)
    g_b_out = jnp.sum(attn_grad.astype(jnp.float32), axis=0)
    g_w_out = jnp.dot(attended_low.T, attn_grad, preferred_element_type=jnp.float32)
    attended_grad = jnp.dot(attn_grad, w_out.T, preferred_element_type=jnp.float32).astype(
        jnp.bfloat16
    )
    grad_heads = to_groups(
        attended_grad.reshape(canvases, local_tokens, model_width), rows_here
    ).reshape(canvases, 4, group_len, HEADS, HEAD_DIM)
    grad_heads_f = grad_heads.astype(jnp.float32)
    delta = jnp.sum(grad_heads_f.transpose(0, 1, 3, 2, 4) * attn_heads, axis=-1)
    row_count = lax.axis_size("rows")
    here = lax.axis_index("rows")
    carried = jnp.stack([key_rows, value_rows])
    pending = jnp.zeros((2,) + key_rows.shape, jnp.float32)
    query_grad = jnp.zeros((canvases, 4, group_len, HEADS, HEAD_DIM), jnp.float32)
    for turn_index in range(row_count):
        source = (here - turn_index) % row_count
        key_lat = lax.dynamic_slice_in_dim(all_lat, source * group_len, group_len, 2)
        scores, same_latent, key_heads = block_scores(query_heads, carried[0], lat_groups, key_lat)
        value_heads = carried[1].reshape(canvases, 4, group_len, HEADS, HEAD_DIM)
        softmax_weights = jnp.where(same_latent, jnp.exp(scores - log_norm[..., None]), 0.0)
        weight_grad = jnp.einsum(
            "cgqhe,cgkhe->cghqk", grad_heads, value_heads, preferred_element_type=jnp.float32
        )
        score_grad = (softmax_weights * (weight_grad - delta[..., None])).astype(jnp.bfloat16)
        query_grad = query_grad + score_scale * jnp.einsum(
            "cghqk,cgkhe->cgqhe", score_grad, key_heads, preferred_element_type=jnp.float32
        )
        key_part = score_scale * jnp.einsum(
            "cghqk,cgqhe->cgkhe", score_grad, query_heads, preferred_element_type=jnp.float32
        )
        value_part = jnp.einsum(
            "cghqk,cgqhe->cgkhe", softmax_weights, grad_heads_f, precision=PRECISE
        )
        pending = pending + jnp.stack([key_part, value_part]).reshape(pending.shape)
        if turn_index + 1 < row_count:
            carried = passed_along(carried, "rows", 1)
        pending = passed_along(pending.astype(jnp.bfloat16), "rows", 1).astype(pending.dtype)
    query_low = query_grad.reshape(canvases, 4, group_len, model_width).astype(jnp.bfloat16)
    grouped_grad = jnp.concatenate(
        [query_low, pending[0].astype(jnp.bfloat16), pending[1].astype(jnp.bfloat16)], axis=-1
    )
    qkv_grad = from_groups(grouped_grad, rows_here).reshape(-1, 3 * model_width)
    qkv_grad_f = qkv_grad.astype(jnp.float32)
    g_bias_qv = jnp.concatenate(
        [
            jnp.sum(qkv_grad_f[:, :model_width], axis=0),
            jnp.sum(qkv_grad_f[:, 2 * model_width :], axis=0),
        ]
    )
    g_w_qkv = jnp.dot(conv_low.T, qkv_grad, preferred_element_type=jnp.float32)
    conv_one_grad = (
        jnp.dot(qkv_grad, w_qkv.T, preferred_element_type=jnp.float32)
        .astype(jnp.bfloat16)
        .reshape(canvases, rows_here, SIDE, model_width)
    )
    conv_one_pad = pad_columns(padded_2(conv_one_grad, (("rows", 1),), 1))
    attn_in_grad = grid_taps(conv_one_pad, conv_attn_f[::-1], rows_here, SIDE).reshape(
        canvases, local_tokens, model_width
    )
    g_conv_attn = kernel_grad(attn_pad, conv_one_grad)
    token_part, shift_one_grad, scale_one_grad = norm_one_pull(attn_in_grad)
    input_grad = token_part + middle_grad
    token_mod_grad = jnp.concatenate(
        [
            shift_one_grad,
            scale_one_grad,
            gate_one_grad,
            shift_two_grad,
            scale_two_grad,
            gate_two_grad,
        ],
        axis=-1,
    )
    mod_grad = jnp.einsum("cnk,cnf->ckf", onehot, token_mod_grad, precision=PRECISE)
    cond_f = cond_low.astype(jnp.float32)
    summed = (
        lax.psum(g_conv_attn.astype(jnp.bfloat16), "rows").astype(jnp.float32),
        lax.psum(g_w_qkv.astype(jnp.bfloat16), "rows").astype(jnp.float32),
        lax.psum(g_bias_qv.astype(jnp.bfloat16), "rows").astype(jnp.float32),
        lax.psum(g_w_out.astype(jnp.bfloat16), "rows").astype(jnp.float32),
        lax.psum(g_b_out.astype(jnp.bfloat16), "rows").astype(jnp.float32),
        lax.psum(g_w_up.astype(jnp.bfloat16), "rows").astype(jnp.float32),
        lax.psum(g_b_up.astype(jnp.bfloat16), "rows").astype(jnp.float32),
        lax.psum(g_conv_ffn.astype(jnp.bfloat16), "rows").astype(jnp.float32),
        lax.psum(g_w_down.astype(jnp.bfloat16), "rows").astype(jnp.float32),
        lax.psum(g_b_down.astype(jnp.bfloat16), "rows").astype(jnp.float32),
        lax.psum(mod_grad.astype(jnp.bfloat16), "rows").astype(jnp.float32),
    )
    mod_total = summed[10]
    g_w_ada = jnp.einsum("ckd,ckf->df", cond_f, mod_total, precision=PRECISE)
    g_b_ada = jnp.sum(mod_total, axis=(0, 1))
    shares = (
        lax.psum_scatter(
            g_w_ada.astype(jnp.bfloat16), "canvas", scatter_dimension=0, tiled=True
        ).astype(jnp.float32),
        lax.psum_scatter(
            g_b_ada.astype(jnp.bfloat16), "canvas", scatter_dimension=0, tiled=True
        ).astype(jnp.float32),
        lax.psum_scatter(
            summed[0].astype(jnp.bfloat16), "canvas", scatter_dimension=1, tiled=True
        ).astype(jnp.float32),
        lax.psum_scatter(
            summed[1].astype(jnp.bfloat16), "canvas", scatter_dimension=0, tiled=True
        ).astype(jnp.float32),
        lax.psum_scatter(
            summed[2].astype(jnp.bfloat16), "canvas", scatter_dimension=0, tiled=True
        ).astype(jnp.float32),
        lax.psum_scatter(
            summed[3].astype(jnp.bfloat16), "canvas", scatter_dimension=0, tiled=True
        ).astype(jnp.float32),
        lax.psum_scatter(
            summed[4].astype(jnp.bfloat16), "canvas", scatter_dimension=0, tiled=True
        ).astype(jnp.float32),
        lax.psum_scatter(
            summed[5].astype(jnp.bfloat16), "canvas", scatter_dimension=0, tiled=True
        ).astype(jnp.float32),
        lax.psum_scatter(
            summed[6].astype(jnp.bfloat16), "canvas", scatter_dimension=0, tiled=True
        ).astype(jnp.float32),
        lax.psum_scatter(
            summed[7].astype(jnp.bfloat16), "canvas", scatter_dimension=1, tiled=True
        ).astype(jnp.float32),
        lax.psum_scatter(
            summed[8].astype(jnp.bfloat16), "canvas", scatter_dimension=0, tiled=True
        ).astype(jnp.float32),
        lax.psum_scatter(
            summed[9].astype(jnp.bfloat16), "canvas", scatter_dimension=0, tiled=True
        ).astype(jnp.float32),
    )
    cond_grad = silu_pull(
        jnp.einsum("ckf,df->ckd", mod_total, w_ada.astype(jnp.float32), precision=PRECISE)
    )[0]
    return (
        result,
        input_grad,
        cond_grad,
        shares[0],
        shares[1],
        shares[2],
        shares[3],
        shares[4],
        shares[5],
        shares[6],
        shares[7],
        shares[8],
        shares[9],
        shares[10],
        shares[11],
    )


def solution(mesh):
    placed = (
        P("canvas", "rows", None),
        P("canvas", "rows"),
        P("canvas", None, None),
        P(),
        P(),
        P(),
        P(),
        P(),
        P(),
        P(),
        P(),
        P(),
        P(),
        P(),
        P(),
        P("canvas", "rows", None),
    )
    return jax.shard_map(
        shards,
        mesh=mesh,
        in_specs=placed,
        out_specs=(
            P("canvas", "rows", None),
            P("canvas", "rows", None),
            P("canvas", None, None),
            P("canvas", None),
            P("canvas"),
            P(None, "canvas"),
            P("canvas", None),
            P("canvas"),
            P("canvas", None),
            P("canvas"),
            P("canvas", None),
            P("canvas"),
            P(None, "canvas"),
            P("canvas", None),
            P("canvas"),
        ),
        check_vma=False,
    )
```

profile of v0, /device:TPU:0, one launch (start us, length us, event | category | flops | bytes accessed | tf_op | source)
XLA Modules:
  0.0 879.8 jit_solution(3307992189147079772)
XLA Ops:
  54.4 19.8 %all_gather.9 = s32[2,4,256]{1,0,2:T(2,128)} all-gather(s32[2,4,64]{1,0,2:T(2,128)} %copy.95), channel_id=1, replica_groups=mesh['canvas'=8,'rows'=4] {'rows'}, dimensions={2}, use_global_device_ids=true | all-gather | bytes 10240 | tf_op jit(solution)/shard_map/all_gather | solution.py:165
  80.5 37.6 %all-gather.3.cloned.1.call-done = bf16[2,4,256,768]{3,2,1,0:T(8,128)(2,1)} async-done(((bf16[2,4,64,768]{3,2,1,0:T(8,128)(2,1)}), bf16[2,4,256,768]{3,2,1,0:T(8,128)(2,1)}) %all-gather.3.cloned.1.call-update) | async-done | bytes 3145744 | tf_op jit(solution)/shard_map/all_gather | solution.py:169
  132.8 49.5 %all-gather.5.cloned.1.call-done = bf16[2,4,256,768]{3,2,1,0:T(8,128)(2,1)} async-done(((bf16[2,4,64,768]{3,2,1,0:T(8,128)(2,1)}), bf16[2,4,256,768]{3,2,1,0:T(8,128)(2,1)}) %all-gather.5.cloned.1.call-update) | async-done | bytes 3145744 | tf_op jit(solution)/shard_map/all_gather | solution.py:170
  186.9 10.8 %fusion.53 = (bf16[2,4,64,12,64]{2,4,3,1,0:T(8,128)(2,1)}, f32[2,4,12,64,64]{3,4,2,1,0:T(8,128)}) fusion(f32[2,4,64,12]{2,3,1,0:T(8,128)} %bitcast.271, bf16[2,4,256,12,64]{2,4,3,1,0:T(8,128)(2,1)} %bitcast.253, f32[2,4,12,64,256]{4,3,2,1,0:T(8,128)} %copy-done.17, f32[2,4,12,64]{3,2,1,0:T(8,128)} %copy-done.72, ...), kind=kOutput, calls=%fused_computation.106 | convolution fusion | flops 1215037440 | bytes 11976704 | tf_op jit(solution)/shard_map/cghqk,cgkhe->cghqe/dot_general | solution.py:179
  239.8 10.7 %multiply_convert_fusion = (bf16[2,8,32,3072]{3,2,1,0:T(8,128)(2,1)}, f32[2,8,32,3072]{3,2,1,0:T(8,128)}) fusion(f32[3072]{0:T(1024)S(1)} %bitcast.289, bf16[2,10,34,3072]{3,2,1,0:T(8,128)(2,1)S(1)} %select_maximum_fusion.2, f32[3072]{0:T(1024)S(1)} %bitcast.287, bf16[2,1,32,3072]{3,2,1,0:T(8,128)(2,1)S(1)} %collective-permute-done.3, ...), kind=kLoop, calls=%fused_computation.59 | loop fusion | flops 58195968 | bytes 32354304 | tf_op jit(solution)/shard_map/convert_element_type | solution.py:201
  250.5 17.9 %fusion.34 = (bf16[3072]{0:T(1024)(128)(2,1)}, bf16[3072]{0:T(1024)(128)(2,1)}, bf16[3072]{0:T(1024)(128)(2,1)}, bf16[3072]{0:T(1024)(128)(2,1)}, bf16[3072]{0:T...) fusion(bf16[2,10,34,3072]{3,2,1,0:T(8,128)(2,1)S(1)} %select_ma, ...), kind=kOutput, calls=%fused_computation.58 | convolution fusion | flops 2500826112 | bytes 40949760 | tf_op jit(solution)/shard_map/dot_general | solution.py:211
  276.4 6.0 convolution_add_fusion.2
  285.3 8.5 fusion.150
  293.8 6.4 multiply_reduce_fusion
  316.8 28.3 %collective-permute-done.6 = bf16[2,2,4,64,768]{4,3,2,1,0:T(8,128)(2,1)} collective-permute-done((bf16[2,2,4,64,768]{4,3,2,1,0:T(8,128)(2,1)}, bf16[2,2,4,64,768]{4,3,2,1,0:T(8,128)(2,1)}, u32[]{:S(2)}, u32[]{:S(2)}) %collective-permute-start.6) | collective-permute-done | bytes 1572896 | tf_op jit(solution)/shard_map/ppermute | solution.py:36
  409.5 6.0 fusion.70
  451.7 6.9 convolution_convert_fusion.2
  458.7 8.5 collective-permute-done.9
  481.3 6.7 fusion.62
  527.5 13.6 %collective-permute-done.11 = bf16[2,2,4,64,768]{4,3,2,1,0:T(8,128)(2,1)} collective-permute-done((bf16[2,2,4,64,768]{4,3,2,1,0:T(8,128)(2,1)}, bf16[2,2,4,64,768]{4,3,2,1,0:T(8,128)(2,1)}, u32[]{:S(2)}, u32[]{:S(2)}) %collective-permute-start.11) | collective-permute-done | bytes 1572896 | tf_op jit(solution)/shard_map/ppermute | solution.py:36
  561.1 15.4 %collective-permute-done.12 = bf16[2,2,4,64,768]{4,3,2,1,0:T(8,128)(2,1)} collective-permute-done((bf16[2,2,4,64,768]{4,3,2,1,0:T(8,128)(2,1)}, bf16[2,2,4,64,768]{4,3,2,1,0:T(8,128)(2,1)}, u32[]{:S(2)}, u32[]{:S(2)}) %collective-permute-start.12) | collective-permute-done | bytes 1572896 | tf_op jit(solution)/shard_map/ppermute | solution.py:36
  582.0 5.9 reshape_reshape.16
  594.1 8.2 fusion.99
  629.1 10.9 %reduce-scatter.14.cloned.1.call-done = bf16[96,2304]{1,0:T(8,128)(2,1)} async-done(((bf16[768,2304]{1,0:T(8,128)(2,1)}), bf16[96,2304]{1,0:T(8,128)(2,1)}) %reduce-scatter.14.cloned.1.call-update) | async-done | bytes 442384 | tf_op jit(solution)/shard_map/reduce_scatter | solution.py:333
  670.1 53.4 %all-reduce.14.cloned.1.call-done = (bf16[2,4,4608]{2,1,0:T(4,128)(2,1)}, bf16[96,2304]{1,0:T(8,128)(2,1)}, bf16[96,768]{1,0:T(8,128)(2,1)}, bf16[96,3072]{1,0:T(8,128)(2,1)}, bf16[384,768]{1,0:T(8,128)(2,1)}) async-done(((bf16[2,4,4608]{2,1,0:T(4,128)(2,1)}, bf16[96,2304]{1,0:T(8,128)(2,1)}, bf16[96,768]{1,0:T(8,128)(2,1)}, bf16[96,3072]{1,0:T(8,128)(2,1)}, bf16[384,768]{1,0:T(8,128)(2,1)}), ...) | async-done | bytes 1843216 | tf_op jit(solution)/shard_map/psum | solution.py:318
  733.2 28.3 %reduce-scatter.24.cloned.1.call-done = bf16[384,9]{1,0:T(8,128)(2,1)} async-done(((bf16[3072,9]{1,0:T(8,128)(2,1)}), bf16[384,9]{1,0:T(8,128)(2,1)}) %reduce-scatter.24.cloned.1.call-update) | async-done | bytes 6928
  765.2 33.6 %reduce-scatter.22.cloned.1.call-done = bf16[96,9]{1,0:T(8,128)(2,1)} async-done(((bf16[768,9]{1,0:T(8,128)(2,1)}), bf16[96,9]{1,0:T(8,128)(2,1)}) %reduce-scatter.22.cloned.1.call-update) | async-done | bytes 1744
  801.3 23.9 %all-reduce.9 = (bf16[4608]{0:T(1024)(128)(2,1)}, bf16[1536]{0:T(1024)(128)(2,1)}, bf16[768]{0:T(1024)(128)(2,1)}, bf16[3072]{0:T(1024)(128)(2,1)}, bf16[768]{0:T(1024)(128)(2,1)}) all-reduce(bf16[4608]{0:T(1024)(128)(2,1)} %reduce_sum.344, ...), channel_id=3, replica_groups=mesh['canvas'=8,'rows'=4] {'canvas'}, use_global_device_ids=true, to_apply=%region_14.15.clone | all-reduce | flops 10752 | bytes 43008
  830.3 20.2 %all-reduce.10 = (bf16[9,96]{1,0:T(8,128)(2,1)}, bf16[192]{0:T(256)(128)(2,1)}, bf16[96]{0:T(256)(128)(2,1)}, bf16[384]{0:T(512)(128)(2,1)}, bf16[9,384]{1,0:T(8,128)(2,1)}, /*index=5*/bf16[96]{0:T(256)(128)(2,1)}) all-reduce(bf16[9,96]{1,0:T(8,128)(2,1)S(1)} %copy.151, ...), channel_id=1, replica_groups=mesh['canvas'=8,'rows'=4] {'rows'}, use_global_device_ids=true, to_apply=%region_24.25 | all-reduce | flops 5088 | bytes 20352 | tf_op jit(solution)/shard_map/psum | solution.py:308
  (473 shorter events, 423.9 us)
Async XLA Ops:
  7.2 110.9 %all-gather.3.cloned.1.call-start = ((), (), s32[]{:S(2)}) async-start(), calls=%async_computation.7 | async-start | bytes 3932160 | tf_op jit(solution)/shard_map/all_gather | solution.py:169
  23.9 7.7 collective-permute-start.1
  25.2 7.8 collective-permute-start
  49.6 132.6 %all-gather.5.cloned.1.call-start = ((), (), s32[]{:S(2)}) async-start(), calls=%async_computation.8 | async-start | bytes 3932160 | tf_op jit(solution)/shard_map/all_gather | solution.py:170
  50.4 578.7 %reduce-scatter.16.cloned.1.call-start = ((), (), s32[]{:S(2)}) async-start(), calls=%async_computation.11 | async-start | bytes 1327104 | tf_op jit(solution)/shard_map/reduce_scatter | solution.py:339
  223.6 12.9 %collective-permute-start.3 = (bf16[2,1,32,3072]{3,2,1,0:T(8,128)(2,1)S(1)}, bf16[2,1,32,3072]{3,2,1,0:T(8,128)(2,1)S(1)}, u32[]{:S(2)}, u32[]{:S(2)}) collective-permute-start(bf16[2,1,32,3072]{3,2,1,0:T(8,128)(2,1)S(1)} %get-tuple-element.79), channel_id=1, source_target_pairs={{1,0},{2,1},{3,2},{5,4},{6,5},{7,6},{9,8},{10,9},{11,10},{13,12},{... | collective-permute-start | bytes 1179656 | tf_op jit(solution)/shard_map/ppermute | solution.py:26
  225.0 12.6 %collective-permute-start.2 = (bf16[2,1,32,3072]{3,2,1,0:T(8,128)(2,1)S(1)}, bf16[2,1,32,3072]{3,2,1,0:T(8,128)(2,1)S(1)}, u32[]{:S(2)}, u32[]{:S(2)}) collective-permute-start(bf16[2,1,32,3072]{3,2,1,0:T(8,128)(2,1)S(1)} %get-tuple-element.78), channel_id=1, source_target_pairs={{0,1},{1,2},{2,3},{4,5},{5,6},{6,7},{8,9},{9,10},{10,11},{12,13},{... | collective-permute-start | bytes 1179656 | tf_op jit(solution)/shard_map/ppermute | solution.py:24
  269.6 12.8 %collective-permute-start.5 = (bf16[2,1,32,3072]{3,2,1,0:T(8,128)(2,1)S(1)}, bf16[2,1,32,3072]{3,2,1,0:T(8,128)(2,1)S(1)}, u32[]{:S(2)}, u32[]{:S(2)}) collective-permute-start(bf16[2,1,32,3072]{3,2,1,0:T(8,128)(2,1)S(1)} %get-tuple-element.77), channel_id=1, source_target_pairs={{1,0},{2,1},{3,2},{5,4},{6,5},{7,6},{9,8},{10,9},{11,10},{13,12},{... | collective-permute-start | bytes 1179656 | tf_op jit(solution)/shard_map/ppermute | solution.py:26
  270.9 12.2 %collective-permute-start.4 = (bf16[2,1,32,3072]{3,2,1,0:T(8,128)(2,1)S(1)}, bf16[2,1,32,3072]{3,2,1,0:T(8,128)(2,1)S(1)}, u32[]{:S(2)}, u32[]{:S(2)}) collective-permute-start(bf16[2,1,32,3072]{3,2,1,0:T(8,128)(2,1)S(1)} %get-tuple-element.76), channel_id=1, source_target_pairs={{0,1},{1,2},{2,3},{4,5},{5,6},{6,7},{8,9},{9,10},{10,11},{12,13},{... | collective-permute-start | bytes 1179656 | tf_op jit(solution)/shard_map/ppermute | solution.py:24
  305.8 323.2 %reduce-scatter.20.cloned.1.call-start = ((), (), s32[]{:S(2)}) async-start(), calls=%async_computation.13 | async-start | bytes 5308416 | tf_op jit(solution)/shard_map/reduce_scatter | solution.py:354
  308.7 36.4 %collective-permute-start.6 = (bf16[2,2,4,64,768]{4,3,2,1,0:T(8,128)(2,1)}, bf16[2,2,4,64,768]{4,3,2,1,0:T(8,128)(2,1)}, u32[]{:S(2)}, u32[]{:S(2)}) collective-permute-start(bf16[2,2,4,64,768]{4,3,2,1,0:T(8,128)(2,1)} %pad_maximum_fusion.4), channel_id=1, source_target_pairs={{3,0},{0,1},{1,2},{2,3},{7,4},{4,5},{5,6},{6,7},{11,8},{8,9},{9,10... | collective-permute-start | bytes 4718600 | tf_op jit(solution)/shard_map/ppermute | solution.py:36
  316.7 312.3 %reduce-scatter.18.cloned.1.call-start = ((), (), s32[]{:S(2)}) async-start(), calls=%async_computation.12 | async-start | bytes 5308416 | tf_op jit(solution)/shard_map/reduce_scatter | solution.py:345
  345.1 35.6 %collective-permute-start.7 = (bf16[2,2,4,64,768]{4,3,2,1,0:T(8,128)(2,1)}, bf16[2,2,4,64,768]{4,3,2,1,0:T(8,128)(2,1)}, u32[]{:S(2)}, u32[]{:S(2)}) collective-permute-start(bf16[2,2,4,64,768]{4,3,2,1,0:T(8,128)(2,1)} %collective-permute-done.6), channel_id=1, source_target_pairs={{3,0},{0,1},{1,2},{2,3},{7,4},{4,5},{5,6},{6,7},{11,8},{8,9},{9,10... | collective-permute-start | bytes 4718600 | tf_op jit(solution)/shard_map/ppermute | solution.py:36
  389.6 82.5 %collective-permute-start.8 = (bf16[2,2,4,64,768]{4,3,2,1,0:T(8,128)(2,1)}, bf16[2,2,4,64,768]{4,3,2,1,0:T(8,128)(2,1)}, u32[]{:S(2)}, u32[]{:S(2)}) collective-permute-start(bf16[2,2,4,64,768]{4,3,2,1,0:T(8,128)(2,1)} %collective-permute-done.7), channel_id=1, source_target_pairs={{3,0},{0,1},{1,2},{2,3},{7,4},{4,5},{5,6},{6,7},{11,8},{8,9},{9,10... | collective-permute-start | bytes 4718600 | tf_op jit(solution)/shard_map/ppermute | solution.py:36
  432.4 34.8 %collective-permute-start.9 = (bf16[2,2,4,64,768]{4,3,2,1,0:T(8,128)(2,1)}, bf16[2,2,4,64,768]{4,3,2,1,0:T(8,128)(2,1)}, u32[]{:S(2)}, u32[]{:S(2)}) collective-permute-start(bf16[2,2,4,64,768]{4,3,2,1,0:T(8,128)(2,1)} %pad_maximum_fusion.5), channel_id=1, source_target_pairs={{3,0},{0,1},{1,2},{2,3},{7,4},{4,5},{5,6},{6,7},{11,8},{8,9},{9,10... | collective-permute-start | bytes 4718600 | tf_op jit(solution)/shard_map/ppermute | solution.py:36
  458.6 181.4 %reduce-scatter.14.cloned.1.call-start = ((), (), s32[]{:S(2)}) async-start(), calls=%async_computation.10 | async-start | bytes 3981312 | tf_op jit(solution)/shard_map/reduce_scatter | solution.py:333
  471.7 33.4 %collective-permute-start.10 = (bf16[2,2,4,64,768]{4,3,2,1,0:T(8,128)(2,1)}, bf16[2,2,4,64,768]{4,3,2,1,0:T(8,128)(2,1)}, u32[]{:S(2)}, u32[]{:S(2)}) collective-permute-start(bf16[2,2,4,64,768]{4,3,2,1,0:T(8,128)(2,1)} %fusion.49), channel_id=1, source_target_pairs={{3,0},{0,1},{1,2},{2,3},{7,4},{4,5},{5,6},{6,7},{11,8},{8,9},{9,10... | collective-permute-start | bytes 4718600 | tf_op jit(solution)/shard_map/ppermute | solution.py:36
  509.0 32.2 %collective-permute-start.11 = (bf16[2,2,4,64,768]{4,3,2,1,0:T(8,128)(2,1)}, bf16[2,2,4,64,768]{4,3,2,1,0:T(8,128)(2,1)}, u32[]{:S(2)}, u32[]{:S(2)}) collective-permute-start(bf16[2,2,4,64,768]{4,3,2,1,0:T(8,128)(2,1)} %fusion.50), channel_id=1, source_target_pairs={{3,0},{0,1},{1,2},{2,3},{7,4},{4,5},{5,6},{6,7},{11,8},{8,9},{9,10... | collective-permute-start | bytes 4718600 | tf_op jit(solution)/shard_map/ppermute | solution.py:36
  545.1 31.4 %collective-permute-start.12 = (bf16[2,2,4,64,768]{4,3,2,1,0:T(8,128)(2,1)}, bf16[2,2,4,64,768]{4,3,2,1,0:T(8,128)(2,1)}, u32[]{:S(2)}, u32[]{:S(2)}) collective-permute-start(bf16[2,2,4,64,768]{4,3,2,1,0:T(8,128)(2,1)} %fusion.51), channel_id=1, source_target_pairs={{3,0},{0,1},{1,2},{2,3},{7,4},{4,5},{5,6},{6,7},{11,8},{8,9},{9,10... | collective-permute-start | bytes 4718600 | tf_op jit(solution)/shard_map/ppermute | solution.py:36
  593.8 129.7 %all-reduce.14.cloned.1.call-start = ((), (), s32[]{:S(2)}) async-start(), calls=%async_computation.16 | async-start | bytes 3686400 | tf_op jit(solution)/shard_map/psum | solution.py:318
  603.6 6.8 collective-permute-start.13
  640.0 121.4 %reduce-scatter.24.cloned.1.call-start = ((), (), s32[]{:S(2)}) async-start(), calls=%async_computation.15 | async-start | bytes 884736
  656.2 142.7 %reduce-scatter.22.cloned.1.call-start = ((), (), s32[]{:S(2)}) async-start(), calls=%async_computation.14 | async-start | bytes 221184
  669.8 200.2 %reduce-scatter.12.cloned.1.call-start = ((), (), s32[]{:S(2)}) async-start(), calls=%async_computation.9 | async-start | bytes 7962624 | tf_op jit(solution)/shard_map/reduce_scatter | solution.py:324
  (121 other events, 855.6 us)
Sparse Core Ops, SparseCore 0:
  49.8 68.2 all-gather.2
  119.7 62.5 all-gather.4
  306.0 38.0 reduce-scatter.15
  347.7 53.8 reduce-scatter.19
  458.7 55.7 reduce-scatter.17
  593.9 46.0 reduce-scatter.13
  643.6 79.8 all-reduce.13
  727.5 33.8 reduce-scatter.23
  765.4 33.4 reduce-scatter.21
  802.3 65.5 reduce-scatter.11
where the time goes:
time: 892 us; the launch traced here: 880 us
  waiting for transfers between devices  296 us (33%)
  local copies, waits for them, and re-layouts  195 us (22%)
  matrix products  174 us (20%)
  other arithmetic  102 us (11%)
  blocking collectives  63.9 us (7%)
  starting transfers between devices  30.1 us (3%)
  between operations  18.8 us (2%)
    ppermute x7, waiting for transfers between devices, passed_along(): return lax.ppermute(block, axis, route)  72.7 us
    unnamed x12, waiting for transfers between devices  62.8 us
    psum x1, waiting for transfers between devices, shards(): lax.psum(mod_grad.astype(jnp.bfloat16), 'rows').astype(jnp.float32)  53.4 us
    all_gather x1, waiting for transfers between devices, shards(): value_piece = lax.all_gather(value_rows, 'rows', axis=2, tiled=True)  49.5 us
    all_gather x1, waiting for transfers between devices, shards(): key_piece = lax.all_gather(key_rows, 'rows', axis=2, tiled=True)  37.6 us
    unnamed x251, local copies, waits for them, and re-layouts  30.1 us
    another operation x8, local copies, waits for them, and re-layouts, shards(): pending = pending + jnp.stack([key_part, value_part]).reshape(pending.shape)  24.3 us
    another operation x20, local copies, waits for them, and re-layouts, kernel_grad(): return jnp.stack(tap_sums)  24.3 us
  transfers between devices with their start and end apart: 25, of which 19 were waited for; matrix products, arithmetic and copies ran while one was open for 37% of the time, Pallas kernels for 0%

commit v1 on v0

--- a/solution.py
+++ b/solution.py
@@ -1,6 +1,10 @@
+from types import SimpleNamespace
+
 import jax
 import jax.numpy as jnp
 from jax import lax
+from jax.experimental import pallas as pl
+from jax.experimental.pallas import tpu as pltpu
 from jax.sharding import PartitionSpec as P
 
 HEADS = 12
@@ -11,6 +15,7 @@
 EPSILON = 1e-06
 NEG_FILL = -1e30
 PRECISE = lax.Precision.HIGHEST
+VMEM_LIMIT = 65400 * 2**10
 
 
 def padded_2(cells, sides, width):
@@ -379,6 +384,1203 @@
         shares[11],
     )
 
+BF = jnp.bfloat16
+F32 = jnp.float32
+D = 768
+FF = 3072
+HB = 384
+BIG = -1e30
+
+
+def dot(a, b):
+    return jnp.dot(a, b, preferred_element_type=F32)
+
+
+def dot_t(a, b):
+    return lax.dot_general(a, b, (((1,), (1,)), ((), ())), preferred_element_type=F32)
+
+
+def dot_l(a, b):
+    return lax.dot_general(a, b, (((0,), (0,)), ((), ())), preferred_element_type=F32)
+
+
+def iota(shape, dim):
+    return lax.broadcasted_iota(jnp.int32, shape, dim)
+
+
+def ones_where(mask):
+    return jnp.where(mask, 1.0, 0.0).astype(BF)
+
+
+def taps_of(pr, pc, back):
+    found = []
+    for i in range(3):
+        for j in range(3):
+            di, dj = (1 - i, 1 - j) if back else (i - 1, j - 1)
+            gr = pr if di == 0 else 1 - pr
+            gc = pc if dj == 0 else 1 - pc
+            ro = 0 if di == 0 else (pr - 1 if di < 0 else pr)
+            co = 0 if dj == 0 else (2 * pc + dj - 1) // 2
+            found.append((3 * i + j, 2 * gr + gc, ro, co != 0))
+    return found
+
+
+def shifted(rows, pc):
+    n = rows.shape[0]
+    col = iota(rows.shape, 0) % 16
+    if pc == 1:
+        return jnp.where(col == 0, 0.0, pltpu.roll(rows, 1, 0))
+    return jnp.where(col == 15, 0.0, pltpu.roll(rows, n - 1, 0))
+
+
+def norm_parts(v):
+    mean = jnp.mean(v, axis=-1, keepdims=True)
+    cen = v - mean
+    inv = lax.rsqrt(jnp.mean(cen * cen, axis=-1, keepdims=True) + EPSILON)
+    return cen * inv, inv
+
+
+def norm_back(n, nrm, inv):
+    m1 = jnp.mean(n, axis=-1, keepdims=True)
+    m2 = jnp.mean(n * nrm, axis=-1, keepdims=True)
+    return (n - m1 - nrm * m2) * inv
+
+
+SCRATCH = dict(
+    stg_t=((2, 4, 64, D), BF),
+    stg_c=((2, 4, 64, D), BF),
+    tok=((4, 256, D), BF),
+    cot=((4, 256, D), BF),
+    latc=((4, 1, 256), jnp.int32),
+    lv=((4, 256, 128), F32),
+    oh=((4, 256, 128), BF),
+    modhl=((32, 6 * D), BF),
+    pm=((256, 256), BF),
+    ain=((4, 288, D), BF),
+    c1t=((D, 1024), BF),
+    tmpa=((4, 256, D), BF),
+    qkv=((4, 256, 3 * HB), BF),
+    att=((4, 256, D), BF),
+    fint=((D, 1024), BF),
+    bg=((4, 256, D), BF),
+    mid=((2, 256, D), F32),
+    ub=((4, 288, HB), BF),
+    us=((4, 288, HB), BF),
+    gb=((4, 288, HB), BF),
+    gs=((4, 288, HB), BF),
+    gp=((2, 256, D), F32),
+    act=((4, 256, 2 * D), BF),
+    upg=((4, 256, 2 * D), BF),
+    actt=((HB, 1024), BF),
+    wup=((D, 2 * D), BF),
+    wdn=((2 * D, D), BF),
+    wq=((D, 3 * HB), BF),
+    wo=((D, D), BF),
+    gwd=((4, HB, D), BF),
+    gwu=((4, 192, 2 * D), BF),
+    gwo=((4, 96, D), BF),
+    rd_a=((192, D), BF),
+    rd_b=((192, D), BF),
+    rd_x=((HB, D), BF),
+    rd_y=((HB, D), BF),
+    ru_a=((96, 2 * D), BF),
+    ru_b=((96, 2 * D), BF),
+    ru_x=((192, 2 * D), BF),
+    ru_y=((192, 2 * D), BF),
+    rq_a=((96, 3 * HB), BF),
+    rq_b=((96, 3 * HB), BF),
+    rq_x=((192, 3 * HB), BF),
+    rq_y=((192, 3 * HB), BF),
+    ro_a=((48, D), BF),
+    ro_b=((48, D), BF),
+    ro_x=((96, D), BF),
+    ro_y=((96, D), BF),
+    su=((96, 2 * D), BF),
+    sq=((96, 3 * HB), BF),
+    zd_a=((HB, D), BF),
+    zd_b=((HB, D), BF),
+    zu_a=((96, FF), BF),
+    zu_b=((96, FF), BF),
+    zq_a=((96, 3 * D), BF),
+    zq_b=((96, 3 * D), BF),
+    zo_a=((96, D), BF),
+    zo_b=((96, D), BF),
+    frcv=((2, 4, 64, D), BF),
+    brcv=((2, 4, 64, D), BF),
+    oland=((2, 4, 64, D), BF),
+    gland=((2, 4, 64, D), BF),
+    condc=((16, D), F32),
+    clow=((4, 16, D), BF),
+    mg1=((16, D), F32),
+    mg2=((16, HB), F32),
+    mgs1=((16, D), BF),
+    mgr1=((16, D), BF),
+    mgs2=((16, HB), BF),
+    mgr2=((16, HB), BF),
+    mga1=((16, 16, D), BF),
+    mga2=((16, 16, HB), BF),
+    sg1=((16, FF), F32),
+    sg1s=((1, 16, FF), BF),
+    sg1r=((5, 16, FF), BF),
+    sg2=((16, D), F32),
+    sg2s=((1, 16, D), BF),
+    sg2r=((5, 16, D), BF),
+    cgsum=((16, D), F32),
+    crcv=((2, 8, D), F32),
+)
+N_SEMS = 208
+
+
+def whole_block(
+    tok_h, cot_h, lat_h, cond_r, wada_h, par, wqkv_h, wout_h, wup_h, wdn_h,
+    o_out, o_gin, o_cond, o_wada, o_bada, o_sg1, o_sg2, o_wqkv, o_wout, o_wup, o_wdn,
+    sems, *bufs,
+):
+    v = SimpleNamespace(**dict(zip(SCRATCH, bufs)))
+    stg_t, stg_c, tok, cot, latc, lv, oh = v.stg_t, v.stg_c, v.tok, v.cot, v.latc, v.lv, v.oh
+    modhl, pm, ain, c1t, tmpa, qkv, att = v.modhl, v.pm, v.ain, v.c1t, v.tmpa, v.qkv, v.att
+    fint, bg, mid, ub, us, gb, gs = v.fint, v.bg, v.mid, v.ub, v.us, v.gb, v.gs
+    gp, act, upg, actt, wup, wdn, wq, wo = v.gp, v.act, v.upg, v.actt, v.wup, v.wdn, v.wq, v.wo
+    gwd, gwu, gwo, condc, clow = v.gwd, v.gwu, v.gwo, v.condc, v.clow
+
+    c = lax.axis_index("canvas")
+    r = lax.axis_index("rows")
+    k = c % 2
+    x = (c // 2) % 2
+    y = c // 4
+    col = 2 * y + x
+    r1 = r + 1 - 2 * (r % 2)
+    r2 = (r + 2) % 4
+    r3 = 3 - r
+    sib = (y * 4 + x * 2 + 1 - k, r)
+    px = (y * 4 + (1 - x) * 2 + k, r)
+    py = ((1 - y) * 4 + x * 2 + k, r)
+    owner = r // 2
+    is_own = k == owner
+    owner_c = y * 4 + x * 2 + owner
+
+    count = [0]
+
+    def sem(n=1):
+        first = count[0]
+        count[0] += n
+        return first
+
+    last = []
+
+    def remote(src, dst, ss, rs, dev):
+        return pltpu.make_async_remote_copy(
+            src_ref=src, dst_ref=dst, send_sem=sems.at[ss], recv_sem=sems.at[rs],
+            device_id=dev, device_id_type=pl.DeviceIdType.MESH,
+        )
+
+    def local(src, dst, s):
+        return pltpu.make_async_copy(src, dst, sems.at[s])
+
+    def swap(src, dst, dev):
+        cp = remote(src, dst, sem(), sem(), dev)
+        cp.start()
+        last.append(cp.wait_send)
+        return cp
+
+    barrier = pltpu.get_barrier_semaphore()
+    for dev in (sib, px, py, (c, r1), (c, r2), (c, r3), (sib[0], r1), (sib[0], r2), (sib[0], r3)):
+        pl.semaphore_signal(barrier, inc=1, device_id=dev, device_id_type=pl.DeviceIdType.MESH)
+    s_tok = sem()
+    s_cot = sem()
+    ld_tok = local(tok_h, act.at[pl.ds(0, 2), :, pl.ds(0, D)], s_tok)
+    ld_tok.start()
+    ld_cot = local(cot_h, act.at[pl.ds(0, 2), :, pl.ds(D, D)], s_cot)
+    ld_cot.start()
+    s_wa = sem(2)
+
+    def load_ada(p):
+        return local(wada_h.at[:, pl.ds(p * D, D)], wup.at[:, pl.ds((p % 2) * D, D)], s_wa + p % 2)
+
+    load_ada(0).start()
+    load_ada(1).start()
+    s_w = sem(3)
+    ld_wq = [
+        local(wqkv_h.at[:, pl.ds(pl.multiple_of(part * D + HB * k, 128), HB)], wq.at[:, pl.ds(part * HB, HB)], s_w + part)
+        for part in range(3)
+    ]
+    for cp in ld_wq:
+        cp.start()
+    ld_wo = local(wout_h, wo, sem())
+    ld_wo.start()
+    s_wd = sem(4)
+    ld_wd = [
+        local(wdn_h.at[pl.ds(pl.multiple_of(HB * (2 * b + k), 128), HB), :], wdn.at[pl.ds(HB * b, HB), :], s_wd + b)
+        for b in range(4)
+    ]
+    for cp in ld_wd:
+        cp.start()
+    pi = iota((256, 256), 0)
+    group, place = pi // 64, pi % 64
+    nat = (2 * (place // 16) + group // 2) * 32 + 2 * (place % 16) + group % 2
+    pm[...] = ones_where(iota((256, 256), 1) == nat)
+    for buf in (ain, ub, us, gb, gs):
+        wide = buf.shape[2]
+        for g in range(4):
+            buf[g, 0:16, :] = jnp.zeros((16, wide), BF)
+            buf[g, 272:288, :] = jnp.zeros((16, wide), BF)
+    condc[pl.ds(pl.multiple_of(8 * k, 8), 8), :] = cond_r[...]
+    pl.semaphore_wait(barrier, 9)
+
+    cond_cp = swap(
+        condc.at[pl.ds(pl.multiple_of(8 * k, 8), 8), :], condc.at[pl.ds(pl.multiple_of(8 * k, 8), 8), :], sib
+    )
+    mine64 = pl.ds(pl.multiple_of(r * 64, 64), 64)
+    rt, rl, rc = sem(4), sem(4), sem(4)
+    st, sl, sc = sem(2), sem(2), sem(2)
+
+    def give(src, dst, ss, rs, i):
+        q = 2 * k + i
+        far = remote(src, dst, ss, rs, (c, q))
+        near = local(src, dst, rs)
+
+        @pl.when(q != r)
+        def _():
+            far.start()
+
+        @pl.when(q == r)
+        def _():
+            near.start()
+
+        def done():
+            @pl.when(q != r)
+            def _():
+                far.wait_send()
+
+        return done
+
+    tok_sent, cot_sent = [], []
+    ld_tok.wait()
+    for i in range(2):
+        stg_t[i] = dot(pm[...], act[i, :, 0:D]).astype(BF).reshape(4, 64, D)
+        tok_sent.append(give(stg_t.at[i], tok.at[:, mine64, :], st + i, rt + r, i))
+        last.append(give(lat_h.at[i], latc.at[r], sl + i, rl + r, i))
+    ld_cot.wait()
+    for i in range(2):
+        stg_c[i] = dot(pm[...], act[i, :, D : 2 * D]).astype(BF).reshape(4, 64, D)
+        cot_sent.append(give(stg_c.at[i], cot.at[:, mine64, :], sc + i, rc + r, i))
+
+    cond_cp.wait_recv()
+    cond = condc[...]
+    sig = 1.0 / (1.0 + jnp.exp(-cond))
+    mine_low = (cond * sig).astype(BF)
+    clow[col] = mine_low
+    low_x = swap(clow.at[col], clow.at[col], px)
+    for p in range(6):
+        load_ada(p).wait()
+        mod = dot(mine_low, wup[:, (p % 2) * D : (p % 2) * D + D])
+        mod = mod + par[14 + p // 4 : 15 + p // 4, (p % 4) * D : (p % 4) * D + D]
+        high = mod.astype(BF)
+        modhl[0:16, p * D : (p + 1) * D] = high
+        modhl[16:32, p * D : (p + 1) * D] = (mod - high.astype(F32)).astype(BF)
+        if p + 2 < 6:
+            load_ada(p + 2).start()
+    s_wu = sem(4)
+    ld_wu = [
+        local(wup_h.at[:, pl.ds(pl.multiple_of(HB * (2 * b + k), 128), HB)], wup.at[:, pl.ds(HB * b, HB)], s_wu + b)
+        for b in range(4)
+    ]
+    for cp in ld_wu:
+        cp.start()
+
+    def piece(o, p):
+        return dot(o[:, 0:32], modhl[:, p * D : (p + 1) * D])
+
+    ft, fl, fc = sem(4), sem(4), sem(4)
+    order = (r, r1, r2, r3)
+
+    def arrive(buf, of, rs, fs):
+        passed = []
+        for d in range(4):
+            s = order[d]
+            place = of(s)
+            cp = remote(buf.at[place], buf.at[place], fs + d, rs + s, sib)
+            cp.wait_recv()
+
+            @pl.when(is_own)
+            def _():
+                cp.start()
+
+            def done(cp=cp):
+                @pl.when(is_own)
+                def _():
+                    cp.wait_send()
+
+            passed.append(done)
+        return passed
+
+    def slab(s):
+        return (slice(None), pl.ds(pl.multiple_of(s * 64, 64), 64), slice(None))
+
+    last.extend(arrive(latc, lambda s: s, rl, fl))
+    tok_passed = arrive(tok, slab, rt, ft)
+
+    for s in range(4):
+        rows = jnp.broadcast_to(latc[s].astype(F32), (128, 256)).astype(BF)
+        ids = dot_t(pm[...], rows)
+        for g in range(4):
+            lv[g, s * 64 : s * 64 + 64, :] = ids[g * 64 : g * 64 + 64]
+    for g in range(4):
+        lane = iota((256, 128), 1)
+        want = (lane % 16 - 4 * r).astype(F32)
+        oh[g] = ones_where((want == lv[g]) & (lane < 32))
+
+    def norm_one(n, _):
+        t0 = pl.multiple_of((n % 2) * 128, 128)
+        for pc in range(2):
+            g = 2 * (n // 2) + pc
+            nrm, _inv = norm_parts(tok[g, pl.ds(t0, 128), :].astype(F32))
+            o = oh[g, pl.ds(t0, 128), :]
+            h = (nrm * (1.0 + piece(o, 1)) + piece(o, 0)).astype(BF)
+            ain[g, pl.ds(t0 + 16, 128), :] = h
+            sh = shifted(h.astype(F32), pc).astype(BF)
+            us[g, pl.ds(t0 + 16, 128), :] = sh[:, 0:HB]
+            gs[g, pl.ds(t0 + 16, 128), :] = sh[:, HB:D]
+        return 0
+
+    lax.fori_loop(0, 4, norm_one, 0)
+
+    for hh in range(2):
+        side = us if hh == 0 else gs
+
+        def conv_one(lt, _, hh=hh, side=side):
+            l0 = pl.multiple_of(lt * 128, 128)
+            la = pl.multiple_of(hh * HB + lt * 128, 128)
+            kr = [par[11 + t // 4 : 12 + t // 4, pl.ds((t % 4) * D + la, 128)] for t in range(9)]
+            for g in range(4):
+                for h in range(2):
+                    acc = None
+                    for t, gsrc, ro, moved in taps_of(g // 2, g % 2, False):
+                        rows = pl.ds(16 + 16 * ro + 128 * h, 128)
+                        src = side[gsrc, rows, pl.ds(l0, 128)] if moved else ain[gsrc, rows, pl.ds(la, 128)]
+                        term = src.astype(F32) * kr[t]
+                        acc = term if acc is None else acc + term
+                    low = acc.astype(BF)
+                    tmpa[g, h * 128 : h * 128 + 128, pl.ds(la, 128)] = low
+                    c1t[pl.ds(la, 128), g * 256 + h * 128 : g * 256 + h * 128 + 128] = low.astype(F32).T.astype(BF)
+            return 0
+
+        lax.fori_loop(0, 3, conv_one, 0)
+
+    for cp in ld_wq:
+        cp.wait()
+    kcol = pl.multiple_of(HB * k, 128)
+    b_q = par[10:11, pl.ds(2 * D + kcol, HB)]
+    b_v = par[10:11, pl.ds(3 * D + kcol, HB)]
+
+    def project(g, _):
+        got = dot(tmpa[g], wq[...])
+        qkv[g, :, 0:HB] = ((got[:, 0:HB] + b_q).astype(BF).astype(F32) * 0.125).astype(BF)
+        qkv[g, :, HB : 2 * HB] = got[:, HB : 2 * HB].astype(BF)
+        qkv[g, :, 2 * HB : 3 * HB] = (got[:, 2 * HB : 3 * HB] + b_v).astype(BF)
+        return 0
+
+    lax.fori_loop(0, 4, project, 0)
+
+    lane1 = iota((1, 128), 1)
+    lmf = [jnp.where(lane1 < 64, 1.0, 0.0), jnp.where(lane1 < 64, 0.0, 1.0)]
+    lmb = [m.astype(BF) for m in lmf]
+    sa, ra = sem(4), sem(4)
+
+    def masks_of(g):
+        lane = iota((256, 128), 1)
+        same = lane.astype(F32) == lv[g]
+        oq = jnp.where(same & (lane < 4), 1.0, 0.0).astype(BF)
+        mk = jnp.where(same | (lane >= 4), 0.0, BIG).astype(BF)
+        return oq, mk
+
+    def att_copy(g):
+        place = att.at[g, :, pl.ds(kcol, HB)]
+        return remote(place, place, sa + g, ra + g, sib)
+
+    def attend(g, _):
+        oq, mk = masks_of(g)
+        for hp in range(3):
+            qp = qkv[g, :, hp * 128 : hp * 128 + 128]
+            ka = jnp.concatenate([qkv[g, :, HB + hp * 128 : HB + hp * 128 + 128], mk], axis=1)
+            vp = qkv[g, :, 2 * HB + hp * 128 : 2 * HB + hp * 128 + 128]
+            mixed = None
+            for h in range(2):
+                s = dot_t(jnp.concatenate([qp * lmb[h], oq], axis=1), ka)
+                e = jnp.exp(s - jnp.max(s, axis=1, keepdims=True))
+                o = dot(e.astype(BF), vp) * (lmf[h] / jnp.sum(e, axis=1, keepdims=True))
+                mixed = o if h == 0 else mixed + o
+            att[g, :, pl.ds(pl.multiple_of(kcol + hp * 128, 128), 128)] = mixed.astype(BF)
+        att_copy(g).start()
+        return 0
+
+    lax.fori_loop(0, 4, attend, 0)
+    low_x.wait_recv()
+    low_y = swap(clow.at[pl.ds(2 * y, 2)], clow.at[pl.ds(2 * y, 2)], py)
+    last.extend(arrive(cot, slab, rc, fc))
+
+    ld_wo.wait()
+    kother = pl.multiple_of(HB * (1 - k), 128)
+
+    def norm_two(g, _):
+        for h in range(2):
+            rows = slice(h * 128, h * 128 + 128)
+            a = att[g, rows, :]
+            ao = dot(a, wo[...]) + par[10:11, D : 2 * D]
+            o = oh[g, rows, :]
+            m = tok[g, rows, :].astype(F32) + piece(o, 2) * ao
+            nrm, _inv = norm_parts(m)
+            f = (nrm * (1.0 + piece(o, 4)) + piece(o, 3)).astype(BF)
+            tmpa[g, rows, :] = f
+            at = pl.ds(pl.multiple_of(g * 256 + h * 128, 128), 128)
+            fint[:, at] = f.astype(F32).T.astype(BF)
+            bg[g, rows, :] = (piece(o, 5) * cot[g, rows, :].astype(F32)).astype(BF)
+        return 0
+
+    for g in range(4):
+        att_copy(g).wait()
+    lax.fori_loop(0, 4, norm_two, 0)
+
+    class Scatter:
+        def __init__(self, src, a, b, rx, ry):
+            self.src, self.a, self.b, self.rx, self.ry = src, a, b, rx, ry
+            n = a.shape[0]
+            self.n = n
+            ss = sem(8)
+            wide = a.shape[1]
+            ln = pl.ds(0, wide)
+            self.ln = slice(0, wide)
+            self.ca = remote(src.at[0, pl.ds(0, n), ln], a, ss, ss + 1, px)
+            self.cb = remote(src.at[0, pl.ds(n, n), ln], b, ss + 2, ss + 3, py)
+            self.cx = remote(src.at[1, :, ln], rx, ss + 4, ss + 5, px)
+            self.cy = remote(src.at[2, :, ln], ry, ss + 6, ss + 7, py)
+
+        def s0(self):
+            self.ca.start()
+            self.cb.start()
+
+        def s1(self):
+            self.cb.wait_recv()
+            n = self.n
+            self.src[1, n : 2 * n, self.ln] = (
+                self.src[1, n : 2 * n, self.ln].astype(F32) + self.b[...].astype(F32)
+            ).astype(BF)
+            self.cx.start()
+
+        def s2(self):
+            self.ca.wait_recv()
+            n = self.n
+            self.src[2, 0:n, self.ln] = (self.src[2, 0:n, self.ln].astype(F32) + self.a[...].astype(F32)).astype(BF)
+            self.cy.start()
+
+        def s3(self):
+            self.cx.wait_recv()
+            self.cy.wait_recv()
+            return self.src[3, :, self.ln].astype(F32) + self.rx[...].astype(F32) + self.ry[...].astype(F32)
+
+        def sent(self):
+            for cp in (self.ca, self.cb, self.cx, self.cy):
+                cp.wait_send()
+
+    inner = (r % 3) != 0
+
+    class Line:
+        def __init__(self, out, za, zb):
+            self.out, self.za, self.zb = out, za, zb
+            ss = sem(6)
+            self.up = remote(out, za, ss, ss + 1, (c, r1))
+            self.mid = remote(out, zb, ss + 2, ss + 3, (c, r3))
+            self.down = remote(out, za, ss + 4, ss + 5, (c, r1))
+
+        def s0(self):
+            @pl.when(jnp.logical_not(inner))
+            def _():
+                self.up.start()
+
+        def s1(self):
+            @pl.when(inner)
+            def _():
+                self.up.wait_recv()
+                self.out[...] = (self.out[...].astype(F32) + self.za[...].astype(F32)).astype(BF)
+                self.mid.start()
+
+        def s2(self):
+            @pl.when(inner)
+            def _():
+                self.mid.wait()
+                self.out[...] = (self.out[...].astype(F32) + self.zb[...].astype(F32)).astype(BF)
+                self.down.start()
+
+        def s3(self):
+            @pl.when(inner)
+            def _():
+                self.down.wait_send()
+
+            @pl.when(jnp.logical_not(inner))
+            def _():
+                self.up.wait_send()
+                self.down.wait_recv()
+                self.out[...] = self.za[...]
+
+    class Everyone:
+        def __init__(self, total, send, recv):
+            self.total, self.send, self.recv = total, send, recv
+            ss = sem(10)
+            devs = (sib, px, py, (c, r1), (c, r2))
+            self.cps = [remote(send.at[0], recv.at[i], ss + 2 * i, ss + 2 * i + 1, devs[i]) for i in range(5)]
+
+        def go(self, i):
+            self.send[0] = self.total[...].astype(BF)
+            self.cps[i].start()
+
+        def end(self, i):
+            self.cps[i].wait()
+            self.total[...] = self.send[0].astype(F32) + self.recv[i].astype(F32)
+
+    sum_d = Scatter(gwd, v.rd_a, v.rd_b, v.rd_x, v.rd_y)
+    sum_u = Scatter(gwu, v.ru_a, v.ru_b, v.ru_x, v.ru_y)
+    sum_o = Scatter(gwo, v.ro_a, v.ro_b, v.ro_x, v.ro_y)
+    sum_q = Scatter(gwu, v.rq_a, v.rq_b, v.rq_x, v.rq_y)
+    line_d = Line(o_wdn, v.zd_a, v.zd_b)
+    line_u = Line(o_wup, v.zu_a, v.zu_b)
+    line_o = Line(o_wout, v.zo_a, v.zo_b)
+    line_q = Line(o_wqkv, v.zq_a, v.zq_b)
+    sg1, sg2 = v.sg1, v.sg2
+    all1 = Everyone(sg1, v.sg1s, v.sg1r)
+    all2 = Everyone(sg2, v.sg2s, v.sg2r)
+    sg1[...] = jnp.zeros((16, FF), F32)
+    sg2[...] = jnp.zeros((16, D), F32)
+
+    def block_at(pos):
+        fx = 1 - pos // 2
+        fy = 1 - pos % 2
+        bx = x + fx - 2 * x * fx
+        by = y + fy - 2 * y * fy
+        return 2 * by + bx
+
+    for cp in ld_wd + ld_wu:
+        cp.wait()
+
+    def hidden(pos, _):
+        b = block_at(pos)
+        lo = pl.multiple_of(b * HB, 128)
+        wide = pl.multiple_of(HB * (2 * b + k), 128)
+
+        def up(pr, _):
+            for pc in range(2):
+                g = 2 * pr + pc
+                u = (dot(tmpa[g], wup[:, pl.ds(lo, HB)]) + par[9:10, pl.ds(wide, HB)]).astype(BF)
+                ub[g, 16:272, :] = u
+                us[g, 16:272, :] = shifted(u.astype(F32), pc).astype(BF)
+            return 0
+
+        lax.fori_loop(0, 2, up, 0)
+
+        def conv_gelu(lt, _):
+            l0 = pl.multiple_of(lt * 128, 128)
+            ln = pl.ds(l0, 128)
+            kr = [par[t : t + 1, pl.ds(wide + l0, 128)] for t in range(9)]
+            for g in range(4):
+                for h in range(2):
+                    acc = None
+                    for t, gsrc, ro, moved in taps_of(g // 2, g % 2, False):
+                        src = (us if moved else ub)[gsrc, pl.ds(16 + 16 * ro + 128 * h, 128), ln]
+                        term = src.astype(F32) * kr[t]
+                        acc = term if acc is None else acc + term
+                    sq = acc * acc
+                    th = jnp.tanh(0.7978845608028654 * acc * (1.0 + 0.044715 * sq))
+                    half = 0.5 + 0.5 * th
+                    low = (acc * half).astype(BF)
+                    slope = half + half * (1.0 - th) * acc * (0.7978845608028654 + 0.10703222440890037 * sq)
+                    rows = slice(h * 128, h * 128 + 128)
+                    act[g, rows, pl.ds(lo + l0, 128)] = low
+                    gp[g // 2, rows, pl.ds((g % 2) * HB + l0, 128)] = slope
+                    actt[ln, g * 256 + h * 128 : g * 256 + h * 128 + 128] = low.astype(F32).T.astype(BF)
+            return 0
+
+        lax.fori_loop(0, 3, conv_gelu, 0)
+
+        def down_grad(pr, _):
+            for pc in range(2):
+                g = 2 * pr + pc
+                t = dot_t(bg[g], wdn[pl.ds(lo, HB), :]) * gp[pr, :, pc * HB : pc * HB + HB]
+                t = t.astype(BF)
+                gb[g, 16:272, :] = t
+                gs[g, 16:272, :] = shifted(t.astype(F32), pc).astype(BF)
+            return 0
+
+        lax.fori_loop(0, 2, down_grad, 0)
+
+        def conv_back(lt, _):
+            l0 = pl.multiple_of(lt * 128, 128)
+            ln = pl.ds(l0, 128)
+            kr = [par[t : t + 1, pl.ds(wide + l0, 128)] for t in range(9)]
+            gk = [jnp.zeros((8, 128), F32) for _ in range(10)]
+            for g in range(4):
+                for h in range(2):
+                    here = ub[g, 16 + 128 * h : 144 + 128 * h, ln].astype(F32)
+                    acc = None
+                    for t, gsrc, ro, moved in taps_of(g // 2, g % 2, True):
+                        src = (gs if moved else gb)[gsrc, pl.ds(16 + 16 * ro + 128 * h, 128), ln].astype(F32)
+                        term = src * kr[t]
+                        acc = term if acc is None else acc + term
+                        gk[t] = gk[t] + jnp.sum((src * here).reshape(16, 8, 128), axis=0)
+                    low = acc.astype(BF)
+                    upg[g, h * 128 : h * 128 + 128, pl.ds(lo + l0, 128)] = low
+                    gk[9] = gk[9] + jnp.sum(low.astype(F32).reshape(16, 8, 128), axis=0)
+            for t in range(10):
+                sg1[t : t + 1, pl.ds(wide + l0, 128)] = jnp.sum(gk[t], axis=0, keepdims=True)
+            return 0
+
+        lax.fori_loop(0, 3, conv_back, 0)
+
+        def grad_down(n, _):
+            rows = pl.ds(pl.multiple_of(n * 128, 128), 128)
+            gwd[pos, rows, :] = dot(actt[rows, :], bg[...].reshape(1024, D)).astype(BF)
+            return 0
+
+        lax.fori_loop(0, 3, grad_down, 0)
+        pl.when(pos == 0)(sum_d.s0)
+        pl.when(pos == 1)(sum_d.s1)
+        pl.when(pos == 2)(sum_d.s2)
+        return 0
+
+    lax.fori_loop(0, 4, hidden, 0)
+
+    for done in tok_sent + cot_sent:
+        done()
+
+    def give_half(jj, _):
+        g = 2 * (1 - k) + jj
+        stg_t[jj] = dot_t(upg[g], wup[...]).astype(BF).reshape(4, 64, D)
+        return 0
+
+    lax.fori_loop(0, 2, give_half, 0)
+    f_cp = remote(stg_t, v.frcv, sem(), sem(), sib)
+    f_cp.start()
+
+    def give_branch(jj, _):
+        g = 2 * (1 - k) + jj
+        stg_c[jj] = dot(act[g], wdn[...]).astype(BF).reshape(4, 64, D)
+        return 0
+
+    lax.fori_loop(0, 2, give_branch, 0)
+    b_cp = remote(stg_c, v.brcv, sem(), sem(), sib)
+    b_cp.start()
+
+    def grad_up(pos, _):
+        b = block_at(pos)
+        rows = pl.ds(pl.multiple_of(b * 192, 64), 192)
+
+        def part(nt, _):
+            ln = pl.ds(pl.multiple_of(nt * HB, 128), HB)
+            gwu[pos, :, ln] = dot(fint[rows, :], upg[:, :, ln].reshape(1024, HB)).astype(BF)
+            return 0
+
+        lax.fori_loop(0, 4, part, 0)
+        pl.when(pos == 0)(sum_u.s0)
+        return 0
+
+    lax.fori_loop(0, 4, grad_up, 0)
+    f_cp.wait()
+    b_cp.wait()
+
+    mg1, mg2 = v.mg1, v.mg2
+    mg1[...] = jnp.zeros((16, D), F32)
+    mg2[...] = jnp.zeros((16, HB), F32)
+    o_rows = jnp.zeros((1, D), F32)
+
+    def place_rows(ids, p):
+        lane = iota((128, 128), 1)
+        return ones_where((lane - 4 * p).astype(F32) == ids)
+
+    def two_back(n, carry):
+        bd, bo = carry
+        jj = n // 2
+        g = 2 * k + jj
+        t0 = pl.multiple_of((n % 2) * 128, 128)
+        rows = pl.ds(t0, 128)
+        h64 = pl.ds((n % 2) * 2, 2)
+        o = oh[g, rows, :]
+        gate1 = piece(o, 2)
+        ao = dot(att[g, rows, :], wo[...]) + par[10:11, D : 2 * D]
+        m = tok[g, rows, :].astype(F32) + gate1 * ao
+        nrm, inv = norm_parts(m)
+        fg = dot_t(upg[g, rows, :], wup[...]) + v.frcv[jj, h64].reshape(128, D).astype(F32)
+        cotf = cot[g, rows, :].astype(F32)
+        mg = cotf + norm_back(fg * (1.0 + piece(o, 4)), nrm, inv)
+        mid[jj, rows, :] = mg
+        ag = (gate1 * mg).astype(BF)
+        tmpa[g, rows, :] = ag
+        branch = dot(act[g, rows, :], wdn[...]) + v.brcv[jj, h64].reshape(128, D).astype(F32) + par[10:11, 0:D]
+        stg_c[jj, h64] = (m + piece(o, 5) * branch).astype(BF).reshape(2, 64, D)
+        ids = lv[g, rows, :]
+        total = dot_l(place_rows(ids, 0), (mg * ao).astype(BF))
+        total = total + dot_l(place_rows(ids, 1), fg.astype(BF))
+        total = total + dot_l(place_rows(ids, 2), (fg * nrm).astype(BF))
+        total = total + dot_l(place_rows(ids, 3), (cotf * branch).astype(BF))
+        mg1[...] += total[0:16]
+        bd = bd + jnp.sum(bg[g, rows, :].astype(F32), axis=0, keepdims=True)
+        bo = bo + jnp.sum(ag.astype(F32), axis=0, keepdims=True)
+        return bd, bo
+
+    bd, bo = lax.fori_loop(0, 4, two_back, (o_rows, o_rows))
+    ag_place = tmpa.at[pl.ds(2 * k, 2)]
+    ag_cp = swap(ag_place, ag_place, sib)
+    sg1[10:11, 0:D] = bd
+    sg1[10:11, D : 2 * D] = bo
+
+    def hand_back(src, land, rs):
+        ss = sem(4)
+        for s in range(4):
+            dst = land.at[r % 2, pl.ds(2 * k, 2)]
+            at = rs + (r % 2) * 2 + k
+            far = remote(src.at[:, s], dst, ss + s, at, (owner_c, s))
+            near = local(src.at[:, s], dst, at)
+            here = is_own & (r == s)
+
+            @pl.when(jnp.logical_not(here))
+            def _(far=far):
+                far.start()
+
+            @pl.when(here)
+            def _(near=near):
+                near.start()
+
+            def done(far=far, here=here):
+                @pl.when(jnp.logical_not(here))
+                def _():
+                    far.wait_send()
+
+            last.append(done)
+
+    def landed(land, rs, out, first):
+        for i in range(2):
+            for kk in range(2):
+                place = land.at[i, pl.ds(2 * kk, 2)]
+                local(place, place, rs + 2 * i + kk).wait()
+        for i in range(2):
+            tok[first + i] = dot_l(pm[...], land[i].reshape(256, D)).astype(BF)
+        cp = local(tok.at[pl.ds(first, 2)], out, sem())
+        cp.start()
+        last.append(cp.wait)
+
+    ro_out, ro_gin = sem(4), sem(4)
+    hand_back(stg_c, v.oland, ro_out)
+    sum_u.s1()
+    sum_u.s2()
+    o_wdn[...] = sum_d.s3().astype(BF)
+    line_d.s0()
+    mgs1, mgr1 = v.mgs1, v.mgr1
+    mgs1[...] = mg1[...].astype(BF)
+    mg_cp = swap(mgs1, mgr1, sib)
+    all1.go(0)
+
+    ag_cp.wait_recv()
+    dqkv = act
+    kr_rows = pl.ds(kcol, HB)
+
+    def heads_back(g, _):
+        oq, mk = masks_of(g)
+        for h in range(2):
+            at = pl.ds(pl.multiple_of(g * 256 + h * 128, 128), 128)
+            fint[:, at] = att[g, h * 128 : h * 128 + 128, :].astype(F32).T.astype(BF)
+        act[g, :, 3 * HB : 4 * HB] = dot_t(tmpa[g], wo[kr_rows, :]).astype(BF)
+        for hp in range(3):
+            qp = qkv[g, :, hp * 128 : hp * 128 + 128]
+            kp = qkv[g, :, HB + hp * 128 : HB + hp * 128 + 128]
+            vp = qkv[g, :, 2 * HB + hp * 128 : 2 * HB + hp * 128 + 128]
+            dop = act[g, :, 3 * HB + hp * 128 : 3 * HB + hp * 128 + 128]
+            ka = jnp.concatenate([kp, mk], axis=1)
+            dq = dk = dv = None
+            for h in range(2):
+                s = dot_t(ka, jnp.concatenate([qp * lmb[h], oq], axis=1))
+                e = jnp.exp(s - jnp.max(s, axis=0, keepdims=True))
+                prob = e * (1.0 / jnp.sum(e, axis=0, keepdims=True))
+                dp = dot_t(vp * lmb[h], dop)
+                delta = jnp.sum(prob * dp, axis=0, keepdims=True)
+                ds = (prob * (dp - delta)).astype(BF)
+                dv_h = dot(prob.astype(BF), dop) * lmf[h]
+                dk_h = dot(ds, qp) * lmf[h]
+                dq_h = dot_l(ds, kp) * (lmf[h] * 0.125)
+                dv = dv_h if h == 0 else dv + dv_h
+                dk = dk_h if h == 0 else dk + dk_h
+                dq = dq_h if h == 0 else dq + dq_h
+            dqkv[g, :, hp * 128 : hp * 128 + 128] = dq.astype(BF)
+            dqkv[g, :, HB + hp * 128 : HB + hp * 128 + 128] = dk.astype(BF)
+            dqkv[g, :, 2 * HB + hp * 128 : 2 * HB + hp * 128 + 128] = dv.astype(BF)
+        return 0
+
+    lax.fori_loop(0, 4, heads_back, 0)
+
+    def proj_back(g, _):
+        upg[g, :, 0:D] = dot_t(dqkv[g, :, 0 : 3 * HB], wq[...]).astype(BF)
+        return 0
+
+    lax.fori_loop(0, 4, proj_back, 0)
+    cg_cp = swap(upg.at[:, :, pl.ds(0, D)], bg, sib)
+
+    def grad_out(pos, _):
+        rows = pl.ds(pl.multiple_of(96 * (2 * block_at(pos) + k), 32), 96)
+        gwo[pos] = dot(fint[rows, :], tmpa[...].reshape(1024, D)).astype(BF)
+        pl.when(pos == 0)(sum_o.s0)
+        return 0
+
+    lax.fori_loop(0, 4, grad_out, 0)
+    total_u = sum_u.s3()
+    gwu[3] = total_u.astype(BF)
+    half_u = swap(
+        gwu.at[3, pl.ds(pl.multiple_of(96 * (1 - k), 32), 96), :], v.su, sib
+    )
+    mine96 = pl.ds(pl.multiple_of(96 * k, 32), 96)
+    for b in range(4):
+        o_wup[:, pl.ds(pl.multiple_of(HB * (2 * b + k), 128), HB)] = gwu[3, mine96, b * HB : (b + 1) * HB]
+    half_u.wait()
+    last.remove(half_u.wait_send)
+    for b in range(4):
+        o_wup[:, pl.ds(pl.multiple_of(HB * (2 * b + 1 - k), 128), HB)] = v.su[:, b * HB : (b + 1) * HB]
+    line_u.s0()
+    line_d.s1()
+    sum_o.s1()
+    sum_o.s2()
+    sum_u.sent()
+    all1.end(0)
+    all1.go(1)
+
+    def grad_qkv(pos, _):
+        rows = pl.ds(pl.multiple_of(192 * block_at(pos), 64), 192)
+
+        def part(nt, _):
+            ln = pl.ds(pl.multiple_of(nt * HB, 128), HB)
+            gwu[pos, :, ln] = dot(c1t[rows, :], dqkv[:, :, ln].reshape(1024, HB)).astype(BF)
+            return 0
+
+        lax.fori_loop(0, 3, part, 0)
+        pl.when(pos == 0)(sum_q.s0)
+        return 0
+
+    lax.fori_loop(0, 4, grad_qkv, 0)
+    line_d.s2()
+    line_u.s1()
+    sg2[9:10, pl.ds(kcol, HB)] = jnp.sum(
+        jnp.sum(dqkv[:, :, 0:HB].astype(F32), axis=0), axis=0, keepdims=True
+    )
+    sg2[10:11, pl.ds(kcol, HB)] = jnp.sum(
+        jnp.sum(dqkv[:, :, 2 * HB : 3 * HB].astype(F32), axis=0), axis=0, keepdims=True
+    )
+    cg_cp.wait_recv()
+
+    def cg_sum(pr, _):
+        for pc in range(2):
+            g = 2 * pr + pc
+            t = (upg[g, :, 0:D].astype(F32) + bg[g].astype(F32)).astype(BF)
+            sh = shifted(t.astype(F32), pc).astype(BF)
+            ub[g, 16:272, :] = t[:, 0:HB]
+            gb[g, 16:272, :] = t[:, HB:D]
+            us[g, 16:272, :] = sh[:, 0:HB]
+            gs[g, 16:272, :] = sh[:, HB:D]
+        return 0
+
+    lax.fori_loop(0, 2, cg_sum, 0)
+    for hh in range(2):
+        base, side = (ub, us) if hh == 0 else (gb, gs)
+
+        def conv_one_back(lt, _, hh=hh, base=base, side=side):
+            l0 = pl.multiple_of(lt * 128, 128)
+            la = pl.multiple_of(hh * HB + lt * 128, 128)
+            kr = [par[11 + t // 4 : 12 + t // 4, pl.ds((t % 4) * D + la, 128)] for t in range(9)]
+            gk = [jnp.zeros((8, 128), F32) for _ in range(9)]
+            for pc in range(2):
+                for h in range(2):
+                    here = ain[2 * k + pc, 16 + 128 * h : 144 + 128 * h, pl.ds(la, 128)].astype(F32)
+                    acc = None
+                    for t, gsrc, ro, moved in taps_of(k, pc, True):
+                        at = pl.ds(pl.multiple_of(16 + 16 * ro + 128 * h, 16), 128)
+                        src = (side if moved else base)[gsrc, at, pl.ds(l0, 128)].astype(F32)
+                        term = src * kr[t]
+                        acc = term if acc is None else acc + term
+                        gk[t] = gk[t] + jnp.sum((src * here).reshape(16, 8, 128), axis=0)
+                    gp[pc, h * 128 : h * 128 + 128, pl.ds(la, 128)] = acc
+            for t in range(9):
+                sg2[t : t + 1, pl.ds(la, 128)] = jnp.sum(gk[t], axis=0, keepdims=True)
+            return 0
+
+        lax.fori_loop(0, 3, conv_one_back, 0)
+    all2.go(0)
+    sum_q.s1()
+    sum_q.s2()
+
+    def one_back(n, _):
+        jj = n // 2
+        g = 2 * k + jj
+        rows = pl.ds(pl.multiple_of((n % 2) * 128, 128), 128)
+        h64 = pl.ds((n % 2) * 2, 2)
+        nrm, inv = norm_parts(tok[g, rows, :].astype(F32))
+        ig = gp[jj, rows, :]
+        gi = mid[jj, rows, :] + norm_back(ig * (1.0 + piece(oh[g, rows, :], 1)), nrm, inv)
+        stg_t[jj, h64] = gi.astype(BF).reshape(2, 64, D)
+        ids = lv[g, rows, :]
+        low = ig.astype(BF)
+        scl = (ig * nrm).astype(BF)
+        total = dot_l(place_rows(ids, 0), low[:, 0:HB]) + dot_l(place_rows(ids, 1), low[:, HB:D])
+        total = total + dot_l(place_rows(ids, 2), scl[:, 0:HB]) + dot_l(place_rows(ids, 3), scl[:, HB:D])
+        mg2[...] += total[0:16]
+        return 0
+
+    lax.fori_loop(0, 4, one_back, 0)
+    hand_back(stg_t, v.gland, ro_gin)
+    mgs2, mgr2 = v.mgs2, v.mgr2
+    mgs2[...] = mg2[...].astype(BF)
+    mg2_cp = swap(mgs2, mgr2, sib)
+
+    o_wout[...] = sum_o.s3().astype(BF)
+    line_o.s0()
+    mg_cp.wait_recv()
+    mga1, mga2 = v.mga1, v.mga2
+    slot = 4 * col + r
+
+    class Gather:
+        def __init__(self, own, got, everyone):
+            self.own, self.got, self.everyone = own, got, everyone
+            self.zr, self.zs = sem(4), sem(3)
+            self.xy = sem(4)
+
+        def s0(self):
+            self.everyone[slot] = (self.own[...].astype(F32) + self.got[...].astype(F32)).astype(BF)
+            place = self.everyone.at[slot]
+            for d, s in enumerate((r1, r2, r3)):
+                cp = remote(place, place, self.zs + d, self.zr + r, (c, s))
+                cp.start()
+                last.append(cp.wait_send)
+
+        def s1(self):
+            for s in (r1, r2, r3):
+                place = self.everyone.at[4 * col + s]
+                local(place, place, self.zr + s).wait()
+            place = self.everyone.at[pl.ds(4 * col, 4)]
+            self.cx = remote(place, place, self.xy, self.xy + 1, px)
+            self.cx.start()
+            last.append(self.cx.wait_send)
+
+        def s2(self):
+            self.cx.wait_recv()
+            place = self.everyone.at[pl.ds(8 * y, 8)]
+            self.cy = remote(place, place, self.xy + 2, self.xy + 3, py)
+            self.cy.start()
+            last.append(self.cy.wait_send)
+
+        def s3(self):
+            self.cy.wait_recv()
+
+    gat1 = Gather(mgs1, mgr1, mga1)
+    gat2 = Gather(mgs2, mgr2, mga2)
+    gat1.s0()
+    all1.end(1)
+    all1.go(2)
+    mg2_cp.wait_recv()
+    gat2.s0()
+    all2.end(0)
+    all2.go(1)
+    gat1.s1()
+    line_u.s2()
+    line_d.s3()
+
+    def load_again(p):
+        return local(wada_h.at[:, pl.ds(p * D, D)], wup.at[:, pl.ds((p % 2) * D, D)], s_wa + p % 2)
+
+    load_again(2).start()
+    load_again(3).start()
+    line_o.s1()
+    gat2.s1()
+    all1.end(2)
+    all1.go(3)
+    all2.end(1)
+    all2.go(2)
+
+    def pick(p):
+        ri, ci = iota((16, 16), 0), iota((16, 16), 1)
+        return ones_where((ri // 4 == r) & (ci == 4 * p + ri % 4))
+
+    my1 = mga1[slot]
+    my2 = mga2[slot]
+    cg = jnp.zeros((16, D), F32)
+    for p in range(2, 6):
+        load_again(p).wait()
+        lhs = dot(pick(p - 2), my1).astype(BF)
+        cg = cg + dot_t(lhs, wup[:, (p % 2) * D : (p % 2) * D + D])
+        load_again((p + 2) % 6).start()
+    for p in range(2):
+        load_again(p).wait()
+        for h in range(2):
+            lhs = dot(pick(2 * p + h), my2).astype(BF)
+            cg = cg + dot_t(lhs, wup[:, p * D + h * HB : p * D + h * HB + HB])
+    cond = condc[...]
+    sig = 1.0 / (1.0 + jnp.exp(-cond))
+    cgsum = v.cgsum
+    cgsum[...] = cg * (sig * (1.0 + cond * (1.0 - sig)))
+    crcv = v.crcv
+    cr, cs = sem(2), sem(4)
+    for s in range(4):
+        src = cgsum.at[pl.ds(pl.multiple_of(8 * owner, 8), 8), :]
+        dst = crcv.at[r % 2]
+        far = remote(src, dst, cs + s, cr + r % 2, (c, s))
+        near = local(src, dst, cr + r % 2)
+
+        @pl.when(is_own & (r != s))
+        def _(far=far):
+            far.start()
+
+        @pl.when(is_own & (r == s))
+        def _(near=near):
+            near.start()
+
+        def done(far=far, s=s):
+            @pl.when(is_own & (r != s))
+            def _():
+                far.wait_send()
+
+        last.append(done)
+
+    total_q = sum_q.s3()
+    gwu[3, :, 0 : 3 * HB] = total_q.astype(BF)
+    half_q = swap(
+        gwu.at[3, pl.ds(pl.multiple_of(96 * (1 - k), 32), 96), pl.ds(0, 3 * HB)], v.sq, sib
+    )
+    for part in range(3):
+        o_wqkv[:, pl.ds(pl.multiple_of(part * D + HB * k, 128), HB)] = gwu[3, mine96, part * HB : (part + 1) * HB]
+    half_q.wait_recv()
+    for part in range(3):
+        o_wqkv[:, pl.ds(pl.multiple_of(part * D + HB * (1 - k), 128), HB)] = v.sq[:, part * HB : (part + 1) * HB]
+    line_q.s0()
+    line_u.s3()
+    gat1.s2()
+    line_o.s2()
+    all1.end(3)
+    all1.go(4)
+    all2.end(2)
+    all2.go(3)
+    gat2.s2()
+    line_q.s1()
+    for done in tok_passed:
+        done()
+    landed(v.oland, ro_out, o_out, 0)
+
+    low_y.wait_recv()
+    ri, ci = iota((96, D), 0), iota((96, D), 1)
+    cond_t = dot_t(ones_where(ci == 96 * c + ri), clow[...].reshape(64, D)).astype(BF)
+    ej, en = iota((64, 256), 0), iota((64, 256), 1)
+    bn = iota((8, 256), 1)
+
+    def spread(p):
+        return dot(cond_t, ones_where((en // 16 == ej // 4) & (en % 16 == 4 * p + ej % 4))).astype(BF)
+
+    all1.end(4)
+    o_sg1[...] = sg1[...]
+    all2.end(3)
+    all2.go(4)
+    gat1.s3()
+    o_bada[...] = jnp.zeros((8, D), F32)
+    every1 = mga1[...].reshape(256, D)
+
+    def ada_out(p):
+        cp = local(wdn.at[pl.ds(96 * p, 96), :], o_wada.at[:, pl.ds(p * D, D)], sem())
+        cp.start()
+        last.append(cp.wait)
+
+    for p in range(4):
+        wdn[(p + 2) * 96 : (p + 3) * 96, :] = dot(spread(p), every1).astype(BF)
+        ada_out(p + 2)
+        o_bada[p + 2 : p + 3, :] = dot(ones_where((bn % 16) // 4 == p), every1)[0:1]
+    line_o.s3()
+    line_q.s2()
+    gat2.s3()
+    every2 = mga2[...].reshape(256, HB)
+    for p in range(4):
+        half = (p % 2) * HB
+        wdn[p // 2 * 96 : p // 2 * 96 + 96, half : half + HB] = dot(spread(p), every2).astype(BF)
+        o_bada[p // 2 : p // 2 + 1, (p % 2) * HB : (p % 2) * HB + HB] = dot(ones_where((bn % 16) // 4 == p), every2)[0:1]
+    ada_out(0)
+    ada_out(1)
+    all2.end(4)
+    o_sg2[...] = sg2[...]
+    landed(v.gland, ro_gin, o_gin, 2)
+    for i in range(2):
+        local(crcv.at[i], crcv.at[i], cr + i).wait()
+    o_cond[...] = crcv[0] + crcv[1]
+    line_q.s3()
+    for done in last:
+        done()
+    for s in (sum_d, sum_o, sum_q):
+        s.sent()
+    assert count[0] <= N_SEMS, count[0]
+
+
+def fast_shards(
+    tokens, latent, condition, w_ada, b_ada, conv_attn, w_qkv, bias_qv, w_out, b_out,
+    w_up, b_up, conv_ffn, w_down, b_down, cotangent,
+):
+    f = lambda a: a.astype(F32)
+    conv_rows = jnp.pad(f(conv_attn), ((0, 3), (0, 0))).reshape(3, 4 * D)
+    ada_rows = jnp.pad(f(b_ada), (0, 2 * D)).reshape(2, 4 * D)
+    par = jnp.concatenate(
+        [
+            f(conv_ffn),
+            f(b_up)[None],
+            jnp.concatenate([f(b_down), f(b_out), f(bias_qv)])[None],
+            conv_rows,
+            ada_rows,
+        ]
+    )
+    anyspace = pl.BlockSpec(memory_space=pl.ANY)
+    vm = pl.BlockSpec(memory_space=pltpu.VMEM)
+    outs = (
+        ((2, 256, D), BF),
+        ((2, 256, D), BF),
+        ((8, D), F32),
+        ((96, 6 * D), BF),
+        ((8, D), F32),
+        ((16, FF), F32),
+        ((16, D), F32),
+        ((96, 3 * D), BF),
+        ((96, D), BF),
+        ((96, FF), BF),
+        ((HB, D), BF),
+    )
+    out, gin, gcond, gwada, gbada, sg1, sg2, gwqkv, gwout, gwup, gwdn = pl.pallas_call(
+        whole_block,
+        out_shape=[jax.ShapeDtypeStruct(s, t) for s, t in outs],
+        in_specs=[anyspace, anyspace, vm, vm, anyspace, vm, anyspace, anyspace, anyspace, anyspace],
+        out_specs=[anyspace, anyspace, vm, anyspace] + [vm] * (len(outs) - 4),
+        scratch_shapes=[pltpu.SemaphoreType.DMA((N_SEMS,))] + [pltpu.VMEM(s, t) for s, t in SCRATCH.values()],
+        compiler_params=pltpu.CompilerParams(
+            collective_id=0, has_side_effects=True, vmem_limit_bytes=VMEM_LIMIT
+        ),
+        name="block",
+    )(tokens, cotangent, latent.reshape(2, 1, 256), condition.reshape(8, D), w_ada, par, w_qkv, w_out, w_up, w_down)
+    c = lax.axis_index("canvas")
+
+    def share(a, dim, n):
+        return lax.dynamic_slice_in_dim(a, c * n, n, dim)
+
+    bq = sg2[9:11].reshape(2 * D)
+    return (
+        out,
+        f(gin),
+        gcond.reshape(2, 4, D),
+        f(gwada),
+        share(gbada[0:6].reshape(6 * D), 0, 576),
+        share(sg2[0:9], 1, 96),
+        f(gwqkv),
+        share(bq, 0, 192),
+        f(gwout),
+        share(sg1[10, D : 2 * D], 0, 96),
+        f(gwup),
+        share(sg1[9], 0, 384),
+        share(sg1[0:9], 1, 384),
+        f(gwdn),
+        share(sg1[10, 0:D], 0, 96),
+    )
+
 
 def solution(mesh):
     placed = (
@@ -399,8 +1601,9 @@
         P(),
         P("canvas", "rows", None),
     )
+    fits = mesh.shape["rows"] == 4 and mesh.shape["canvas"] == 8
     return jax.shard_map(
-        shards,
+        fast_shards if fits else shards,
         mesh=mesh,
         in_specs=placed,
         out_specs=(

time: 892 us -> 245 us (0.27); the launches traced: 880 us -> 244 us
  waiting for transfers between devices: 296 us -> 0 us
  Pallas kernels: 0 us -> 219 us
  local copies, waits for them, and re-layouts: 195 us -> 15 us
  matrix products: 174 us -> 0 us
  other arithmetic: 102 us -> 9.15 us
  blocking collectives: 63.9 us -> 0 us
  starting transfers between devices: 30.1 us -> 0 us
  between operations: 18.8 us -> 0.7 us
    pallas_call x0 -> x1, Pallas kernels: none -> 219 us  [fast_shards(): pl.pallas_call(whole_block, out_shape=[jax.ShapeDtypeStruct(s, t) for s,...]
    dot_general x39 -> x0, matrix products: 174 us -> none  [the longest x4 22.3 us: shards(): jnp.einsum('cghqk,cgqhe->cgkhe', softmax_weights, grad_heads_f, precision...]
    another operation x45 -> x0, local copies, waits for them, and re-layouts: 103 us -> none  [the longest x8 24.3 us: shards(): pending = pending + jnp.stack([key_part, value_part]).reshape(pending.shape)]
    all_gather x2 -> x0, waiting for transfers between devices: 87 us -> none  [the longest x1 49.5 us: shards(): value_piece = lax.all_gather(value_rows, 'rows', axis=2, tiled=True)]
    ppermute x15 -> x0, waiting for transfers between devices: 81.9 us -> none  [the longest x7 72.7 us: passed_along(): return lax.ppermute(block, axis, route)]
    unnamed x12 -> x0, waiting for transfers between devices: 62.8 us -> none
    psum x1 -> x0, waiting for transfers between devices: 53.4 us -> none  [shards(): lax.psum(mod_grad.astype(jnp.bfloat16), 'rows').astype(jnp.float32)]
    convert_element_type x26 -> x6, other arithmetic: 49 us -> 7.73 us  [fast_shards(): f = lambda a: a.astype(F32)]
  transfers between devices with their start and end apart: 25 -> 0, of which waited for: 19 -> 0; matrix products, arithmetic and copies ran while one was open for 37% -> 0% of each run, Pallas kernels for 0% -> 0%
where the time goes in v1:
time: 245 us; the launch traced here: 244 us
  Pallas kernels  219 us (89%)
  local copies, waits for them, and re-layouts  15 us (6%)
  other arithmetic  9.15 us (4%)
    pallas_call x1, Pallas kernels, fast_shards(): pl.pallas_call(whole_block, out_shape=[jax.ShapeDtypeStruct(s, t) for s,...  219 us
    convert_element_type x6, other arithmetic, fast_shards(): f = lambda a: a.astype(F32)  7.73 us
    dynamic_slice x6, local copies, waits for them, and re-layouts, share(): return lax.dynamic_slice_in_dim(a, c * n, n, dim)  5.23 us

profile of v1, /device:TPU:0, one launch (start us, length us, event | category | flops | bytes accessed | tf_op | source)
XLA Modules:
  0.0 244.2 jit_solution(16322162582629667999)
XLA Ops:
  0.6 1.3 reshape.56.lat_h
  1.9 1.4 reshape.57.cond_r
  3.3 0.7 broadcast_in_dim.8
  4.0 0.7 pad_maximum_fusion
  4.7 0.7 pad.10
  5.5 0.7 pad.11
  6.2 1.0 concatenate.10
  7.2 0.7 concatenate.11.par
  7.9 219.4 %block.1 = (bf16[2,256,768]{2,1,0:T(8,128)(2,1)}, bf16[2,256,768]{2,1,0:T(8,128)(2,1)}, f32[8,768]{1,0:T(8,128)}, bf16[96,4608]{1,0:T(8,128)(2,1)}, f32[8,768]{1...) custom-call(bf16[2,256,768]{2,1,0:T(8,128)(2,1)} %tok_h.1, ...), custom_call_target="tpu_custom_call" | custom-call | tf_op jit(solution)/shard_map/block/pallas_call | solution.py:1549
  227.3 2.5 %convert_element_type.16 = f32[2,256,768]{2,1,0:T(8,128)} convert(bf16[2,256,768]{2,1,0:T(8,128)(2,1)} %get-tuple-element.27) | non-fusion elementwise | flops 393216 | bytes 2359296 | tf_op jit(solution)/shard_map/convert_element_type | solution.py:1522
  229.7 0.6 reshape.60
  230.4 1.4 convert_element_type.30
  231.7 0.7 dynamic_slice.27
  232.4 1.4 constant_dynamic-slice_fusion.3
  233.8 1.0 convert_element_type.31
  234.8 0.7 slice.23
  235.5 0.6 dynamic_slice.29
  236.2 0.7 convert_element_type.32
  236.9 0.8 fusion.2
  238.2 1.1 convert_element_type.33
  239.4 0.9 slice.25
  240.9 1.3 constant_dynamic-slice_fusion.1
  242.2 1.1 convert_element_type.34
  243.3 0.9 copy.32
  (23 shorter events, 1.3 us)
Async XLA Ops:
  227.2 2.5 %copy-start.6 = (f32[8,768]{1,0:T(8,128)S(1)}, f32[8,768]{1,0:T(8,128)}, u32[]{:S(2)}) copy-start(f32[8,768]{1,0:T(8,128)} %get-tuple-element.28) | copy-start | bytes 73732
  227.3 3.1 %copy-start = (bf16[96,4608]{1,0:T(8,128)(2,1)S(1)}, bf16[96,4608]{1,0:T(8,128)(2,1)}, u32[]{:S(2)}) copy-start(bf16[96,4608]{1,0:T(8,128)(2,1)} %get-tuple-element.29) | copy-start | bytes 2654212
  229.7 2.0 copy-start.7
  229.7 4.1 %copy-start.4 = (bf16[96,2304]{1,0:T(8,128)(2,1)S(1)}, bf16[96,2304]{1,0:T(8,128)(2,1)}, u32[]{:S(2)}) copy-start(bf16[96,2304]{1,0:T(8,128)(2,1)} %get-tuple-element.32) | copy-start | bytes 1327108
  230.4 5.8 %copy-start.5 = (bf16[96,768]{1,0:T(8,128)(2,1)S(1)}, bf16[96,768]{1,0:T(8,128)(2,1)}, u32[]{:S(2)}) copy-start(bf16[96,768]{1,0:T(8,128)(2,1)} %get-tuple-element.33) | copy-start | bytes 442372
  230.4 7.9 %copy-start.3 = (bf16[96,3072]{1,0:T(8,128)(2,1)S(1)}, bf16[96,3072]{1,0:T(8,128)(2,1)}, u32[]{:S(2)}) copy-start(bf16[96,3072]{1,0:T(8,128)(2,1)} %get-tuple-element.35) | copy-start | bytes 1769476
  233.8 8.4 %copy-start.2 = (bf16[384,768]{1,0:T(8,128)(2,1)S(1)}, bf16[384,768]{1,0:T(8,128)(2,1)}, u32[]{:S(2)}) copy-start(bf16[384,768]{1,0:T(8,128)(2,1)} %get-tuple-element.36) | copy-start | bytes 1769476
  238.2 5.1 %copy-start.1 = (bf16[2,256,768]{2,1,0:T(8,128)(2,1)S(1)}, bf16[2,256,768]{2,1,0:T(8,128)(2,1)}, u32[]{:S(2)}) copy-start(bf16[2,256,768]{2,1,0:T(8,128)(2,1)} %get-tuple-element.56) | copy-start | bytes 2359300

commit v2 on v1

--- a/solution.py
+++ b/solution.py
@@ -433,6 +433,28 @@
     return jnp.where(col == 15, 0.0, pltpu.roll(rows, n - 1, 0))
 
 
+def conv_sum(load, kr, taps):
+    total = None
+    for t, gsrc, ro, moved in taps:
+        term = load(gsrc, ro, moved).astype(F32) * kr[t]
+        total = term if total is None else total + term
+    return total
+
+
+def conv_both(load, here, kr, gk, taps):
+    total = None
+    for t, gsrc, ro, moved in taps:
+        src = load(gsrc, ro, moved).astype(F32)
+        term = src * kr[t]
+        total = term if total is None else total + term
+        gk[t] = gk[t] + fold_rows(src * here)
+    return total
+
+
+def fold_rows(rows):
+    return jnp.sum(rows.reshape(rows.shape[0] // 8, 8, 128), axis=0)
+
+
 def norm_parts(v):
     mean = jnp.mean(v, axis=-1, keepdims=True)
     cen = v - mean
@@ -471,13 +493,13 @@
     gp=((2, 256, D), F32),
     act=((4, 256, 2 * D), BF),
     upg=((4, 256, 2 * D), BF),
+    upr=((4, 256, 2 * D), BF),
     actt=((HB, 1024), BF),
     wup=((D, 2 * D), BF),
     wdn=((2 * D, D), BF),
     wq=((D, 3 * HB), BF),
     wo=((D, D), BF),
     gwd=((4, HB, D), BF),
-    gwu=((4, 192, 2 * D), BF),
     gwo=((4, 96, D), BF),
     rd_a=((192, D), BF),
     rd_b=((192, D), BF),
@@ -527,12 +549,16 @@
     sg2r=((5, 16, D), BF),
     cgsum=((16, D), F32),
     crcv=((2, 8, D), F32),
+    lat_own=((2, 1, 256), jnp.int32),
+    cond_own=((8, D), F32),
+    par=((16, FF), F32),
 )
-N_SEMS = 208
+N_SEMS = 240
 
 
 def whole_block(
-    tok_h, cot_h, lat_h, cond_r, wada_h, par, wqkv_h, wout_h, wup_h, wdn_h,
+    tok_h, cot_h, lat_in, cond_in, wada_h, wqkv_h, wout_h, wup_h, wdn_h,
+    p_bada, p_conv1, p_bqv, p_bout, p_bup, p_conv2, p_bdn,
     o_out, o_gin, o_cond, o_wada, o_bada, o_sg1, o_sg2, o_wqkv, o_wout, o_wup, o_wdn,
     sems, *bufs,
 ):
@@ -541,7 +567,8 @@
     modhl, pm, ain, c1t, tmpa, qkv, att = v.modhl, v.pm, v.ain, v.c1t, v.tmpa, v.qkv, v.att
     fint, bg, mid, ub, us, gb, gs = v.fint, v.bg, v.mid, v.ub, v.us, v.gb, v.gs
     gp, act, upg, actt, wup, wdn, wq, wo = v.gp, v.act, v.upg, v.actt, v.wup, v.wdn, v.wq, v.wo
-    gwd, gwu, gwo, condc, clow = v.gwd, v.gwu, v.gwo, v.condc, v.clow
+    upr = v.upr
+    gwd, gwo, condc, clow = v.gwd, v.gwo, v.condc, v.clow
 
     c = lax.axis_index("canvas")
     r = lax.axis_index("rows")
@@ -624,7 +651,26 @@
         for g in range(4):
             buf[g, 0:16, :] = jnp.zeros((16, wide), BF)
             buf[g, 272:288, :] = jnp.zeros((16, wide), BF)
-    condc[pl.ds(pl.multiple_of(8 * k, 8), 8), :] = cond_r[...]
+    lat_h, par = v.lat_own, v.par
+    for i in range(2):
+        lat_h[i] = lat_in[i : i + 1, :]
+        v.cond_own[4 * i : 4 * i + 4, :] = cond_in[i]
+    condc[pl.ds(pl.multiple_of(8 * k, 8), 8), :] = v.cond_own[...]
+    par[0:9, :] = p_conv2[...].astype(F32)
+
+    def row_of(ref):
+        return ref[...].astype(F32).reshape(1, ref.shape[0])
+
+    par[9:10, :] = row_of(p_bup)
+    par[10:11, 0:D] = row_of(p_bdn)
+    par[10:11, D : 2 * D] = row_of(p_bout)
+    par[10:11, 2 * D : 4 * D] = row_of(p_bqv)
+    taps1 = p_conv1[...].astype(F32)
+    for t in range(9):
+        par[11 + t // 4 : 12 + t // 4, (t % 4) * D : (t % 4) * D + D] = taps1[t : t + 1]
+    ada = row_of(p_bada)
+    par[14:15, :] = ada[:, 0 : 4 * D]
+    par[15:16, 0 : 2 * D] = ada[:, 4 * D : 6 * D]
     pl.semaphore_wait(barrier, 9)
 
     cond_cp = swap(
@@ -660,10 +706,10 @@
         stg_t[i] = dot(pm[...], act[i, :, 0:D]).astype(BF).reshape(4, 64, D)
         tok_sent.append(give(stg_t.at[i], tok.at[:, mine64, :], st + i, rt + r, i))
         last.append(give(lat_h.at[i], latc.at[r], sl + i, rl + r, i))
+
     ld_cot.wait()
     for i in range(2):
         stg_c[i] = dot(pm[...], act[i, :, D : 2 * D]).astype(BF).reshape(4, 64, D)
-        cot_sent.append(give(stg_c.at[i], cot.at[:, mine64, :], sc + i, rc + r, i))
 
     cond_cp.wait_recv()
     cond = condc[...]
@@ -719,6 +765,8 @@
 
     last.extend(arrive(latc, lambda s: s, rl, fl))
     tok_passed = arrive(tok, slab, rt, ft)
+    for i in range(2):
+        cot_sent.append(give(stg_c.at[i], cot.at[:, mine64, :], sc + i, rc + r, i))
 
     for s in range(4):
         rows = jnp.broadcast_to(latc[s].astype(F32), (128, 256)).astype(BF)
@@ -754,13 +802,12 @@
             kr = [par[11 + t // 4 : 12 + t // 4, pl.ds((t % 4) * D + la, 128)] for t in range(9)]
             for g in range(4):
                 for h in range(2):
-                    acc = None
-                    for t, gsrc, ro, moved in taps_of(g // 2, g % 2, False):
+
+                    def load(gsrc, ro, moved):
                         rows = pl.ds(16 + 16 * ro + 128 * h, 128)
-                        src = side[gsrc, rows, pl.ds(l0, 128)] if moved else ain[gsrc, rows, pl.ds(la, 128)]
-                        term = src.astype(F32) * kr[t]
-                        acc = term if acc is None else acc + term
-                    low = acc.astype(BF)
+                        return side[gsrc, rows, pl.ds(l0, 128)] if moved else ain[gsrc, rows, pl.ds(la, 128)]
+
+                    low = conv_sum(load, kr, taps_of(g // 2, g % 2, False)).astype(BF)
                     tmpa[g, h * 128 : h * 128 + 128, pl.ds(la, 128)] = low
                     c1t[pl.ds(la, 128), g * 256 + h * 128 : g * 256 + h * 128 + 128] = low.astype(F32).T.astype(BF)
             return 0
@@ -773,14 +820,17 @@
     b_q = par[10:11, pl.ds(2 * D + kcol, HB)]
     b_v = par[10:11, pl.ds(3 * D + kcol, HB)]
 
-    def project(g, _):
-        got = dot(tmpa[g], wq[...])
-        qkv[g, :, 0:HB] = ((got[:, 0:HB] + b_q).astype(BF).astype(F32) * 0.125).astype(BF)
-        qkv[g, :, HB : 2 * HB] = got[:, HB : 2 * HB].astype(BF)
-        qkv[g, :, 2 * HB : 3 * HB] = (got[:, 2 * HB : 3 * HB] + b_v).astype(BF)
+    def project(n, _):
+        two = pl.ds(2 * n, 2)
+        rows = tmpa[two].reshape(512, D)
+        got = dot(rows, wq[:, 0:HB]) + b_q
+        qkv[two, :, 0:HB] = (got.astype(BF).astype(F32) * 0.125).astype(BF).reshape(2, 256, HB)
+        qkv[two, :, HB : 2 * HB] = dot(rows, wq[:, HB : 2 * HB]).astype(BF).reshape(2, 256, HB)
+        got = dot(rows, wq[:, 2 * HB : 3 * HB]) + b_v
+        qkv[two, :, 2 * HB : 3 * HB] = got.astype(BF).reshape(2, 256, HB)
         return 0
 
-    lax.fori_loop(0, 4, project, 0)
+    lax.fori_loop(0, 2, project, 0)
 
     lane1 = iota((1, 128), 1)
     lmf = [jnp.where(lane1 < 64, 1.0, 0.0), jnp.where(lane1 < 64, 0.0, 1.0)]
@@ -800,16 +850,16 @@
 
     def attend(g, _):
         oq, mk = masks_of(g)
+        oq2 = jnp.concatenate([oq, oq], axis=0)
         for hp in range(3):
             qp = qkv[g, :, hp * 128 : hp * 128 + 128]
             ka = jnp.concatenate([qkv[g, :, HB + hp * 128 : HB + hp * 128 + 128], mk], axis=1)
             vp = qkv[g, :, 2 * HB + hp * 128 : 2 * HB + hp * 128 + 128]
-            mixed = None
-            for h in range(2):
-                s = dot_t(jnp.concatenate([qp * lmb[h], oq], axis=1), ka)
-                e = jnp.exp(s - jnp.max(s, axis=1, keepdims=True))
-                o = dot(e.astype(BF), vp) * (lmf[h] / jnp.sum(e, axis=1, keepdims=True))
-                mixed = o if h == 0 else mixed + o
+            qa = jnp.concatenate([qp * lmb[0], qp * lmb[1]], axis=0)
+            s = dot_t(jnp.concatenate([qa, oq2], axis=1), ka)
+            e = jnp.exp(s - jnp.max(s, axis=1, keepdims=True))
+            o = dot(e.astype(BF), vp) * (1.0 / jnp.sum(e, axis=1, keepdims=True))
+            mixed = o[0:256] * lmf[0] + o[256:512] * lmf[1]
             att[g, :, pl.ds(pl.multiple_of(kcol + hp * 128, 128), 128)] = mixed.astype(BF)
         att_copy(g).start()
         return 0
@@ -847,13 +897,10 @@
             n = a.shape[0]
             self.n = n
             ss = sem(8)
-            wide = a.shape[1]
-            ln = pl.ds(0, wide)
-            self.ln = slice(0, wide)
-            self.ca = remote(src.at[0, pl.ds(0, n), ln], a, ss, ss + 1, px)
-            self.cb = remote(src.at[0, pl.ds(n, n), ln], b, ss + 2, ss + 3, py)
-            self.cx = remote(src.at[1, :, ln], rx, ss + 4, ss + 5, px)
-            self.cy = remote(src.at[2, :, ln], ry, ss + 6, ss + 7, py)
+            self.ca = remote(src(0, 0, n), a, ss, ss + 1, px)
+            self.cb = remote(src(0, n, n), b, ss + 2, ss + 3, py)
+            self.cx = remote(src(1, 0, 2 * n), rx, ss + 4, ss + 5, px)
+            self.cy = remote(src(2, 0, 2 * n), ry, ss + 6, ss + 7, py)
 
         def s0(self):
             self.ca.start()
@@ -861,22 +908,21 @@
 
         def s1(self):
             self.cb.wait_recv()
-            n = self.n
-            self.src[1, n : 2 * n, self.ln] = (
-                self.src[1, n : 2 * n, self.ln].astype(F32) + self.b[...].astype(F32)
-            ).astype(BF)
+            part = self.src(1, self.n, self.n)
+            part[...] = (part[...].astype(F32) + self.b[...].astype(F32)).astype(BF)
             self.cx.start()
 
         def s2(self):
             self.ca.wait_recv()
-            n = self.n
-            self.src[2, 0:n, self.ln] = (self.src[2, 0:n, self.ln].astype(F32) + self.a[...].astype(F32)).astype(BF)
+            part = self.src(2, 0, self.n)
+            part[...] = (part[...].astype(F32) + self.a[...].astype(F32)).astype(BF)
             self.cy.start()
 
         def s3(self):
             self.cx.wait_recv()
             self.cy.wait_recv()
-            return self.src[3, :, self.ln].astype(F32) + self.rx[...].astype(F32) + self.ry[...].astype(F32)
+            part = self.src(3, 0, 2 * self.n)
+            return part[...].astype(F32) + self.rx[...].astype(F32) + self.ry[...].astype(F32)
 
         def sent(self):
             for cp in (self.ca, self.cb, self.cx, self.cy):
@@ -885,49 +931,92 @@
     inner = (r % 3) != 0
 
     class Line:
-        def __init__(self, out, za, zb):
-            self.out, self.za, self.zb = out, za, zb
-            ss = sem(6)
-            self.up = remote(out, za, ss, ss + 1, (c, r1))
-            self.mid = remote(out, zb, ss + 2, ss + 3, (c, r3))
-            self.down = remote(out, za, ss + 4, ss + 5, (c, r1))
+        def __init__(self, out, za, zb, cuts):
+            n = out.shape[0] // cuts
+            self.parts = []
+            for i in range(cuts):
+                rows = pl.ds(i * n, n)
+                o, a, b = out.at[rows], za.at[rows], zb.at[rows]
+                ss = sem(6)
+                up = remote(o, a, ss, ss + 1, (c, r1))
+                mid = remote(o, b, ss + 2, ss + 3, (c, r3))
+                down = remote(o, a, ss + 4, ss + 5, (c, r1))
+                self.parts.append((o, a, b, up, mid, down))
 
         def s0(self):
             @pl.when(jnp.logical_not(inner))
             def _():
-                self.up.start()
+                for part in self.parts:
+                    part[3].start()
 
         def s1(self):
             @pl.when(inner)
             def _():
-                self.up.wait_recv()
-                self.out[...] = (self.out[...].astype(F32) + self.za[...].astype(F32)).astype(BF)
-                self.mid.start()
+                for o, a, _b, up, mid, _down in self.parts:
+                    up.wait_recv()
+                    o[...] = (o[...].astype(F32) + a[...].astype(F32)).astype(BF)
+                    mid.start()
 
         def s2(self):
             @pl.when(inner)
             def _():
-                self.mid.wait()
-                self.out[...] = (self.out[...].astype(F32) + self.zb[...].astype(F32)).astype(BF)
-                self.down.start()
+                for o, _a, b, _up, mid, down in self.parts:
+                    mid.wait()
+                    o[...] = (o[...].astype(F32) + b[...].astype(F32)).astype(BF)
+                    down.start()
 
         def s3(self):
             @pl.when(inner)
             def _():
-                self.down.wait_send()
+                for part in self.parts:
+                    part[5].wait_send()
 
             @pl.when(jnp.logical_not(inner))
             def _():
-                self.up.wait_send()
-                self.down.wait_recv()
-                self.out[...] = self.za[...]
+                for o, a, _b, up, _mid, down in self.parts:
+                    up.wait_send()
+                    down.wait_recv()
+                    o[...] = a[...]
+
+    class Gather:
+        def __init__(self, own, got, everyone):
+            self.own, self.got, self.everyone = own, got, everyone
+            self.zr, self.zs = sem(4), sem(3)
+            self.xy = sem(4)
+
+        def s0(self):
+            self.everyone[slot] = (self.own[...].astype(F32) + self.got[...].astype(F32)).astype(BF)
+            place = self.everyone.at[slot]
+            for d, s in enumerate((r1, r2, r3)):
+                cp = remote(place, place, self.zs + d, self.zr + r, (c, s))
+                cp.start()
+                last.append(cp.wait_send)
+
+        def s1(self):
+            for s in (r1, r2, r3):
+                place = self.everyone.at[4 * col + s]
+                local(place, place, self.zr + s).wait()
+            place = self.everyone.at[pl.ds(4 * col, 4)]
+            self.cx = remote(place, place, self.xy, self.xy + 1, px)
+            self.cx.start()
+            last.append(self.cx.wait_send)
+
+        def s2(self):
+            self.cx.wait_recv()
+            place = self.everyone.at[pl.ds(8 * y, 8)]
+            self.cy = remote(place, place, self.xy + 2, self.xy + 3, py)
+            self.cy.start()
+            last.append(self.cy.wait_send)
+
+        def s3(self):
+            self.cy.wait_recv()
 
     class Everyone:
         def __init__(self, total, send, recv):
             self.total, self.send, self.recv = total, send, recv
-            ss = sem(10)
-            devs = (sib, px, py, (c, r1), (c, r2))
-            self.cps = [remote(send.at[0], recv.at[i], ss + 2 * i, ss + 2 * i + 1, devs[i]) for i in range(5)]
+            ss = sem(6)
+            devs = (sib, px, py)
+            self.cps = [remote(send.at[0], recv.at[i], ss + 2 * i, ss + 2 * i + 1, devs[i]) for i in range(3)]
 
         def go(self, i):
             self.send[0] = self.total[...].astype(BF)
@@ -937,17 +1026,28 @@
             self.cps[i].wait()
             self.total[...] = self.send[0].astype(F32) + self.recv[i].astype(F32)
 
-    sum_d = Scatter(gwd, v.rd_a, v.rd_b, v.rd_x, v.rd_y)
-    sum_u = Scatter(gwu, v.ru_a, v.ru_b, v.ru_x, v.ru_y)
-    sum_o = Scatter(gwo, v.ro_a, v.ro_b, v.ro_x, v.ro_y)
-    sum_q = Scatter(gwu, v.rq_a, v.rq_b, v.rq_x, v.rq_y)
-    line_d = Line(o_wdn, v.zd_a, v.zd_b)
-    line_u = Line(o_wup, v.zu_a, v.zu_b)
-    line_o = Line(o_wout, v.zo_a, v.zo_b)
-    line_q = Line(o_wqkv, v.zq_a, v.zq_b)
+        def plane(self):
+            self.end(2)
+            self.send[0] = self.total[...].astype(BF)
+
+    mga1, mga2 = v.mga1, v.mga2
+    mgs1, mgr1, mgs2, mgr2 = v.mgs1, v.mgr1, v.mgs2, v.mgr2
+    slot = 4 * col + r
+    gat1 = Gather(mgs1, mgr1, mga1)
+    gat2 = Gather(mgs2, mgr2, mga2)
+    sum_d = Scatter(lambda p, r0, n: gwd.at[p, pl.ds(r0, n)], v.rd_a, v.rd_b, v.rd_x, v.rd_y)
+    sum_u = Scatter(lambda p, r0, n: upr.at[p, pl.ds(r0, n)], v.ru_a, v.ru_b, v.ru_x, v.ru_y)
+    sum_o = Scatter(lambda p, r0, n: gwo.at[p, pl.ds(r0, n)], v.ro_a, v.ro_b, v.ro_x, v.ro_y)
+    sum_q = Scatter(lambda p, r0, n: wup.at[pl.ds(192 * p + r0, n), pl.ds(0, 3 * HB)], v.rq_a, v.rq_b, v.rq_x, v.rq_y)
+    line_d = Line(o_wdn, v.zd_a, v.zd_b, 2)
+    line_u = Line(o_wup, v.zu_a, v.zu_b, 2)
+    line_o = Line(o_wout, v.zo_a, v.zo_b, 1)
+    line_q = Line(o_wqkv, v.zq_a, v.zq_b, 2)
     sg1, sg2 = v.sg1, v.sg2
     all1 = Everyone(sg1, v.sg1s, v.sg1r)
     all2 = Everyone(sg2, v.sg2s, v.sg2r)
+    line_a = Line(v.sg1s.at[0], v.sg1r.at[3], v.sg1r.at[4], 1)
+    line_b = Line(v.sg2s.at[0], v.sg2r.at[3], v.sg2r.at[4], 1)
     sg1[...] = jnp.zeros((16, FF), F32)
     sg2[...] = jnp.zeros((16, D), F32)
 
@@ -967,10 +1067,12 @@
         wide = pl.multiple_of(HB * (2 * b + k), 128)
 
         def up(pr, _):
+            both = dot(tmpa[pl.ds(2 * pr, 2)].reshape(512, D), wup[:, pl.ds(lo, HB)])
             for pc in range(2):
                 g = 2 * pr + pc
-                u = (dot(tmpa[g], wup[:, pl.ds(lo, HB)]) + par[9:10, pl.ds(wide, HB)]).astype(BF)
+                u = (both[pc * 256 : pc * 256 + 256] + par[9:10, pl.ds(wide, HB)]).astype(BF)
                 ub[g, 16:272, :] = u
+                upr[g, :, pl.ds(lo, HB)] = u
                 us[g, 16:272, :] = shifted(u.astype(F32), pc).astype(BF)
             return 0
 
@@ -982,11 +1084,11 @@
             kr = [par[t : t + 1, pl.ds(wide + l0, 128)] for t in range(9)]
             for g in range(4):
                 for h in range(2):
-                    acc = None
-                    for t, gsrc, ro, moved in taps_of(g // 2, g % 2, False):
-                        src = (us if moved else ub)[gsrc, pl.ds(16 + 16 * ro + 128 * h, 128), ln]
-                        term = src.astype(F32) * kr[t]
-                        acc = term if acc is None else acc + term
+
+                    def load(gsrc, ro, moved):
+                        return (us if moved else ub)[gsrc, pl.ds(16 + 16 * ro + 128 * h, 128), ln]
+
+                    acc = conv_sum(load, kr, taps_of(g // 2, g % 2, False))
                     sq = acc * acc
                     th = jnp.tanh(0.7978845608028654 * acc * (1.0 + 0.044715 * sq))
                     half = 0.5 + 0.5 * th
@@ -994,96 +1096,52 @@
                     slope = half + half * (1.0 - th) * acc * (0.7978845608028654 + 0.10703222440890037 * sq)
                     rows = slice(h * 128, h * 128 + 128)
                     act[g, rows, pl.ds(lo + l0, 128)] = low
-                    gp[g // 2, rows, pl.ds((g % 2) * HB + l0, 128)] = slope
+                    upg[g, rows, pl.ds(lo + l0, 128)] = slope.astype(BF)
                     actt[ln, g * 256 + h * 128 : g * 256 + h * 128 + 128] = low.astype(F32).T.astype(BF)
             return 0
 
         lax.fori_loop(0, 3, conv_gelu, 0)
 
-        def down_grad(pr, _):
-            for pc in range(2):
-                g = 2 * pr + pc
-                t = dot_t(bg[g], wdn[pl.ds(lo, HB), :]) * gp[pr, :, pc * HB : pc * HB + HB]
-                t = t.astype(BF)
-                gb[g, 16:272, :] = t
-                gs[g, 16:272, :] = shifted(t.astype(F32), pc).astype(BF)
-            return 0
-
-        lax.fori_loop(0, 2, down_grad, 0)
-
-        def conv_back(lt, _):
-            l0 = pl.multiple_of(lt * 128, 128)
-            ln = pl.ds(l0, 128)
-            kr = [par[t : t + 1, pl.ds(wide + l0, 128)] for t in range(9)]
-            gk = [jnp.zeros((8, 128), F32) for _ in range(10)]
-            for g in range(4):
-                for h in range(2):
-                    here = ub[g, 16 + 128 * h : 144 + 128 * h, ln].astype(F32)
-                    acc = None
-                    for t, gsrc, ro, moved in taps_of(g // 2, g % 2, True):
-                        src = (gs if moved else gb)[gsrc, pl.ds(16 + 16 * ro + 128 * h, 128), ln].astype(F32)
-                        term = src * kr[t]
-                        acc = term if acc is None else acc + term
-                        gk[t] = gk[t] + jnp.sum((src * here).reshape(16, 8, 128), axis=0)
-                    low = acc.astype(BF)
-                    upg[g, h * 128 : h * 128 + 128, pl.ds(lo + l0, 128)] = low
-                    gk[9] = gk[9] + jnp.sum(low.astype(F32).reshape(16, 8, 128), axis=0)
-            for t in range(10):
-                sg1[t : t + 1, pl.ds(wide + l0, 128)] = jnp.sum(gk[t], axis=0, keepdims=True)
-            return 0
-
-        lax.fori_loop(0, 3, conv_back, 0)
-
         def grad_down(n, _):
-            rows = pl.ds(pl.multiple_of(n * 128, 128), 128)
-            gwd[pos, rows, :] = dot(actt[rows, :], bg[...].reshape(1024, D)).astype(BF)
+            ln = pl.ds(pl.multiple_of(n * 256, 128), 256)
+            gwd[pos, :, ln] = dot(actt[...], bg[:, :, ln].reshape(1024, 256)).astype(BF)
             return 0
 
         lax.fori_loop(0, 3, grad_down, 0)
         pl.when(pos == 0)(sum_d.s0)
-        pl.when(pos == 1)(sum_d.s1)
-        pl.when(pos == 2)(sum_d.s2)
+
+        @pl.when(pos == 2)
+        def _():
+            sum_d.s1()
+            sum_d.s2()
+
         return 0
 
     lax.fori_loop(0, 4, hidden, 0)
 
     for done in tok_sent + cot_sent:
         done()
-
-    def give_half(jj, _):
-        g = 2 * (1 - k) + jj
-        stg_t[jj] = dot_t(upg[g], wup[...]).astype(BF).reshape(4, 64, D)
-        return 0
-
-    lax.fori_loop(0, 2, give_half, 0)
-    f_cp = remote(stg_t, v.frcv, sem(), sem(), sib)
-    f_cp.start()
-
-    def give_branch(jj, _):
-        g = 2 * (1 - k) + jj
-        stg_c[jj] = dot(act[g], wdn[...]).astype(BF).reshape(4, 64, D)
-        return 0
-
-    lax.fori_loop(0, 2, give_branch, 0)
+    other2 = pl.ds(2 * (1 - k), 2)
+    mine2 = pl.ds(2 * k, 2)
+
+    def half_f(which, n):
+        return dot_t(upg[which].reshape(512, 2 * D), wup[n * HB : n * HB + HB, :])
+
+    def half_b(which, n):
+        return dot(act[which].reshape(512, 2 * D), wdn[:, n * HB : n * HB + HB])
+
+    for n in range(2):
+        cols = slice(n * HB, n * HB + HB)
+        stg_c[:, :, :, cols] = half_b(other2, n).astype(BF).reshape(2, 4, 64, HB)
     b_cp = remote(stg_c, v.brcv, sem(), sem(), sib)
     b_cp.start()
-
-    def grad_up(pos, _):
-        b = block_at(pos)
-        rows = pl.ds(pl.multiple_of(b * 192, 64), 192)
-
-        def part(nt, _):
-            ln = pl.ds(pl.multiple_of(nt * HB, 128), HB)
-            gwu[pos, :, ln] = dot(fint[rows, :], upg[:, :, ln].reshape(1024, HB)).astype(BF)
-            return 0
-
-        lax.fori_loop(0, 4, part, 0)
-        pl.when(pos == 0)(sum_u.s0)
-        return 0
-
-    lax.fori_loop(0, 4, grad_up, 0)
-    f_cp.wait()
-    b_cp.wait()
+    for n in range(2):
+        cols = slice(n * HB, n * HB + HB)
+        mid[:, :, cols] = half_b(mine2, n).reshape(2, 256, HB)
+
+    def down_total():
+        o_wdn[...] = sum_d.s3().astype(BF)
+        line_d.s0()
 
     mg1, mg2 = v.mg1, v.mg2
     mg1[...] = jnp.zeros((16, D), F32)
@@ -1093,42 +1151,6 @@
     def place_rows(ids, p):
         lane = iota((128, 128), 1)
         return ones_where((lane - 4 * p).astype(F32) == ids)
-
-    def two_back(n, carry):
-        bd, bo = carry
-        jj = n // 2
-        g = 2 * k + jj
-        t0 = pl.multiple_of((n % 2) * 128, 128)
-        rows = pl.ds(t0, 128)
-        h64 = pl.ds((n % 2) * 2, 2)
-        o = oh[g, rows, :]
-        gate1 = piece(o, 2)
-        ao = dot(att[g, rows, :], wo[...]) + par[10:11, D : 2 * D]
-        m = tok[g, rows, :].astype(F32) + gate1 * ao
-        nrm, inv = norm_parts(m)
-        fg = dot_t(upg[g, rows, :], wup[...]) + v.frcv[jj, h64].reshape(128, D).astype(F32)
-        cotf = cot[g, rows, :].astype(F32)
-        mg = cotf + norm_back(fg * (1.0 + piece(o, 4)), nrm, inv)
-        mid[jj, rows, :] = mg
-        ag = (gate1 * mg).astype(BF)
-        tmpa[g, rows, :] = ag
-        branch = dot(act[g, rows, :], wdn[...]) + v.brcv[jj, h64].reshape(128, D).astype(F32) + par[10:11, 0:D]
-        stg_c[jj, h64] = (m + piece(o, 5) * branch).astype(BF).reshape(2, 64, D)
-        ids = lv[g, rows, :]
-        total = dot_l(place_rows(ids, 0), (mg * ao).astype(BF))
-        total = total + dot_l(place_rows(ids, 1), fg.astype(BF))
-        total = total + dot_l(place_rows(ids, 2), (fg * nrm).astype(BF))
-        total = total + dot_l(place_rows(ids, 3), (cotf * branch).astype(BF))
-        mg1[...] += total[0:16]
-        bd = bd + jnp.sum(bg[g, rows, :].astype(F32), axis=0, keepdims=True)
-        bo = bo + jnp.sum(ag.astype(F32), axis=0, keepdims=True)
-        return bd, bo
-
-    bd, bo = lax.fori_loop(0, 4, two_back, (o_rows, o_rows))
-    ag_place = tmpa.at[pl.ds(2 * k, 2)]
-    ag_cp = swap(ag_place, ag_place, sib)
-    sg1[10:11, 0:D] = bd
-    sg1[10:11, D : 2 * D] = bo
 
     def hand_back(src, land, rs):
         ss = sem(4)
@@ -1166,22 +1188,138 @@
         last.append(cp.wait)
 
     ro_out, ro_gin = sem(4), sem(4)
+
+    b_cp.wait()
+
+    def out_half(n, bd):
+        jj = n // 2
+        g = 2 * k + jj
+        rows = pl.ds(pl.multiple_of((n % 2) * 128, 128), 128)
+        h64 = pl.ds((n % 2) * 2, 2)
+        o = oh[g, rows, :]
+        ao = dot(att[g, rows, :], wo[...]) + par[10:11, D : 2 * D]
+        m = tok[g, rows, :].astype(F32) + piece(o, 2) * ao
+        gp[jj, rows, :] = m
+        branch = mid[jj, rows, :] + v.brcv[jj, h64].reshape(128, D).astype(F32) + par[10:11, 0:D]
+        stg_c[jj, h64] = (m + piece(o, 5) * branch).astype(BF).reshape(2, 64, D)
+        low = (cot[g, rows, :].astype(F32) * branch).astype(BF)
+        mg1[...] += dot_l(place_rows(lv[g, rows, :], 3), low)[0:16]
+        return bd + jnp.sum(bg[g, rows, :].astype(F32), axis=0, keepdims=True)
+
+    sg1[10:11, 0:D] = lax.fori_loop(0, 4, out_half, o_rows)
     hand_back(stg_c, v.oland, ro_out)
+    def hidden_back(pos, _):
+        b = block_at(pos)
+        lo = pl.multiple_of(b * HB, 128)
+        wide = pl.multiple_of(HB * (2 * b + k), 128)
+        pl.when(pos == 2)(down_total)
+
+        def down_grad(pr, _):
+            both = dot_t(bg[pl.ds(2 * pr, 2)].reshape(512, D), wdn[pl.ds(lo, HB), :])
+            for pc in range(2):
+                g = 2 * pr + pc
+                t = both[pc * 256 : pc * 256 + 256] * upg[g, :, pl.ds(lo, HB)].astype(F32)
+                t = t.astype(BF)
+                gb[g, 16:272, :] = t
+                gs[g, 16:272, :] = shifted(t.astype(F32), pc).astype(BF)
+            return 0
+
+        lax.fori_loop(0, 2, down_grad, 0)
+
+        def conv_back(lt, _):
+            l0 = pl.multiple_of(lt * 128, 128)
+            ln = pl.ds(l0, 128)
+            kr = [par[t : t + 1, pl.ds(wide + l0, 128)] for t in range(9)]
+            gk = [jnp.zeros((8, 128), F32) for _ in range(10)]
+            for g in range(4):
+                for h in range(2):
+                    here = upr[g, h * 128 : h * 128 + 128, pl.ds(lo + l0, 128)].astype(F32)
+
+                    def load(gsrc, ro, moved):
+                        return (gs if moved else gb)[gsrc, pl.ds(16 + 16 * ro + 128 * h, 128), ln]
+
+                    acc = conv_both(load, here, kr, gk, taps_of(g // 2, g % 2, True))
+                    low = acc.astype(BF)
+                    upg[g, h * 128 : h * 128 + 128, pl.ds(lo + l0, 128)] = low
+                    gk[9] = gk[9] + fold_rows(low.astype(F32))
+            for t in range(10):
+                sg1[t : t + 1, pl.ds(wide + l0, 128)] = jnp.sum(gk[t], axis=0, keepdims=True)
+            return 0
+
+        lax.fori_loop(0, 3, conv_back, 0)
+
+        return 0
+
+    lax.fori_loop(0, 4, hidden_back, 0)
+
+    for n in range(2):
+        cols = slice(n * HB, n * HB + HB)
+        stg_t[:, :, :, cols] = half_f(other2, n).astype(BF).reshape(2, 4, 64, HB)
+    f_cp = remote(stg_t, v.frcv, sem(), sem(), sib)
+    f_cp.start()
+    for n in range(2):
+        cols = slice(n * HB, n * HB + HB)
+        mid[:, :, cols] = half_f(mine2, n).reshape(2, 256, HB)
+
+    def pos_of(b):
+        bx, by = b % 2, b // 2
+        fx = (bx - x) * (bx - x)
+        fy = (by - y) * (by - y)
+        return 2 * (1 - fx) + 1 - fy
+
+    def grad_up(nt, _):
+        ln = pl.ds(pl.multiple_of(nt * 256, 128), 256)
+        got = dot(fint[...], upg[:, :, ln].reshape(1024, 256)).astype(BF)
+        for b in range(4):
+            upr[pos_of(b), 0:192, ln] = got[b * 192 : b * 192 + 192]
+        return 0
+
+    lax.fori_loop(0, 6, grad_up, 0)
+    sum_u.s0()
+    line_d.s1()
+    f_cp.wait()
+
+    def two_back(n, bo):
+        jj = n // 2
+        g = 2 * k + jj
+        rows = pl.ds(pl.multiple_of((n % 2) * 128, 128), 128)
+        h64 = pl.ds((n % 2) * 2, 2)
+        o = oh[g, rows, :]
+        gate1 = piece(o, 2)
+        nrm, inv = norm_parts(gp[jj, rows, :])
+        fg = mid[jj, rows, :] + v.frcv[jj, h64].reshape(128, D).astype(F32)
+        mg = cot[g, rows, :].astype(F32) + norm_back(fg * (1.0 + piece(o, 4)), nrm, inv)
+        mid[jj, rows, :] = mg
+        ag = (gate1 * mg).astype(BF)
+        tmpa[g, rows, :] = ag
+        ids = lv[g, rows, :]
+        ao = dot(att[g, rows, :], wo[...]) + par[10:11, D : 2 * D]
+        total = dot_l(place_rows(ids, 0), (mg * ao).astype(BF))
+        total = total + dot_l(place_rows(ids, 1), fg.astype(BF))
+        total = total + dot_l(place_rows(ids, 2), (fg * nrm).astype(BF))
+        mg1[...] += total[0:16]
+        return bo + jnp.sum(ag.astype(F32), axis=0, keepdims=True)
+
+    sg1[10:11, D : 2 * D] = lax.fori_loop(0, 4, two_back, o_rows)
+    ag_place = tmpa.at[pl.ds(2 * k, 2)]
+    ag_cp = swap(ag_place, ag_place, sib)
+
     sum_u.s1()
     sum_u.s2()
-    o_wdn[...] = sum_d.s3().astype(BF)
-    line_d.s0()
-    mgs1, mgr1 = v.mgs1, v.mgr1
     mgs1[...] = mg1[...].astype(BF)
     mg_cp = swap(mgs1, mgr1, sib)
     all1.go(0)
 
     ag_cp.wait_recv()
+    mg_cp.wait_recv()
+    gat1.s0()
     dqkv = act
     kr_rows = pl.ds(kcol, HB)
 
     def heads_back(g, _):
+        pl.when(g == 2)(line_d.s2)
         oq, mk = masks_of(g)
+        mk2 = jnp.concatenate([mk, mk], axis=0)
         for h in range(2):
             at = pl.ds(pl.multiple_of(g * 256 + h * 128, 128), 128)
             fint[:, at] = att[g, h * 128 : h * 128 + 128, :].astype(F32).T.astype(BF)
@@ -1191,27 +1329,33 @@
             kp = qkv[g, :, HB + hp * 128 : HB + hp * 128 + 128]
             vp = qkv[g, :, 2 * HB + hp * 128 : 2 * HB + hp * 128 + 128]
             dop = act[g, :, 3 * HB + hp * 128 : 3 * HB + hp * 128 + 128]
-            ka = jnp.concatenate([kp, mk], axis=1)
-            dq = dk = dv = None
+            k2 = jnp.concatenate([kp * lmb[0], kp * lmb[1]], axis=0)
+            v2 = jnp.concatenate([vp * lmb[0], vp * lmb[1]], axis=0)
+            s = dot_t(jnp.concatenate([k2, mk2], axis=1), jnp.concatenate([qp, oq], axis=1))
+            dp = dot_t(v2, dop)
+            probs, dss = [], []
             for h in range(2):
-                s = dot_t(ka, jnp.concatenate([qp * lmb[h], oq], axis=1))
-                e = jnp.exp(s - jnp.max(s, axis=0, keepdims=True))
+                sh = s[h * 256 : h * 256 + 256]
+                dph = dp[h * 256 : h * 256 + 256]
+                e = jnp.exp(sh - jnp.max(sh, axis=0, keepdims=True))
                 prob = e * (1.0 / jnp.sum(e, axis=0, keepdims=True))
-                dp = dot_t(vp * lmb[h], dop)
-                delta = jnp.sum(prob * dp, axis=0, keepdims=True)
-                ds = (prob * (dp - delta)).astype(BF)
-                dv_h = dot(prob.astype(BF), dop) * lmf[h]
-                dk_h = dot(ds, qp) * lmf[h]
-                dq_h = dot_l(ds, kp) * (lmf[h] * 0.125)
-                dv = dv_h if h == 0 else dv + dv_h
-                dk = dk_h if h == 0 else dk + dk_h
-                dq = dq_h if h == 0 else dq + dq_h
+                delta = jnp.sum(prob * dph, axis=0, keepdims=True)
+                probs.append(prob.astype(BF))
+                dss.append((prob * (dph - delta)).astype(BF))
+            ds2 = jnp.concatenate(dss, axis=0)
+            dv2 = dot(jnp.concatenate(probs, axis=0), dop)
+            dk2 = dot(ds2, qp)
+            dq = dot_l(ds2, k2) * 0.125
+            dv = dv2[0:256] * lmf[0] + dv2[256:512] * lmf[1]
+            dk = dk2[0:256] * lmf[0] + dk2[256:512] * lmf[1]
             dqkv[g, :, hp * 128 : hp * 128 + 128] = dq.astype(BF)
             dqkv[g, :, HB + hp * 128 : HB + hp * 128 + 128] = dk.astype(BF)
             dqkv[g, :, 2 * HB + hp * 128 : 2 * HB + hp * 128 + 128] = dv.astype(BF)
         return 0
 
     lax.fori_loop(0, 4, heads_back, 0)
+    all1.end(0)
+    all1.go(1)
 
     def proj_back(g, _):
         upg[g, :, 0:D] = dot_t(dqkv[g, :, 0 : 3 * HB], wq[...]).astype(BF)
@@ -1220,6 +1364,24 @@
     lax.fori_loop(0, 4, proj_back, 0)
     cg_cp = swap(upg.at[:, :, pl.ds(0, D)], bg, sib)
 
+    def grad_qkv(nt, _):
+        ln = pl.ds(pl.multiple_of(nt * HB, 128), HB)
+        got = dot(c1t[...], dqkv[:, :, ln].reshape(1024, HB)).astype(BF)
+        for b in range(4):
+            wup[pl.ds(pl.multiple_of(192 * pos_of(b), 64), 192), ln] = got[b * 192 : b * 192 + 192]
+        return 0
+
+    lax.fori_loop(0, 3, grad_qkv, 0)
+    sum_q.s0()
+    all1.end(1)
+    all1.go(2)
+    gat1.s1()
+    sg2[9:10, pl.ds(kcol, HB)] = jnp.sum(
+        jnp.sum(dqkv[:, :, 0:HB].astype(F32), axis=0), axis=0, keepdims=True
+    )
+    sg2[10:11, pl.ds(kcol, HB)] = jnp.sum(
+        jnp.sum(dqkv[:, :, 2 * HB : 3 * HB].astype(F32), axis=0), axis=0, keepdims=True
+    )
     def grad_out(pos, _):
         rows = pl.ds(pl.multiple_of(96 * (2 * block_at(pos) + k), 32), 96)
         gwo[pos] = dot(fint[rows, :], tmpa[...].reshape(1024, D)).astype(BF)
@@ -1228,46 +1390,20 @@
 
     lax.fori_loop(0, 4, grad_out, 0)
     total_u = sum_u.s3()
-    gwu[3] = total_u.astype(BF)
+    upr[3, 0:192, :] = total_u.astype(BF)
     half_u = swap(
-        gwu.at[3, pl.ds(pl.multiple_of(96 * (1 - k), 32), 96), :], v.su, sib
+        upr.at[3, pl.ds(pl.multiple_of(96 * (1 - k), 32), 96), :], v.su, sib
     )
     mine96 = pl.ds(pl.multiple_of(96 * k, 32), 96)
     for b in range(4):
-        o_wup[:, pl.ds(pl.multiple_of(HB * (2 * b + k), 128), HB)] = gwu[3, mine96, b * HB : (b + 1) * HB]
+        o_wup[:, pl.ds(pl.multiple_of(HB * (2 * b + k), 128), HB)] = upr[3, mine96, b * HB : (b + 1) * HB]
     half_u.wait()
     last.remove(half_u.wait_send)
     for b in range(4):
         o_wup[:, pl.ds(pl.multiple_of(HB * (2 * b + 1 - k), 128), HB)] = v.su[:, b * HB : (b + 1) * HB]
     line_u.s0()
-    line_d.s1()
-    sum_o.s1()
-    sum_o.s2()
-    sum_u.sent()
-    all1.end(0)
-    all1.go(1)
-
-    def grad_qkv(pos, _):
-        rows = pl.ds(pl.multiple_of(192 * block_at(pos), 64), 192)
-
-        def part(nt, _):
-            ln = pl.ds(pl.multiple_of(nt * HB, 128), HB)
-            gwu[pos, :, ln] = dot(c1t[rows, :], dqkv[:, :, ln].reshape(1024, HB)).astype(BF)
-            return 0
-
-        lax.fori_loop(0, 3, part, 0)
-        pl.when(pos == 0)(sum_q.s0)
-        return 0
-
-    lax.fori_loop(0, 4, grad_qkv, 0)
-    line_d.s2()
-    line_u.s1()
-    sg2[9:10, pl.ds(kcol, HB)] = jnp.sum(
-        jnp.sum(dqkv[:, :, 0:HB].astype(F32), axis=0), axis=0, keepdims=True
-    )
-    sg2[10:11, pl.ds(kcol, HB)] = jnp.sum(
-        jnp.sum(dqkv[:, :, 2 * HB : 3 * HB].astype(F32), axis=0), axis=0, keepdims=True
-    )
+    all1.plane()
+    line_a.s0()
     cg_cp.wait_recv()
 
     def cg_sum(pr, _):
@@ -1282,6 +1418,9 @@
         return 0
 
     lax.fori_loop(0, 2, cg_sum, 0)
+    sum_q.s1()
+    sum_q.s2()
+    gat1.s2()
     for hh in range(2):
         base, side = (ub, us) if hh == 0 else (gb, gs)
 
@@ -1293,13 +1432,12 @@
             for pc in range(2):
                 for h in range(2):
                     here = ain[2 * k + pc, 16 + 128 * h : 144 + 128 * h, pl.ds(la, 128)].astype(F32)
-                    acc = None
-                    for t, gsrc, ro, moved in taps_of(k, pc, True):
+
+                    def load(gsrc, ro, moved):
                         at = pl.ds(pl.multiple_of(16 + 16 * ro + 128 * h, 16), 128)
-                        src = (side if moved else base)[gsrc, at, pl.ds(l0, 128)].astype(F32)
-                        term = src * kr[t]
-                        acc = term if acc is None else acc + term
-                        gk[t] = gk[t] + jnp.sum((src * here).reshape(16, 8, 128), axis=0)
+                        return (side if moved else base)[gsrc, at, pl.ds(l0, 128)]
+
+                    acc = conv_both(load, here, kr, gk, taps_of(k, pc, True))
                     gp[pc, h * 128 : h * 128 + 128, pl.ds(la, 128)] = acc
             for t in range(9):
                 sg2[t : t + 1, pl.ds(la, 128)] = jnp.sum(gk[t], axis=0, keepdims=True)
@@ -1307,8 +1445,7 @@
 
         lax.fori_loop(0, 3, conv_one_back, 0)
     all2.go(0)
-    sum_q.s1()
-    sum_q.s2()
+    line_u.s1()
 
     def one_back(n, _):
         jj = n // 2
@@ -1328,74 +1465,23 @@
         return 0
 
     lax.fori_loop(0, 4, one_back, 0)
-    hand_back(stg_t, v.gland, ro_gin)
-    mgs2, mgr2 = v.mgs2, v.mgr2
     mgs2[...] = mg2[...].astype(BF)
     mg2_cp = swap(mgs2, mgr2, sib)
 
-    o_wout[...] = sum_o.s3().astype(BF)
-    line_o.s0()
-    mg_cp.wait_recv()
-    mga1, mga2 = v.mga1, v.mga2
-    slot = 4 * col + r
-
-    class Gather:
-        def __init__(self, own, got, everyone):
-            self.own, self.got, self.everyone = own, got, everyone
-            self.zr, self.zs = sem(4), sem(3)
-            self.xy = sem(4)
-
-        def s0(self):
-            self.everyone[slot] = (self.own[...].astype(F32) + self.got[...].astype(F32)).astype(BF)
-            place = self.everyone.at[slot]
-            for d, s in enumerate((r1, r2, r3)):
-                cp = remote(place, place, self.zs + d, self.zr + r, (c, s))
-                cp.start()
-                last.append(cp.wait_send)
-
-        def s1(self):
-            for s in (r1, r2, r3):
-                place = self.everyone.at[4 * col + s]
-                local(place, place, self.zr + s).wait()
-            place = self.everyone.at[pl.ds(4 * col, 4)]
-            self.cx = remote(place, place, self.xy, self.xy + 1, px)
-            self.cx.start()
-            last.append(self.cx.wait_send)
-
-        def s2(self):
-            self.cx.wait_recv()
-            place = self.everyone.at[pl.ds(8 * y, 8)]
-            self.cy = remote(place, place, self.xy + 2, self.xy + 3, py)
-            self.cy.start()
-            last.append(self.cy.wait_send)
-
-        def s3(self):
-            self.cy.wait_recv()
-
-    gat1 = Gather(mgs1, mgr1, mga1)
-    gat2 = Gather(mgs2, mgr2, mga2)
-    gat1.s0()
-    all1.end(1)
-    all1.go(2)
+    sum_o.s1()
+    sum_o.s2()
+    all2.end(0)
+    all2.go(1)
+    line_a.s1()
     mg2_cp.wait_recv()
     gat2.s0()
-    all2.end(0)
-    all2.go(1)
-    gat1.s1()
-    line_u.s2()
-    line_d.s3()
+    hand_back(stg_t, v.gland, ro_gin)
 
     def load_again(p):
-        return local(wada_h.at[:, pl.ds(p * D, D)], wup.at[:, pl.ds((p % 2) * D, D)], s_wa + p % 2)
+        return local(wada_h.at[:, pl.ds(p * D, D)], wdn.at[pl.ds((p % 2) * D, D), :], s_wa + p % 2)
 
     load_again(2).start()
     load_again(3).start()
-    line_o.s1()
-    gat2.s1()
-    all1.end(2)
-    all1.go(3)
-    all2.end(1)
-    all2.go(2)
 
     def pick(p):
         ri, ci = iota((16, 16), 0), iota((16, 16), 1)
@@ -1407,13 +1493,13 @@
     for p in range(2, 6):
         load_again(p).wait()
         lhs = dot(pick(p - 2), my1).astype(BF)
-        cg = cg + dot_t(lhs, wup[:, (p % 2) * D : (p % 2) * D + D])
+        cg = cg + dot_t(lhs, wdn[(p % 2) * D : (p % 2) * D + D, :])
         load_again((p + 2) % 6).start()
     for p in range(2):
         load_again(p).wait()
         for h in range(2):
             lhs = dot(pick(2 * p + h), my2).astype(BF)
-            cg = cg + dot_t(lhs, wup[:, p * D + h * HB : p * D + h * HB + HB])
+            cg = cg + dot_t(lhs, wdn[p * D : p * D + D, h * HB : h * HB + HB])
     cond = condc[...]
     sig = 1.0 / (1.0 + jnp.exp(-cond))
     cgsum = v.cgsum
@@ -1442,25 +1528,31 @@
         last.append(done)
 
     total_q = sum_q.s3()
-    gwu[3, :, 0 : 3 * HB] = total_q.astype(BF)
+    wup[576:768, 0 : 3 * HB] = total_q.astype(BF)
     half_q = swap(
-        gwu.at[3, pl.ds(pl.multiple_of(96 * (1 - k), 32), 96), pl.ds(0, 3 * HB)], v.sq, sib
+        wup.at[pl.ds(pl.multiple_of(576 + 96 * (1 - k), 32), 96), pl.ds(0, 3 * HB)], v.sq, sib
     )
     for part in range(3):
-        o_wqkv[:, pl.ds(pl.multiple_of(part * D + HB * k, 128), HB)] = gwu[3, mine96, part * HB : (part + 1) * HB]
+        o_wqkv[:, pl.ds(pl.multiple_of(part * D + HB * k, 128), HB)] = wup[
+            pl.ds(pl.multiple_of(576 + 96 * k, 32), 96), part * HB : (part + 1) * HB
+        ]
     half_q.wait_recv()
     for part in range(3):
         o_wqkv[:, pl.ds(pl.multiple_of(part * D + HB * (1 - k), 128), HB)] = v.sq[:, part * HB : (part + 1) * HB]
     line_q.s0()
-    line_u.s3()
-    gat1.s2()
-    line_o.s2()
-    all1.end(3)
-    all1.go(4)
-    all2.end(2)
-    all2.go(3)
+    all2.end(1)
+    all2.go(2)
+    line_u.s2()
+    o_wout[...] = sum_o.s3().astype(BF)
+    line_o.s0()
+    all2.plane()
+    line_b.s0()
+    gat2.s1()
+    line_q.s1()
+    line_o.s1()
+    line_a.s2()
     gat2.s2()
-    line_q.s1()
+    line_b.s1()
     for done in tok_passed:
         done()
     landed(v.oland, ro_out, o_out, 0)
@@ -1474,12 +1566,8 @@
     def spread(p):
         return dot(cond_t, ones_where((en // 16 == ej // 4) & (en % 16 == 4 * p + ej % 4))).astype(BF)
 
-    all1.end(4)
-    o_sg1[...] = sg1[...]
-    all2.end(3)
-    all2.go(4)
     gat1.s3()
-    o_bada[...] = jnp.zeros((8, D), F32)
+    o_bada[...] = jnp.zeros((8, 6 * D), F32)
     every1 = mga1[...].reshape(256, D)
 
     def ada_out(p):
@@ -1490,55 +1578,93 @@
     for p in range(4):
         wdn[(p + 2) * 96 : (p + 3) * 96, :] = dot(spread(p), every1).astype(BF)
         ada_out(p + 2)
-        o_bada[p + 2 : p + 3, :] = dot(ones_where((bn % 16) // 4 == p), every1)[0:1]
-    line_o.s3()
+        o_bada[0:1, (p + 2) * D : (p + 3) * D] = dot(ones_where((bn % 16) // 4 == p), every1)[0:1]
     line_q.s2()
+    line_o.s2()
     gat2.s3()
     every2 = mga2[...].reshape(256, HB)
     for p in range(4):
         half = (p % 2) * HB
         wdn[p // 2 * 96 : p // 2 * 96 + 96, half : half + HB] = dot(spread(p), every2).astype(BF)
-        o_bada[p // 2 : p // 2 + 1, (p % 2) * HB : (p % 2) * HB + HB] = dot(ones_where((bn % 16) // 4 == p), every2)[0:1]
+        o_bada[0:1, p * HB : (p + 1) * HB] = dot(ones_where((bn % 16) // 4 == p), every2)[0:1]
     ada_out(0)
     ada_out(1)
-    all2.end(4)
-    o_sg2[...] = sg2[...]
+    line_b.s2()
+    line_d.s3()
+    line_u.s3()
     landed(v.gland, ro_gin, o_gin, 2)
     for i in range(2):
         local(crcv.at[i], crcv.at[i], cr + i).wait()
-    o_cond[...] = crcv[0] + crcv[1]
+    both = crcv[0] + crcv[1]
+    for i in range(2):
+        o_cond[i] = both[4 * i : 4 * i + 4]
+    line_a.s3()
+    o_sg1[...] = v.sg1s[0].astype(F32)
+    line_b.s3()
+    o_sg2[...] = v.sg2s[0].astype(F32)
+    line_o.s3()
     line_q.s3()
     for done in last:
         done()
-    for s in (sum_d, sum_o, sum_q):
+    for s in (sum_d, sum_u, sum_o, sum_q):
         s.sent()
     assert count[0] <= N_SEMS, count[0]
+
+
+def finish(
+    out, gin, gcond, wada, bada_h, sg1_h, sg2_h, wqkv, wout, wup, wdn,
+    f_out, f_gin, f_gcond, f_wada, f_bada, f_conv1, f_wqkv, f_bqv, f_wout, f_bout, f_wup, f_bup, f_conv2, f_wdn,
+    f_bdn, sems, *bufs,
+):
+    c = lax.axis_index("canvas")
+    bada, sg1, sg2, narrow, wide = bufs[0], bufs[1], bufs[2], bufs[3:9], bufs[9:15]
+    small = ((sg1_h, sg1), (sg2_h, sg2), (bada_h, bada))
+    large = ((wada, f_wada), (gin, f_gin), (wup, f_wup), (wdn, f_wdn), (wqkv, f_wqkv), (wout, f_wout))
+    ins = [pltpu.make_async_copy(src, buf, sems.at[i]) for i, ((src, _), buf) in enumerate(zip(large, narrow))]
+    ins += [pltpu.make_async_copy(src, buf, sems.at[6 + i]) for i, (src, buf) in enumerate(small)]
+    outs = [pltpu.make_async_copy(buf, dst, sems.at[9 + i]) for i, ((_, dst), buf) in enumerate(zip(large, wide))]
+    ins.append(pltpu.make_async_copy(out, bufs[15], sems.at[15]))
+    ins.append(pltpu.make_async_copy(gcond, f_gcond, sems.at[16]))
+    outs.append(pltpu.make_async_copy(bufs[15], f_out, sems.at[15]))
+    for cp in ins:
+        cp.start()
+    for i in range(6):
+        ins[i].wait()
+        wide[i][...] = narrow[i][...].astype(F32)
+        outs[i].start()
+    for cp in ins[6:]:
+        cp.wait()
+    outs[6].start()
+
+    def cut(rows, n):
+        wide = rows.shape[1]
+        return pltpu.roll(rows, lax.rem(wide - c * n, wide), 1)[:, 0:n]
+
+    f_bada[...] = cut(bada[...], 576)[0:1]
+    f_conv1[...] = cut(sg2[...], 96)[0:9]
+    both = jnp.concatenate([sg2[8:16, :], sg2[8:16, :]], axis=1)
+    f_bqv[...] = cut(jnp.where(iota((8, 2 * D), 1) < D, both, pltpu.roll(both, 7, 0)), 192)[1:2]
+    f_bout[...] = cut(sg1[8:16, D : 2 * D], 96)[2:3]
+    f_bdn[...] = cut(sg1[8:16, 0:D], 96)[2:3]
+    ln = pl.ds(pl.multiple_of(c * HB, 128), HB)
+    f_bup[...] = sg1[9:10, ln]
+    f_conv2[...] = sg1[0:9, ln]
+    for cp in outs:
+        cp.wait()
 
 
 def fast_shards(
     tokens, latent, condition, w_ada, b_ada, conv_attn, w_qkv, bias_qv, w_out, b_out,
     w_up, b_up, conv_ffn, w_down, b_down, cotangent,
 ):
-    f = lambda a: a.astype(F32)
-    conv_rows = jnp.pad(f(conv_attn), ((0, 3), (0, 0))).reshape(3, 4 * D)
-    ada_rows = jnp.pad(f(b_ada), (0, 2 * D)).reshape(2, 4 * D)
-    par = jnp.concatenate(
-        [
-            f(conv_ffn),
-            f(b_up)[None],
-            jnp.concatenate([f(b_down), f(b_out), f(bias_qv)])[None],
-            conv_rows,
-            ada_rows,
-        ]
-    )
     anyspace = pl.BlockSpec(memory_space=pl.ANY)
     vm = pl.BlockSpec(memory_space=pltpu.VMEM)
     outs = (
         ((2, 256, D), BF),
         ((2, 256, D), BF),
-        ((8, D), F32),
+        ((2, 4, D), F32),
         ((96, 6 * D), BF),
-        ((8, D), F32),
+        ((8, 6 * D), F32),
         ((16, FF), F32),
         ((16, D), F32),
         ((96, 3 * D), BF),
@@ -1546,39 +1672,42 @@
         ((96, FF), BF),
         ((HB, D), BF),
     )
-    out, gin, gcond, gwada, gbada, sg1, sg2, gwqkv, gwout, gwup, gwdn = pl.pallas_call(
+    got = pl.pallas_call(
         whole_block,
         out_shape=[jax.ShapeDtypeStruct(s, t) for s, t in outs],
-        in_specs=[anyspace, anyspace, vm, vm, anyspace, vm, anyspace, anyspace, anyspace, anyspace],
+        in_specs=[anyspace, anyspace, vm, vm] + [anyspace] * 5 + [vm] * 7,
         out_specs=[anyspace, anyspace, vm, anyspace] + [vm] * (len(outs) - 4),
         scratch_shapes=[pltpu.SemaphoreType.DMA((N_SEMS,))] + [pltpu.VMEM(s, t) for s, t in SCRATCH.values()],
         compiler_params=pltpu.CompilerParams(
             collective_id=0, has_side_effects=True, vmem_limit_bytes=VMEM_LIMIT
         ),
         name="block",
-    )(tokens, cotangent, latent.reshape(2, 1, 256), condition.reshape(8, D), w_ada, par, w_qkv, w_out, w_up, w_down)
-    c = lax.axis_index("canvas")
-
-    def share(a, dim, n):
-        return lax.dynamic_slice_in_dim(a, c * n, n, dim)
-
-    bq = sg2[9:11].reshape(2 * D)
+    )(
+        tokens, cotangent, latent, condition, w_ada, w_qkv, w_out, w_up, w_down,
+        b_ada, conv_attn, bias_qv, b_out, b_up, conv_ffn, b_down,
+    )
+    big = ((96, 6 * D), (2, 256, D), (96, FF), (HB, D), (96, 3 * D), (96, D))
+    shapes = (
+        (2, 256, D), (2, 256, D), (2, 4, D), (96, 6 * D), (1, 576), (9, 96), (96, 3 * D), (1, 192), (96, D), (1, 96),
+        (96, FF), (1, HB), (9, HB), (HB, D), (1, 96),
+    )
+    out, gin, gcond, wada, bada, conv1, wqkv, bqv, wout, bout, wup, bup, conv2, wdn, bdn = pl.pallas_call(
+        finish,
+        out_shape=[jax.ShapeDtypeStruct(s, F32 if i else BF) for i, s in enumerate(shapes)],
+        in_specs=[anyspace] * 11,
+        out_specs=[anyspace if i in (0, 1, 3, 6, 8, 10, 13) else vm for i in range(len(shapes))],
+        scratch_shapes=[pltpu.SemaphoreType.DMA((17,))]
+        + [pltpu.VMEM(s, F32) for s in ((8, 6 * D), (16, FF), (16, D))]
+        + [pltpu.VMEM(s, BF) for s in big]
+        + [pltpu.VMEM(s, F32) for s in big]
+        + [pltpu.VMEM((2, 256, D), BF)],
+        compiler_params=pltpu.CompilerParams(vmem_limit_bytes=VMEM_LIMIT),
+        name="finish",
+    )(*got)
+    flat = lambda a: a.reshape(a.shape[1])
     return (
-        out,
-        f(gin),
-        gcond.reshape(2, 4, D),
-        f(gwada),
-        share(gbada[0:6].reshape(6 * D), 0, 576),
-        share(sg2[0:9], 1, 96),
-        f(gwqkv),
-        share(bq, 0, 192),
-        f(gwout),
-        share(sg1[10, D : 2 * D], 0, 96),
-        f(gwup),
-        share(sg1[9], 0, 384),
-        share(sg1[0:9], 1, 384),
-        f(gwdn),
-        share(sg1[10, 0:D], 0, 96),
+        out, gin, gcond, wada, flat(bada), conv1, wqkv, flat(bqv), wout, flat(bout),
+        wup, flat(bup), conv2, wdn, flat(bdn),
     )
 
 

time: 245 us -> 205 us (0.84)
  Pallas kernels: 219 us -> 202 us
  local copies, waits for them, and re-layouts: 15 us -> 0 us
  other arithmetic: 9.15 us -> 2.55 us
    pallas_call x1, Pallas kernels: 219 us -> 197 us  [fast_shards(): pl.pallas_call(whole_block, out_shape=[jax.ShapeDtypeStruct(s, t) for s,...]
    convert_element_type x6 -> x0, other arithmetic: 7.73 us -> none  [fast_shards(): f = lambda a: a.astype(F32)]
    dynamic_slice x6 -> x0, local copies, waits for them, and re-layouts: 5.23 us -> none  [share(): return lax.dynamic_slice_in_dim(a, c * n, n, dim)]
    pallas_call x0 -> x1, Pallas kernels: none -> 5.17 us  [fast_shards(): pl.pallas_call(finish, out_shape=[jax.ShapeDtypeStruct(s, F32 if i else B...]
    reshape x7 -> x0, local copies, waits for them, and re-layouts: 3.29 us -> none  [the longest x1 1.36 us: fast_shards(): condition.reshape(8, D)]
    pallas_call x0 -> x2, other arithmetic: none -> 2.55 us  [fast_shards(): pl.pallas_call(finish, out_shape=[jax.ShapeDtypeStruct(s, F32 if i else B...]
where the time goes in v2:
time: 205 us
  Pallas kernels  202 us (99%)
  other arithmetic  2.55 us (1%)
    pallas_call x1, Pallas kernels, fast_shards(): pl.pallas_call(whole_block, out_shape=[jax.ShapeDtypeStruct(s, t) for s,...  197 us
    pallas_call x1, Pallas kernels, fast_shards(): pl.pallas_call(finish, out_shape=[jax.ShapeDtypeStruct(s, F32 if i else B...  5.17 us

profile of v2, /device:TPU:0, one launch (start us, length us, event | category | flops | bytes accessed | tf_op | source)
XLA Modules:
  0.0 204.9 jit_solution(9725707160868875181)
XLA Ops:
  0.7 196.5 %block.1 = (bf16[2,256,768]{2,1,0:T(8,128)(2,1)}, bf16[2,256,768]{2,1,0:T(8,128)(2,1)}, f32[2,4,768]{2,1,0:T(4,128)}, bf16[96,4608]{1,0:T(8,128)(2,1)}, f32[8,46...) custom-call(bf16[2,256,768]{2,1,0:T(8,128)(2,1)} %tok_h.1, ...), custom_call_target="tpu_custom_call" | custom-call | tf_op jit(solution)/shard_map/block/pallas_call | solution.py:1675
  197.2 5.2 %finish.1 = (bf16[2,256,768]{2,1,0:T(8,128)(2,1)}, f32[2,256,768]{2,1,0:T(8,128)}, f32[2,4,768]{2,1,0:T(4,128)}, f32[96,4608]{1,0:T(8,128)}, f32[1,576]{1,0:T(1,...) custom-call(bf16[2,256,768]{2,1,0:T(8,128)(2,1)} %get-tuple-element., ...), custom_call_target="tpu_custom_call" | custom-call | tf_op jit(solution)/shard_map/finish/pallas_call | solution.py:1694
  202.3 1.3 reduce.1
  203.6 1.3 reduce

commit v3 on v2

--- a/solution.py
+++ b/solution.py
@@ -553,7 +553,7 @@
     cond_own=((8, D), F32),
     par=((16, FF), F32),
 )
-N_SEMS = 240
+N_SEMS = 340
 
 
 def whole_block(
@@ -740,7 +740,7 @@
     ft, fl, fc = sem(4), sem(4), sem(4)
     order = (r, r1, r2, r3)
 
-    def arrive(buf, of, rs, fs):
+    def arrive(buf, of, rs, fs, then=None):
         passed = []
         for d in range(4):
             s = order[d]
@@ -758,40 +758,35 @@
                     cp.wait_send()
 
             passed.append(done)
+            if then is not None:
+                then(s)
         return passed
 
     def slab(s):
         return (slice(None), pl.ds(pl.multiple_of(s * 64, 64), 64), slice(None))
 
     last.extend(arrive(latc, lambda s: s, rl, fl))
-    tok_passed = arrive(tok, slab, rt, ft)
+    def norm_one(s):
+        rows = jnp.broadcast_to(latc[s].astype(F32), (128, 256)).astype(BF)
+        ids = dot_t(pm[...], rows)
+        lane = iota((256, 128), 1)
+        want = (lane % 16 - 4 * r).astype(F32)
+        o = ones_where((want == ids) & (lane < 32))
+        at = pl.ds(pl.multiple_of(s * 64, 64), 64)
+        lv[:, at, :] = ids.reshape(4, 64, 128)
+        oh[:, at, :] = o.reshape(4, 64, 128)
+        nrm, _inv = norm_parts(tok[:, at, :].reshape(256, D).astype(F32))
+        h = (nrm * (1.0 + piece(o, 1)) + piece(o, 0)).astype(BF)
+        padded = pl.ds(pl.multiple_of(s * 64 + 16, 16), 64)
+        ain[:, padded, :] = h.reshape(4, 64, D)
+        for g in range(4):
+            sh = shifted(h[g * 64 : g * 64 + 64].astype(F32), g % 2).astype(BF)
+            us[g, padded, :] = sh[:, 0:HB]
+            gs[g, padded, :] = sh[:, HB:D]
+
+    tok_passed = arrive(tok, slab, rt, ft, norm_one)
     for i in range(2):
         cot_sent.append(give(stg_c.at[i], cot.at[:, mine64, :], sc + i, rc + r, i))
-
-    for s in range(4):
-        rows = jnp.broadcast_to(latc[s].astype(F32), (128, 256)).astype(BF)
-        ids = dot_t(pm[...], rows)
-        for g in range(4):
-            lv[g, s * 64 : s * 64 + 64, :] = ids[g * 64 : g * 64 + 64]
-    for g in range(4):
-        lane = iota((256, 128), 1)
-        want = (lane % 16 - 4 * r).astype(F32)
-        oh[g] = ones_where((want == lv[g]) & (lane < 32))
-
-    def norm_one(n, _):
-        t0 = pl.multiple_of((n % 2) * 128, 128)
-        for pc in range(2):
-            g = 2 * (n // 2) + pc
-            nrm, _inv = norm_parts(tok[g, pl.ds(t0, 128), :].astype(F32))
-            o = oh[g, pl.ds(t0, 128), :]
-            h = (nrm * (1.0 + piece(o, 1)) + piece(o, 0)).astype(BF)
-            ain[g, pl.ds(t0 + 16, 128), :] = h
-            sh = shifted(h.astype(F32), pc).astype(BF)
-            us[g, pl.ds(t0 + 16, 128), :] = sh[:, 0:HB]
-            gs[g, pl.ds(t0 + 16, 128), :] = sh[:, HB:D]
-        return 0
-
-    lax.fori_loop(0, 4, norm_one, 0)
 
     for hh in range(2):
         side = us if hh == 0 else gs
@@ -867,7 +862,6 @@
     lax.fori_loop(0, 4, attend, 0)
     low_x.wait_recv()
     low_y = swap(clow.at[pl.ds(2 * y, 2)], clow.at[pl.ds(2 * y, 2)], py)
-    last.extend(arrive(cot, slab, rc, fc))
 
     ld_wo.wait()
     kother = pl.multiple_of(HB * (1 - k), 128)
@@ -884,12 +878,18 @@
             tmpa[g, rows, :] = f
             at = pl.ds(pl.multiple_of(g * 256 + h * 128, 128), 128)
             fint[:, at] = f.astype(F32).T.astype(BF)
-            bg[g, rows, :] = (piece(o, 5) * cot[g, rows, :].astype(F32)).astype(BF)
         return 0
 
     for g in range(4):
         att_copy(g).wait()
     lax.fori_loop(0, 4, norm_two, 0)
+    last.extend(arrive(cot, slab, rc, fc))
+
+    def gate_cot(g, _):
+        bg[g] = (piece(oh[g], 5) * cot[g].astype(F32)).astype(BF)
+        return 0
+
+    lax.fori_loop(0, 4, gate_cot, 0)
 
     class Scatter:
         def __init__(self, src, a, b, rx, ry):
@@ -931,23 +931,21 @@
     inner = (r % 3) != 0
 
     class Line:
-        def __init__(self, out, za, zb, cuts):
-            n = out.shape[0] // cuts
+        def __init__(self, pieces):
             self.parts = []
-            for i in range(cuts):
-                rows = pl.ds(i * n, n)
-                o, a, b = out.at[rows], za.at[rows], zb.at[rows]
+            for o, a, b in pieces:
                 ss = sem(6)
                 up = remote(o, a, ss, ss + 1, (c, r1))
                 mid = remote(o, b, ss + 2, ss + 3, (c, r3))
                 down = remote(o, a, ss + 4, ss + 5, (c, r1))
                 self.parts.append((o, a, b, up, mid, down))
 
-        def s0(self):
+        def s0(self, which=None):
             @pl.when(jnp.logical_not(inner))
             def _():
-                for part in self.parts:
-                    part[3].start()
+                for i, part in enumerate(self.parts):
+                    if which is None or which == i:
+                        part[3].start()
 
         def s1(self):
             @pl.when(inner)
@@ -1011,6 +1009,69 @@
         def s3(self):
             self.cy.wait_recv()
 
+    def by_rows(out, za, zb, cuts):
+        n = out.shape[0] // cuts
+        rows = [pl.ds(i * n, n) for i in range(cuts)]
+        return Line([(out.at[at], za.at[at], zb.at[at]) for at in rows])
+
+    class Columns:
+        def __init__(self, src, a, b, rx, ry, su, out, za, zb):
+            self.src, self.a, self.b, self.rx, self.ry, self.su, self.out = src, a, b, rx, ry, su, out
+            count = su.shape[1] // HB
+            self.lanes = [pl.ds(t * HB, HB) for t in range(count)]
+            self.cps = []
+            for ln in self.lanes:
+                ss = sem(10)
+                self.cps.append(
+                    (
+                        remote(src(0, 0, 96, ln), a.at[:, ln], ss, ss + 1, px),
+                        remote(src(0, 96, 96, ln), b.at[:, ln], ss + 2, ss + 3, py),
+                        remote(src(1, 0, 192, ln), rx.at[:, ln], ss + 4, ss + 5, px),
+                        remote(src(2, 0, 192, ln), ry.at[:, ln], ss + 6, ss + 7, py),
+                        remote(
+                            src(3, pl.multiple_of(96 * (1 - k), 32), 96, ln), su.at[:, ln], ss + 8, ss + 9, sib
+                        ),
+                    )
+                )
+            both = [pl.ds(t * D, D) for t in range(count)]
+            self.line = Line([(out.at[:, at], za.at[:, at], zb.at[:, at]) for at in both])
+
+        def s0(self, t):
+            self.cps[t][0].start()
+            self.cps[t][1].start()
+
+        def s1(self, t):
+            ca, cb, cx, cy, _ = self.cps[t]
+            ln = self.lanes[t]
+            cb.wait_recv()
+            part = self.src(1, 96, 96, ln)
+            part[...] = (part[...].astype(F32) + self.b[:, ln].astype(F32)).astype(BF)
+            cx.start()
+            ca.wait_recv()
+            part = self.src(2, 0, 96, ln)
+            part[...] = (part[...].astype(F32) + self.a[:, ln].astype(F32)).astype(BF)
+            cy.start()
+
+        def s3(self, t):
+            ln = self.lanes[t]
+            self.cps[t][2].wait_recv()
+            self.cps[t][3].wait_recv()
+            part = self.src(3, 0, 192, ln)
+            part[...] = (part[...].astype(F32) + self.rx[:, ln].astype(F32) + self.ry[:, ln].astype(F32)).astype(BF)
+            self.cps[t][4].start()
+            mine = self.src(3, pl.multiple_of(96 * k, 32), 96, ln)
+            self.out[:, pl.ds(pl.multiple_of(t * D + HB * k, 128), HB)] = mine[...]
+
+        def s4(self, t):
+            self.cps[t][4].wait()
+            self.out[:, pl.ds(pl.multiple_of(t * D + HB * (1 - k), 128), HB)] = self.su[:, self.lanes[t]]
+            self.line.s0(t)
+
+        def sent(self):
+            for cps in self.cps:
+                for cp in cps[0:4]:
+                    cp.wait_send()
+
     class Everyone:
         def __init__(self, total, send, recv):
             self.total, self.send, self.recv = total, send, recv
@@ -1036,18 +1097,24 @@
     gat1 = Gather(mgs1, mgr1, mga1)
     gat2 = Gather(mgs2, mgr2, mga2)
     sum_d = Scatter(lambda p, r0, n: gwd.at[p, pl.ds(r0, n)], v.rd_a, v.rd_b, v.rd_x, v.rd_y)
-    sum_u = Scatter(lambda p, r0, n: upr.at[p, pl.ds(r0, n)], v.ru_a, v.ru_b, v.ru_x, v.ru_y)
+    sum_u = Columns(
+        lambda p, r0, n, ln: upr.at[p, pl.ds(r0, n), ln],
+        v.ru_a, v.ru_b, v.ru_x, v.ru_y, v.su, o_wup, v.zu_a, v.zu_b,
+    )
+    sum_q = Columns(
+        lambda p, r0, n, ln: wup.at[pl.ds(192 * p + r0, n), ln],
+        v.rq_a, v.rq_b, v.rq_x, v.rq_y, v.sq, o_wqkv, v.zq_a, v.zq_b,
+    )
     sum_o = Scatter(lambda p, r0, n: gwo.at[p, pl.ds(r0, n)], v.ro_a, v.ro_b, v.ro_x, v.ro_y)
-    sum_q = Scatter(lambda p, r0, n: wup.at[pl.ds(192 * p + r0, n), pl.ds(0, 3 * HB)], v.rq_a, v.rq_b, v.rq_x, v.rq_y)
-    line_d = Line(o_wdn, v.zd_a, v.zd_b, 2)
-    line_u = Line(o_wup, v.zu_a, v.zu_b, 2)
-    line_o = Line(o_wout, v.zo_a, v.zo_b, 1)
-    line_q = Line(o_wqkv, v.zq_a, v.zq_b, 2)
+    line_d = by_rows(o_wdn, v.zd_a, v.zd_b, 4)
+    line_u = sum_u.line
+    line_o = by_rows(o_wout, v.zo_a, v.zo_b, 1)
+    line_q = sum_q.line
     sg1, sg2 = v.sg1, v.sg2
     all1 = Everyone(sg1, v.sg1s, v.sg1r)
     all2 = Everyone(sg2, v.sg2s, v.sg2r)
-    line_a = Line(v.sg1s.at[0], v.sg1r.at[3], v.sg1r.at[4], 1)
-    line_b = Line(v.sg2s.at[0], v.sg2r.at[3], v.sg2r.at[4], 1)
+    line_a = Line([(v.sg1s.at[0], v.sg1r.at[3], v.sg1r.at[4])])
+    line_b = Line([(v.sg2s.at[0], v.sg2r.at[3], v.sg2r.at[4])])
     sg1[...] = jnp.zeros((16, FF), F32)
     sg2[...] = jnp.zeros((16, D), F32)
 
@@ -1152,12 +1219,12 @@
         lane = iota((128, 128), 1)
         return ones_where((lane - 4 * p).astype(F32) == ids)
 
-    def hand_back(src, land, rs):
-        ss = sem(4)
-        for s in range(4):
+    def hand_back(src, land, rs, slabs):
+        for s in slabs:
+            ss = sem()
             dst = land.at[r % 2, pl.ds(2 * k, 2)]
             at = rs + (r % 2) * 2 + k
-            far = remote(src.at[:, s], dst, ss + s, at, (owner_c, s))
+            far = remote(src.at[:, s], dst, ss, at, (owner_c, s))
             near = local(src.at[:, s], dst, at)
             here = is_own & (r == s)
 
@@ -1201,18 +1268,24 @@
         m = tok[g, rows, :].astype(F32) + piece(o, 2) * ao
         gp[jj, rows, :] = m
         branch = mid[jj, rows, :] + v.brcv[jj, h64].reshape(128, D).astype(F32) + par[10:11, 0:D]
+        v.brcv[jj, h64] = ao.astype(BF).reshape(2, 64, D)
         stg_c[jj, h64] = (m + piece(o, 5) * branch).astype(BF).reshape(2, 64, D)
         low = (cot[g, rows, :].astype(F32) * branch).astype(BF)
         mg1[...] += dot_l(place_rows(lv[g, rows, :], 3), low)[0:16]
         return bd + jnp.sum(bg[g, rows, :].astype(F32), axis=0, keepdims=True)
 
     sg1[10:11, 0:D] = lax.fori_loop(0, 4, out_half, o_rows)
-    hand_back(stg_c, v.oland, ro_out)
-    def hidden_back(pos, _):
-        b = block_at(pos)
+    hand_back(stg_c, v.oland, ro_out, range(4))
+    def pos_of(b):
+        bx, by = b % 2, b // 2
+        fx = (bx - x) * (bx - x)
+        fy = (by - y) * (by - y)
+        return 2 * (1 - fx) + 1 - fy
+
+    def hidden_back(b, _):
         lo = pl.multiple_of(b * HB, 128)
         wide = pl.multiple_of(HB * (2 * b + k), 128)
-        pl.when(pos == 2)(down_total)
+        pl.when(b == 2)(down_total)
 
         def down_grad(pr, _):
             both = dot_t(bg[pl.ds(2 * pr, 2)].reshape(512, D), wdn[pl.ds(lo, HB), :])
@@ -1247,6 +1320,18 @@
             return 0
 
         lax.fori_loop(0, 3, conv_back, 0)
+        got = dot(fint[...], upg[:, :, pl.ds(lo, HB)].reshape(1024, HB)).astype(BF)
+        for rb in range(4):
+            upr[pos_of(rb), 0:192, pl.ds(lo, HB)] = got[rb * 192 : rb * 192 + 192]
+        for t in range(4):
+
+            @pl.when(b == t)
+            def _(t=t):
+                sum_u.s0(t)
+                if t >= 1:
+                    sum_u.s1(t - 1)
+                if t >= 3:
+                    sum_u.s3(t - 3)
 
         return 0
 
@@ -1257,29 +1342,18 @@
         stg_t[:, :, :, cols] = half_f(other2, n).astype(BF).reshape(2, 4, 64, HB)
     f_cp = remote(stg_t, v.frcv, sem(), sem(), sib)
     f_cp.start()
+    sum_u.s3(1)
+    sum_u.s4(0)
     for n in range(2):
         cols = slice(n * HB, n * HB + HB)
         mid[:, :, cols] = half_f(mine2, n).reshape(2, 256, HB)
 
-    def pos_of(b):
-        bx, by = b % 2, b // 2
-        fx = (bx - x) * (bx - x)
-        fy = (by - y) * (by - y)
-        return 2 * (1 - fx) + 1 - fy
-
-    def grad_up(nt, _):
-        ln = pl.ds(pl.multiple_of(nt * 256, 128), 256)
-        got = dot(fint[...], upg[:, :, ln].reshape(1024, 256)).astype(BF)
-        for b in range(4):
-            upr[pos_of(b), 0:192, ln] = got[b * 192 : b * 192 + 192]
-        return 0
-
-    lax.fori_loop(0, 6, grad_up, 0)
-    sum_u.s0()
-    line_d.s1()
+    sum_u.s1(3)
+    sum_u.s4(1)
     f_cp.wait()
 
     def two_back(n, bo):
+        pl.when(n == 3)(line_d.s1)
         jj = n // 2
         g = 2 * k + jj
         rows = pl.ds(pl.multiple_of((n % 2) * 128, 128), 128)
@@ -1293,7 +1367,7 @@
         ag = (gate1 * mg).astype(BF)
         tmpa[g, rows, :] = ag
         ids = lv[g, rows, :]
-        ao = dot(att[g, rows, :], wo[...]) + par[10:11, D : 2 * D]
+        ao = v.brcv[jj, h64].reshape(128, D).astype(F32)
         total = dot_l(place_rows(ids, 0), (mg * ao).astype(BF))
         total = total + dot_l(place_rows(ids, 1), fg.astype(BF))
         total = total + dot_l(place_rows(ids, 2), (fg * nrm).astype(BF))
@@ -1304,20 +1378,22 @@
     ag_place = tmpa.at[pl.ds(2 * k, 2)]
     ag_cp = swap(ag_place, ag_place, sib)
 
-    sum_u.s1()
-    sum_u.s2()
+    sum_u.s3(2)
+    sum_u.s3(3)
+    sum_u.s4(2)
     mgs1[...] = mg1[...].astype(BF)
     mg_cp = swap(mgs1, mgr1, sib)
     all1.go(0)
 
     ag_cp.wait_recv()
     mg_cp.wait_recv()
+    sum_u.s4(3)
     gat1.s0()
     dqkv = act
     kr_rows = pl.ds(kcol, HB)
 
     def heads_back(g, _):
-        pl.when(g == 2)(line_d.s2)
+        pl.when(g == 3)(line_d.s2)
         oq, mk = masks_of(g)
         mk2 = jnp.concatenate([mk, mk], axis=0)
         for h in range(2):
@@ -1356,6 +1432,7 @@
     lax.fori_loop(0, 4, heads_back, 0)
     all1.end(0)
     all1.go(1)
+    line_u.s1()
 
     def proj_back(g, _):
         upg[g, :, 0:D] = dot_t(dqkv[g, :, 0 : 3 * HB], wq[...]).astype(BF)
@@ -1369,10 +1446,15 @@
         got = dot(c1t[...], dqkv[:, :, ln].reshape(1024, HB)).astype(BF)
         for b in range(4):
             wup[pl.ds(pl.multiple_of(192 * pos_of(b), 64), 192), ln] = got[b * 192 : b * 192 + 192]
+        for t in range(3):
+
+            @pl.when(nt == t)
+            def _(t=t):
+                sum_q.s0(t)
+
         return 0
 
     lax.fori_loop(0, 3, grad_qkv, 0)
-    sum_q.s0()
     all1.end(1)
     all1.go(2)
     gat1.s1()
@@ -1389,19 +1471,8 @@
         return 0
 
     lax.fori_loop(0, 4, grad_out, 0)
-    total_u = sum_u.s3()
-    upr[3, 0:192, :] = total_u.astype(BF)
-    half_u = swap(
-        upr.at[3, pl.ds(pl.multiple_of(96 * (1 - k), 32), 96), :], v.su, sib
-    )
-    mine96 = pl.ds(pl.multiple_of(96 * k, 32), 96)
-    for b in range(4):
-        o_wup[:, pl.ds(pl.multiple_of(HB * (2 * b + k), 128), HB)] = upr[3, mine96, b * HB : (b + 1) * HB]
-    half_u.wait()
-    last.remove(half_u.wait_send)
-    for b in range(4):
-        o_wup[:, pl.ds(pl.multiple_of(HB * (2 * b + 1 - k), 128), HB)] = v.su[:, b * HB : (b + 1) * HB]
-    line_u.s0()
+    for t in range(3):
+        sum_q.s1(t)
     all1.plane()
     line_a.s0()
     cg_cp.wait_recv()
@@ -1418,8 +1489,8 @@
         return 0
 
     lax.fori_loop(0, 2, cg_sum, 0)
-    sum_q.s1()
-    sum_q.s2()
+    sum_o.s1()
+    sum_o.s2()
     gat1.s2()
     for hh in range(2):
         base, side = (ub, us) if hh == 0 else (gb, gs)
@@ -1445,13 +1516,16 @@
 
         lax.fori_loop(0, 3, conv_one_back, 0)
     all2.go(0)
-    line_u.s1()
+    sum_q.s3(0)
+    sum_q.s3(1)
+    line_u.s2()
+    sum_q.s4(0)
 
     def one_back(n, _):
-        jj = n // 2
+        jj = n % 2
         g = 2 * k + jj
-        rows = pl.ds(pl.multiple_of((n % 2) * 128, 128), 128)
-        h64 = pl.ds((n % 2) * 2, 2)
+        rows = pl.ds(pl.multiple_of((n // 2) * 128, 128), 128)
+        h64 = pl.ds((n // 2) * 2, 2)
         nrm, inv = norm_parts(tok[g, rows, :].astype(F32))
         ig = gp[jj, rows, :]
         gi = mid[jj, rows, :] + norm_back(ig * (1.0 + piece(oh[g, rows, :], 1)), nrm, inv)
@@ -1464,18 +1538,22 @@
         mg2[...] += total[0:16]
         return 0
 
-    lax.fori_loop(0, 4, one_back, 0)
+    lax.fori_loop(0, 2, one_back, 0)
+    hand_back(stg_t, v.gland, ro_gin, range(2))
+    sum_q.s4(1)
+    lax.fori_loop(2, 4, one_back, 0)
     mgs2[...] = mg2[...].astype(BF)
     mg2_cp = swap(mgs2, mgr2, sib)
 
-    sum_o.s1()
-    sum_o.s2()
+    sum_q.s3(2)
+    mg2_cp.wait_recv()
+    gat2.s0()
+    hand_back(stg_t, v.gland, ro_gin, range(2, 4))
+    sum_q.s4(2)
+    o_wout[...] = sum_o.s3().astype(BF)
+    line_o.s0()
     all2.end(0)
     all2.go(1)
-    line_a.s1()
-    mg2_cp.wait_recv()
-    gat2.s0()
-    hand_back(stg_t, v.gland, ro_gin)
 
     def load_again(p):
         return local(wada_h.at[:, pl.ds(p * D, D)], wdn.at[pl.ds((p % 2) * D, D), :], s_wa + p % 2)
@@ -1527,30 +1605,17 @@
 
         last.append(done)
 
-    total_q = sum_q.s3()
-    wup[576:768, 0 : 3 * HB] = total_q.astype(BF)
-    half_q = swap(
-        wup.at[pl.ds(pl.multiple_of(576 + 96 * (1 - k), 32), 96), pl.ds(0, 3 * HB)], v.sq, sib
-    )
-    for part in range(3):
-        o_wqkv[:, pl.ds(pl.multiple_of(part * D + HB * k, 128), HB)] = wup[
-            pl.ds(pl.multiple_of(576 + 96 * k, 32), 96), part * HB : (part + 1) * HB
-        ]
-    half_q.wait_recv()
-    for part in range(3):
-        o_wqkv[:, pl.ds(pl.multiple_of(part * D + HB * (1 - k), 128), HB)] = v.sq[:, part * HB : (part + 1) * HB]
-    line_q.s0()
     all2.end(1)
     all2.go(2)
-    line_u.s2()
-    o_wout[...] = sum_o.s3().astype(BF)
-    line_o.s0()
+    line_a.s1()
+    line_q.s1()
+    line_o.s1()
     all2.plane()
     line_b.s0()
     gat2.s1()
-    line_q.s1()
-    line_o.s1()
     line_a.s2()
+    line_q.s2()
+    line_o.s2()
     gat2.s2()
     line_b.s1()
     for done in tok_passed:
@@ -1579,8 +1644,6 @@
         wdn[(p + 2) * 96 : (p + 3) * 96, :] = dot(spread(p), every1).astype(BF)
         ada_out(p + 2)
         o_bada[0:1, (p + 2) * D : (p + 3) * D] = dot(ones_where((bn % 16) // 4 == p), every1)[0:1]
-    line_q.s2()
-    line_o.s2()
     gat2.s3()
     every2 = mga2[...].reshape(256, HB)
     for p in range(4):
@@ -1640,10 +1703,10 @@
         wide = rows.shape[1]
         return pltpu.roll(rows, lax.rem(wide - c * n, wide), 1)[:, 0:n]
 
-    f_bada[...] = cut(bada[...], 576)[0:1]
+    f_bada[...] = cut(bada[...], 576)[0]
     f_conv1[...] = cut(sg2[...], 96)[0:9]
     both = jnp.concatenate([sg2[8:16, :], sg2[8:16, :]], axis=1)
-    f_bqv[...] = cut(jnp.where(iota((8, 2 * D), 1) < D, both, pltpu.roll(both, 7, 0)), 192)[1:2]
+    f_bqv[...] = cut(jnp.where(iota((8, 2 * D), 1) < D, both, pltpu.roll(both, 7, 0)), 192)[1]
     f_bout[...] = cut(sg1[8:16, D : 2 * D], 96)[2:3]
     f_bdn[...] = cut(sg1[8:16, 0:D], 96)[2:3]
     ln = pl.ds(pl.multiple_of(c * HB, 128), HB)
@@ -1688,7 +1751,7 @@
     )
     big = ((96, 6 * D), (2, 256, D), (96, FF), (HB, D), (96, 3 * D), (96, D))
     shapes = (
-        (2, 256, D), (2, 256, D), (2, 4, D), (96, 6 * D), (1, 576), (9, 96), (96, 3 * D), (1, 192), (96, D), (1, 96),
+        (2, 256, D), (2, 256, D), (2, 4, D), (96, 6 * D), (576,), (9, 96), (96, 3 * D), (192,), (96, D), (1, 96),
         (96, FF), (1, HB), (9, HB), (HB, D), (1, 96),
     )
     out, gin, gcond, wada, bada, conv1, wqkv, bqv, wout, bout, wup, bup, conv2, wdn, bdn = pl.pallas_call(
@@ -1706,7 +1769,7 @@
     )(*got)
     flat = lambda a: a.reshape(a.shape[1])
     return (
-        out, gin, gcond, wada, flat(bada), conv1, wqkv, flat(bqv), wout, flat(bout),
+        out, gin, gcond, wada, bada, conv1, wqkv, bqv, wout, flat(bout),
         wup, flat(bup), conv2, wdn, flat(bdn),
     )
 

time: 205 us -> 194 us (0.946)
  Pallas kernels: 202 us -> 192 us
    pallas_call x1, Pallas kernels: 197 us -> 187 us  [fast_shards(): pl.pallas_call(whole_block, out_shape=[jax.ShapeDtypeStruct(s, t) for s,...]
where the time goes in v3:
time: 194 us
  Pallas kernels  192 us (99%)
    pallas_call x1, Pallas kernels, fast_shards(): pl.pallas_call(whole_block, out_shape=[jax.ShapeDtypeStruct(s, t) for s,...  187 us
    pallas_call x1, Pallas kernels, fast_shards(): pl.pallas_call(finish, out_shape=[jax.ShapeDtypeStruct(s, F32 if i else B...  5.17 us

profile of v3, /device:TPU:0, one launch (start us, length us, event | category | flops | bytes accessed | tf_op | source)
XLA Modules:
  0.0 193.6 jit_solution(16303241403243175512)
XLA Ops:
  0.7 186.5 %block.1 = (bf16[2,256,768]{2,1,0:T(8,128)(2,1)}, bf16[2,256,768]{2,1,0:T(8,128)(2,1)}, f32[2,4,768]{2,1,0:T(4,128)}, bf16[96,4608]{1,0:T(8,128)(2,1)}, f32[8,46...) custom-call(bf16[2,256,768]{2,1,0:T(8,128)(2,1)} %tok_h.1, ...), custom_call_target="tpu_custom_call" | custom-call | tf_op jit(solution)/shard_map/block/pallas_call | solution.py:1738
  187.2 5.2 %finish.1 = (bf16[2,256,768]{2,1,0:T(8,128)(2,1)}, f32[2,256,768]{2,1,0:T(8,128)}, f32[2,4,768]{2,1,0:T(4,128)}, f32[96,4608]{1,0:T(8,128)}, f32[576]{0:T(1024)}...) custom-call(bf16[2,256,768]{2,1,0:T(8,128)(2,1)} %get-tuple-element., ...), custom_call_target="tpu_custom_call" | custom-call | tf_op jit(solution)/shard_map/finish/pallas_call | solution.py:1757
  192.4 1.3 reduce

commit v4 on v3

--- a/solution.py
+++ b/solution.py
@@ -1521,6 +1521,24 @@
     line_u.s2()
     sum_q.s4(0)
 
+    def sums_back(n, _):
+        jj = n // 2
+        g = 2 * k + jj
+        rows = pl.ds(pl.multiple_of((n % 2) * 128, 128), 128)
+        nrm, _inv = norm_parts(tok[g, rows, :].astype(F32))
+        ig = gp[jj, rows, :]
+        ids = lv[g, rows, :]
+        low = ig.astype(BF)
+        scl = (ig * nrm).astype(BF)
+        total = dot_l(place_rows(ids, 0), low[:, 0:HB]) + dot_l(place_rows(ids, 1), low[:, HB:D])
+        total = total + dot_l(place_rows(ids, 2), scl[:, 0:HB]) + dot_l(place_rows(ids, 3), scl[:, HB:D])
+        mg2[...] += total[0:16]
+        return 0
+
+    lax.fori_loop(0, 4, sums_back, 0)
+    mgs2[...] = mg2[...].astype(BF)
+    mg2_cp = swap(mgs2, mgr2, sib)
+
     def one_back(n, _):
         jj = n % 2
         g = 2 * k + jj
@@ -1530,24 +1548,16 @@
         ig = gp[jj, rows, :]
         gi = mid[jj, rows, :] + norm_back(ig * (1.0 + piece(oh[g, rows, :], 1)), nrm, inv)
         stg_t[jj, h64] = gi.astype(BF).reshape(2, 64, D)
-        ids = lv[g, rows, :]
-        low = ig.astype(BF)
-        scl = (ig * nrm).astype(BF)
-        total = dot_l(place_rows(ids, 0), low[:, 0:HB]) + dot_l(place_rows(ids, 1), low[:, HB:D])
-        total = total + dot_l(place_rows(ids, 2), scl[:, 0:HB]) + dot_l(place_rows(ids, 3), scl[:, HB:D])
-        mg2[...] += total[0:16]
         return 0
 
     lax.fori_loop(0, 2, one_back, 0)
+    mg2_cp.wait_recv()
+    gat2.s0()
     hand_back(stg_t, v.gland, ro_gin, range(2))
     sum_q.s4(1)
     lax.fori_loop(2, 4, one_back, 0)
-    mgs2[...] = mg2[...].astype(BF)
-    mg2_cp = swap(mgs2, mgr2, sib)
 
     sum_q.s3(2)
-    mg2_cp.wait_recv()
-    gat2.s0()
     hand_back(stg_t, v.gland, ro_gin, range(2, 4))
     sum_q.s4(2)
     o_wout[...] = sum_o.s3().astype(BF)
@@ -1707,10 +1717,10 @@
     f_conv1[...] = cut(sg2[...], 96)[0:9]
     both = jnp.concatenate([sg2[8:16, :], sg2[8:16, :]], axis=1)
     f_bqv[...] = cut(jnp.where(iota((8, 2 * D), 1) < D, both, pltpu.roll(both, 7, 0)), 192)[1]
-    f_bout[...] = cut(sg1[8:16, D : 2 * D], 96)[2:3]
-    f_bdn[...] = cut(sg1[8:16, 0:D], 96)[2:3]
+    f_bout[...] = cut(sg1[8:16, D : 2 * D], 96)[2]
+    f_bdn[...] = cut(sg1[8:16, 0:D], 96)[2]
     ln = pl.ds(pl.multiple_of(c * HB, 128), HB)
-    f_bup[...] = sg1[9:10, ln]
+    f_bup[...] = sg1[9:10, ln][0]
     f_conv2[...] = sg1[0:9, ln]
     for cp in outs:
         cp.wait()
@@ -1751,8 +1761,8 @@
     )
     big = ((96, 6 * D), (2, 256, D), (96, FF), (HB, D), (96, 3 * D), (96, D))
     shapes = (
-        (2, 256, D), (2, 256, D), (2, 4, D), (96, 6 * D), (576,), (9, 96), (96, 3 * D), (192,), (96, D), (1, 96),
-        (96, FF), (1, HB), (9, HB), (HB, D), (1, 96),
+        (2, 256, D), (2, 256, D), (2, 4, D), (96, 6 * D), (576,), (9, 96), (96, 3 * D), (192,), (96, D), (96,),
+        (96, FF), (HB,), (9, HB), (HB, D), (96,),
     )
     out, gin, gcond, wada, bada, conv1, wqkv, bqv, wout, bout, wup, bup, conv2, wdn, bdn = pl.pallas_call(
         finish,
@@ -1767,10 +1777,9 @@
         compiler_params=pltpu.CompilerParams(vmem_limit_bytes=VMEM_LIMIT),
         name="finish",
     )(*got)
-    flat = lambda a: a.reshape(a.shape[1])
     return (
-        out, gin, gcond, wada, bada, conv1, wqkv, bqv, wout, flat(bout),
-        wup, flat(bup), conv2, wdn, flat(bdn),
+        out, gin, gcond, wada, bada, conv1, wqkv, bqv, wout, bout,
+        wup, bup, conv2, wdn, bdn,
     )
 
 

time: 194 us -> 193 us (level)
  no operation moved by 1% of the time
where the time goes in v4:
time: 193 us
  Pallas kernels  192 us (99%)
    pallas_call x1, Pallas kernels, fast_shards(): pl.pallas_call(whole_block, out_shape=[jax.ShapeDtypeStruct(s, t) for s,...  187 us
    pallas_call x1, Pallas kernels, fast_shards(): pl.pallas_call(finish, out_shape=[jax.ShapeDtypeStruct(s, F32 if i else B...  5.17 us

profile of v4, /device:TPU:0, one launch (start us, length us, event | category | flops | bytes accessed | tf_op | source)
XLA Modules:
  0.0 192.7 jit_solution(5722788228178139701)
XLA Ops:
  0.7 186.7 %block.1 = (bf16[2,256,768]{2,1,0:T(8,128)(2,1)}, bf16[2,256,768]{2,1,0:T(8,128)(2,1)}, f32[2,4,768]{2,1,0:T(4,128)}, bf16[96,4608]{1,0:T(8,128)(2,1)}, f32[8,46...) custom-call(bf16[2,256,768]{2,1,0:T(8,128)(2,1)} %tok_h.1, ...), custom_call_target="tpu_custom_call" | custom-call | tf_op jit(solution)/shard_map/block/pallas_call | solution.py:1748
  187.3 5.2 %finish.1 = (bf16[2,256,768]{2,1,0:T(8,128)(2,1)}, f32[2,256,768]{2,1,0:T(8,128)}, f32[2,4,768]{2,1,0:T(4,128)}, f32[96,4608]{1,0:T(8,128)}, f32[576]{0:T(1024)}...) custom-call(bf16[2,256,768]{2,1,0:T(8,128)(2,1)} %get-tuple-element., ...), custom_call_target="tpu_custom_call" | custom-call | tf_op jit(solution)/shard_map/finish/pallas_call | solution.py:1767
